TPU v7x, 32 devices: a whole 2x2x4 slice. The times are simulated.
32 devices in a mesh: prow: 8 (over y, x, core), pcol: 4 (over z).
Axes of the slice: x: 2, y: 2, z: 4, core: 2. Of those that a mesh axis runs over, the one named last changes fastest.
Arguments:
- matrix: bfloat16 [4, 2048, 4, 1024], P(None, 'prow', None, 'pcol'), may hold values from -6 to 6
- pivots: int32 [2, 256], replicated, may hold values from 0 to 8191, as said below
- lower_inverse: bfloat16 [2, 256, 256], replicated, as said below
- upper_inverse: bfloat16 [2, 256, 256], replicated, as said below
Outputs:
- factored: bfloat16 [4, 2048, 4, 1024], P(None, 'prow', None, 'pcol')
Inputs may be any that keep to these rules, and one draw needn't show every extreme that they name: For each panel k and each i, pivots[k, i] is either k * 256 + i or a row at or after (k + 1) * 256; entry 0 of each list is k * 256; the rows of one panel's list are distinct, and each list names row 8191. Each lower_inverse[k] is unit lower triangular. Each upper_inverse[k] is upper triangular with positive diagonal.
All inputs are finite; a program needn't handle non-finite values.
Results may differ from a plain program's by a relative error of at most 0.0079.
Values may be sent and summed in bfloat16 or wider, within the bound.
No kernel may reach another device: no remote copies, remote signals or barrier semaphores. Data moves between devices by JAX's collectives and lax.ppermute only.
A program may use at most 64 MiB of HBM per device.

v0:
```python
import jax
import jax.numpy as jnp
from jax import lax
from jax.sharding import PartitionSpec as P


def spread(block, axis, source):
    block = jnp.where(lax.axis_index(axis) == source, block, jnp.zeros_like(block))
    return lax.psum(block, axis)


def local(matrix, pivots, lower_inverse, upper_inverse):
    row_count = lax.axis_size("prow")
    col_count = lax.axis_size("pcol")
    my_row = lax.axis_index("prow")
    my_col = lax.axis_index("pcol")
    blocks_down, block, blocks_across, _ = matrix.shape
    local_rows = blocks_down * block
    local_cols = blocks_across * block
    current = matrix.reshape(local_rows, local_cols)
    row_place = jnp.arange(local_rows)
    col_place = jnp.arange(local_cols)
    global_rows = (row_place // block * row_count + my_row) * block + row_place % block
    global_cols = (col_place // block * col_count + my_col) * block + col_place % block
    for panel in range(pivots.shape[0]):
        start = panel * block
        chosen = pivots[panel]
        block_row = chosen // block
        is_mine = block_row % row_count == my_row
        local_index = block_row // row_count * block + chosen % block
        safe_index = jnp.where(is_mine, local_index, 0)
        picked = jnp.where(is_mine[:, None], current[safe_index], jnp.zeros((), jnp.bfloat16))
        top_holder = panel % row_count
        top_first = panel // row_count * block
        is_top = my_row == top_holder
        top_local = current[top_first : top_first + block]
        incoming = lax.psum(picked, "prow").astype(jnp.float32)
        old_top = spread(top_local, "prow", top_holder)
        incoming = incoming.astype(jnp.bfloat16)
        target = jnp.where(is_mine, local_index, local_rows)
        current = current.at[target].set(old_top, mode="drop")
        top_now = current[top_first : top_first + block]
        current = current.at[top_first : top_first + block].set(
            jnp.where(is_top, incoming, top_now)
        )
        panel_holder = panel % col_count
        panel_first = panel // col_count * block
        panel_cols = current[:, panel_first : panel_first + block]
        factor = jnp.dot(
            panel_cols, upper_inverse[panel], preferred_element_type=jnp.float32
        ).astype(jnp.bfloat16)
        lower = spread(factor, "pcol", panel_holder)
        top_rows_now = current[top_first : top_first + block]
        upper_local = jnp.dot(
            lower_inverse[panel], top_rows_now, preferred_element_type=jnp.float32
        ).astype(jnp.bfloat16)
        upper = spread(upper_local, "prow", top_holder)
        row_mask = global_rows >= start + block
        col_mask = global_cols >= start + block
        product = jnp.dot(lower, upper, preferred_element_type=jnp.float32)
        changed = (current.astype(jnp.float32) - product).astype(jnp.bfloat16)
        current = jnp.where(row_mask[:, None] & col_mask[None, :], changed, current)
        panel_now = current[:, panel_first : panel_first + block]
        is_panel = my_col == panel_holder
        current = current.at[:, panel_first : panel_first + block].set(
            jnp.where(is_panel & row_mask[:, None], lower, panel_now)
        )
        top_now = current[top_first : top_first + block]
        current = current.at[top_first : top_first + block].set(
            jnp.where(is_top & col_mask[None, :], upper, top_now)
        )
    return current.reshape(matrix.shape)


def solution(mesh):
    in_specs = (P(None, "prow", None, "pcol"), P(), P(), P())
    out_specs = P(None, "prow", None, "pcol")
    return jax.shard_map(local, mesh=mesh, in_specs=in_specs, out_specs=out_specs, check_vma=False)
```

profile of v0, /device:TPU:0, one launch (start us, length us, event | category | flops | bytes accessed | tf_op | source)
XLA Modules:
  0.0 360.5 jit_solution(1832008782098364760)
XLA Ops:
  6.5 0.8 and_select_fusion.5
  7.3 0.8 fusion.48
  8.1 2.1 copy.23
  10.2 1.3 slice_select_fusion.4
  11.5 0.9 copy.24
  12.4 1.2 gather_fusion
  13.5 0.9 broadcast_select_fusion.1
  14.5 0.0 all-reduce.19.cloned.1.call-update
  14.5 0.0 all-reduce.11.cloned.1.call-start
  14.6 0.7 compare_reduce_fusion
  15.3 58.7 %all-reduce.19.cloned.1.call-done = (bf16[256,1024]{1,0:T(8,128)(2,1)}, bf16[256,1024]{1,0:T(8,128)(2,1)}) async-done(((bf16[256,1024]{1,0:T(8,128)(2,1)}, bf16[256,1024]{1,0:T(8,128)(2,1)}), (bf16[256,1024]{1,0:T(8,128)(2,1)}, bf16[256,1024]{1,0:T(8,128)(2,1)})) %all-reduce.19.cloned.1.call-update) | async-done | bytes 1048592 | tf_op jit(solution)/shard_map/psum | solution.py:9
  74.1 3.3 scatter_fusion
  77.4 0.0 copy-start.5
  77.4 1.1 fusion.3
  78.5 0.0 all-reduce.11.cloned.1.call-update
  78.6 0.0 all-reduce.9.cloned.1.call-start
  78.6 0.2 fusion.10
  78.9 1.1 fusion
  80.0 0.0 all-reduce.9.cloned.1.call-update
  80.0 0.0 all-reduce.17.cloned.1.call-start
  80.1 52.2 %all-reduce.11.cloned.1.call-done = bf16[256,1024]{1,0:T(8,128)(2,1)} async-done(((bf16[256,1024]{1,0:T(8,128)(2,1)}), bf16[256,1024]{1,0:T(8,128)(2,1)}) %all-reduce.11.cloned.1.call-update) | async-done | bytes 524304 | tf_op jit(solution)/shard_map/psum | solution.py:9
  132.3 40.1 %all-reduce.9.cloned.1.call-done = bf16[1024,256]{1,0:T(8,128)(2,1)} async-done(((bf16[1024,256]{1,0:T(8,128)(2,1)}), bf16[1024,256]{1,0:T(8,128)(2,1)}) %all-reduce.9.cloned.1.call-update) | async-done | bytes 524304 | tf_op jit(solution)/shard_map/psum | solution.py:9
  172.4 3.6 and_select_fusion
  176.0 2.9 fusion.6
  178.9 2.3 broadcast_select_fusion.2
  181.2 3.4 gather_fusion.1
  184.6 0.9 broadcast_select_fusion
  185.5 0.0 all-reduce.17.cloned.1.call-update
  185.6 0.0 all-reduce.15.cloned.1.call-start
  185.6 56.8 %all-reduce.17.cloned.1.call-done = (bf16[256,1024]{1,0:T(8,128)(2,1)}, bf16[256,1024]{1,0:T(8,128)(2,1)}) async-done(((bf16[256,1024]{1,0:T(8,128)(2,1)}, bf16[256,1024]{1,0:T(8,128)(2,1)}), (bf16[256,1024]{1,0:T(8,128)(2,1)}, bf16[256,1024]{1,0:T(8,128)(2,1)})) %all-reduce.17.cloned.1.call-update) | async-done | bytes 1048592 | tf_op jit(solution)/shard_map/psum | solution.py:9
  242.4 5.4 %scatter_fusion.1 = bf16[1024,1024]{1,0:T(8,128)(2,1)} fusion(bf16[1024,1024]{1,0:T(8,128)(2,1)} %get-tuple-element.92, s32[256]{0:T(256)S(1)} %bitcast.62, bf16[256,1024]{1,0:T(8,128)(2,1)} %get-tuple-element.77), kind=kCustom, calls=%fused_computation.3 | custom fusion | bytes 1573888 | tf_op jit(solution)/shard_map/scatter | solution.py:41
  247.8 0.0 copy-done.2
  247.8 2.2 fusion.5
  250.0 0.0 all-reduce.15.cloned.1.call-update
  250.0 0.2 all-reduce.13.cloned.1.call-start
  250.2 2.0 fusion.11
  252.3 2.2 fusion.1
  254.5 0.0 all-reduce.13.cloned.1.call-update
  254.6 49.2 %all-reduce.15.cloned.1.call-done = bf16[256,1024]{1,0:T(8,128)(2,1)} async-done(((bf16[256,1024]{1,0:T(8,128)(2,1)}), bf16[256,1024]{1,0:T(8,128)(2,1)}) %all-reduce.15.cloned.1.call-update) | async-done | bytes 524304 | tf_op jit(solution)/shard_map/psum | solution.py:9
  303.8 39.8 %all-reduce.13.cloned.1.call-done = bf16[1024,256]{0,1:T(8,128)(2,1)} async-done(((bf16[1024,256]{0,1:T(8,128)(2,1)}), bf16[1024,256]{0,1:T(8,128)(2,1)}) %all-reduce.13.cloned.1.call-update) | async-done | bytes 524304 | tf_op jit(solution)/shard_map/psum | solution.py:9
  343.6 3.7 %and_select_fusion.1 = bf16[1024,1024]{1,0:T(8,128)(2,1)S(1)} fusion(bf16[1024,1024]{1,0:T(8,128)(2,1)} %fusion.11, bf16[1024,256]{0,1:T(8,128)(2,1)} %all-reduce.13.cloned.1.call-done, bf16[256,1024]{1,0:T(8,128)(2,1)} %all-reduce.15.cloned.1.call-done, pred[1024]{0:T(1024)(128)(4,1)S(1)} %fusion.39, pred[1024]{0:T(1024)(128)(4,1)S(1)} %fusion.37), kind=kOutput, calls=%fused_computation.7 | convolution fusion | flops 542113792 | bytes 5244928 | tf_op jit(solution)/shard_map/dot_general | solution.py:60
  347.3 0.1 slice.176
  347.4 0.2 copy.22
  347.6 1.8 select_select_fusion
  349.4 0.2 copy.18
  349.6 0.1 constant_dynamic-update-slice_fusion
  349.7 1.3 fusion.7
  350.9 2.8 reshape.658
  (25 shorter events, 0.2 us)
Async XLA Ops:
  6.5 67.5 %all-reduce.19.cloned.1.call-start = ((), (), s32[]{:S(2)}) async-start(), calls=%async_computation.5 | async-start | bytes 2097152 | tf_op jit(solution)/shard_map/psum | solution.py:9
  14.5 117.8 %all-reduce.11.cloned.1.call-start = ((), (), s32[]{:S(2)}) async-start(), calls=%async_computation.1 | async-start | bytes 1048576 | tf_op jit(solution)/shard_map/psum | solution.py:9
  74.1 3.3 copy-start.1
  74.1 3.4 copy-start.4
  77.4 1.4 copy-start.5
  78.6 93.8 %all-reduce.9.cloned.1.call-start = ((), (), s32[]{:S(2)}) async-start(), calls=%async_computation | async-start | bytes 1048576 | tf_op jit(solution)/shard_map/psum | solution.py:9
  80.0 162.4 %all-reduce.17.cloned.1.call-start = ((), (), s32[]{:S(2)}) async-start(), calls=%async_computation.4 | async-start | bytes 2097152 | tf_op jit(solution)/shard_map/psum | solution.py:9
  172.4 3.6 copy-start
  172.4 6.5 %copy-start.3 = (bf16[256,1024]{1,0:T(8,128)(2,1)S(1)}, bf16[256,1024]{1,0:T(8,128)(2,1)}, u32[]{:S(2)}) copy-start(bf16[256,1024]{1,0:T(8,128)(2,1)} %all-reduce.11.cloned.1.call-done) | copy-start | bytes 1572868
  185.6 118.2 %all-reduce.15.cloned.1.call-start = ((), (), s32[]{:S(2)}) async-start(), calls=%async_computation.3 | async-start | bytes 1048576 | tf_op jit(solution)/shard_map/psum | solution.py:9
  242.4 5.4 %copy-start.2 = (bf16[256,1024]{1,0:T(8,128)(2,1)S(1)}, bf16[256,1024]{1,0:T(8,128)(2,1)}, u32[]{:S(2)}) copy-start(bf16[256,1024]{1,0:T(8,128)(2,1)} %get-tuple-element.78) | copy-start | bytes 1572868
  250.0 93.6 %all-reduce.13.cloned.1.call-start = ((), (), s32[]{:S(2)}) async-start(), calls=%async_computation.2 | async-start | bytes 1048576 | tf_op jit(solution)/shard_map/psum | solution.py:9
Sparse Core Ops, SparseCore 0:
  14.6 59.3 all-reduce.18
  78.7 53.5 all-reduce.10
  134.8 37.5 all-reduce.8
  185.7 56.6 all-reduce.16
  250.1 53.5 all-reduce.14
  306.0 37.5 all-reduce.12
where the time goes:
time: 361 us
  waiting for transfers between devices  297 us (82%)
  local copies, waits for them, and re-layouts  20.3 us (6%)
  other arithmetic  15.3 us (4%)
  matrix products  13.9 us (4%)
  between operations  13.7 us (4%)
    psum x6, waiting for transfers between devices, spread(): return lax.psum(block, axis)  297 us
    scatter x2, local copies, waits for them, and re-layouts, local(): current = current.at[target].set(old_top, mode='drop')  8.71 us
    dot_general x2, matrix products, local(): product = jnp.dot(lower, upper, preferred_element_type=jnp.float32)  7.27 us
  transfers between devices with their start and end apart: 6, of which 6 were waited for; matrix products, arithmetic and copies ran while one was open for 2% of the time, Pallas kernels for 0%

commit v1 on v0

v1 whole, which is shorter than its diff:
```python
import jax
import jax.numpy as jnp
from jax import lax
from jax.sharding import PartitionSpec as P


def levels_of(count):
    bits = count.bit_length() - 1
    return list(range(1, bits))


def exchange_pairs(count, level):
    order = levels_of(count)
    back = order[::-1]
    return [(i, i ^ (1 << (order[level] if i % 2 == 0 else back[level]))) for i in range(count)]


def spread_pairs(count, level):
    order = levels_of(count)
    back = order[::-1]
    pairs = []
    for parity, bits in ((0, order), (1, back)):
        held = [parity]
        for step in range(level):
            held += [i ^ (1 << bits[step]) for i in held]
        pairs += [(i, i ^ (1 << bits[level])) for i in held]
    return pairs


def far_steps(count):
    steps = []
    distance = count // 2
    while distance >= 2:
        steps.append([(i, i + distance) for i in range(count) if i % (2 * distance) < 2])
        distance //= 2
    return steps


def twin(count):
    return [(i, i ^ 1) for i in range(count)]


def member(index, targets):
    return sum((index == t).astype(jnp.int32) for t in targets) > 0


def local(matrix, pivots, lower_inverse, upper_inverse):
    nr = lax.axis_size("prow")
    nc = lax.axis_size("pcol")
    my_row = lax.axis_index("prow")
    my_col = lax.axis_index("pcol")
    down, block, across, _ = matrix.shape
    rows = down * block
    even_row = my_row % 2 == 0
    even_col = my_col % 2 == 0
    both = ("prow", "pcol")

    first, second = pivots[0], pivots[1]
    place = jnp.arange(block)
    hits = second[:, None] == first[None, :]
    second_source = jnp.where(hits.any(1), jnp.argmax(hits, 1), second)
    source = jnp.concatenate([first, second_source])
    after = jnp.where(first == place, place, first)
    moved = (first[:, None] == (block + place)[None, :])
    via_top = jnp.where(moved.any(1), jnp.sum(jnp.where(moved, second[None, :], 0), 1), after)
    back = first[:, None] == second[None, :]
    first_goes = jnp.where(back.any(1), block + jnp.argmax(back, 1), via_top)
    taken = (block + place)[:, None] == first[None, :]
    second_goes = jnp.where(taken.any(1), jnp.argmax(taken, 1), second)
    goes = jnp.concatenate([first_goes, second_goes])

    source_block = source // block
    mine = source_block % nr == my_row
    source_local = jnp.where(mine, source_block // nr * block + source % block, 0)
    flat = matrix.reshape(rows, across * block)
    picked = jnp.where(mine[:, None], flat[source_local], jnp.zeros((), jnp.bfloat16))

    own = matrix[:, :, 0, :]
    have, other = [], []
    for b in range(down):
        piece = own[b]
        for pairs in far_steps(nc):
            got = lax.ppermute(piece, "pcol", pairs)
            piece = jnp.where(member(my_col, [t for _, t in pairs]), got, piece)
        have.append(piece)
        other.append(lax.ppermute(piece, "pcol", twin(nc)))
    have = jnp.stack(have)
    other = jnp.stack(other)
    panel0 = jnp.where(even_col, have, other)
    panel1 = jnp.where(even_col, other, have)

    def gather_rows(part):
        keep = jnp.where(even_row, part[:block], part[block:])
        give = jnp.where(even_row, part[block:], part[:block])
        total = keep + lax.ppermute(give, "prow", twin(nr))
        for level in range(len(levels_of(nr))):
            total = total + lax.ppermute(total, "prow", exchange_pairs(nr, level))
        return total

    def pair_up(part):
        got = lax.ppermute(part, "prow", twin(nr))
        return jnp.where(even_row, part, got), jnp.where(even_row, got, part)

    head = gather_rows(picked[:, :block])
    tail = gather_rows(picked[:, block:])
    head0, head1 = pair_up(head)
    tail0, tail1 = pair_up(tail)
    rows0 = jnp.concatenate([head0, tail0], 1)
    rows1 = jnp.concatenate([head1, tail1], 1)

    side = head
    for pairs in far_steps(nc):
        joint = []
        for i in range(nr):
            joint += [(i * nc + s, i * nc + t) for s, t in pairs if s % 2 == (1 - i % 2)]
        got = lax.ppermute(side, both, joint)
        right = member(my_row * nc + my_col, [t for _, t in joint])
        side = jnp.where(right, got, side)
    joint = []
    for i in range(nr):
        joint += [(i * nc + s, i * nc + (s ^ 1)) for s in range(nc) if s % 2 == (1 - i % 2)]
    got = lax.ppermute(side, both, joint)
    side = jnp.where(member(my_row * nc + my_col, [t for _, t in joint]), got, side)
    side01, side10 = pair_up(side)

    def spread_rows(part):
        for level in range(len(levels_of(nr))):
            pairs = spread_pairs(nr, level)
            got = lax.ppermute(part, "prow", pairs)
            part = jnp.where(member(my_row, [t for _, t in pairs]), got, part)
        a, b = pair_up(part)
        return jnp.concatenate([a, b], 0)

    top = spread_rows(flat[:block])
    top_panels = spread_rows(jnp.concatenate([panel0[0], panel1[0]], 1))

    return finish(
        flat, rows0, rows1, side10, side01, top, top_panels, panel0, panel1,
        goes, lower_inverse, upper_inverse, my_row, my_col, nr, nc, matrix.shape,
    )


def finish(flat, rows0, rows1, side10, side01, top, top_panels, panel0, panel1,
           goes, lower_inverse, upper_inverse, my_row, my_col, nr, nc, shape):
    down, block, across, _ = shape
    f32, bf = jnp.float32, jnp.bfloat16
    dot = lambda a, b: jnp.dot(a, b, preferred_element_type=f32)
    u0 = dot(lower_inverse[0], rows0).astype(bf)
    u0p = dot(lower_inverse[0], side01).astype(bf)
    lp = dot(side10, upper_inverse[0]).astype(bf)
    r1 = (rows1.astype(f32) - dot(lp, u0)).astype(bf)
    u1 = dot(lower_inverse[1], r1).astype(bf)
    outs = []
    col = jnp.arange(across * block) // block * nc + my_col
    for b in range(down):
        g = (b * nr + my_row) * block + jnp.arange(block)
        onehot = (g[:, None] == goes[None, :]).astype(bf)
        hit = (g[:, None] == goes[None, :]).any(1)[:, None]
        s = jnp.where(hit, dot(onehot, top).astype(bf), flat[b * block:(b + 1) * block])
        tp = dot(onehot, top_panels).astype(bf)
        z0 = jnp.where(hit, tp[:, :block], panel0[b])
        z1 = jnp.where(hit, tp[:, block:], panel1[b])
        l0 = dot(z0, upper_inverse[0]).astype(bf)
        a1 = (s.astype(f32) - dot(l0, u0)).astype(bf)
        p1 = (z1.astype(f32) - dot(l0, u0p)).astype(bf)
        l1 = dot(p1, upper_inverse[1]).astype(bf)
        a2 = (a1.astype(f32) - dot(l1, u1)).astype(bf)
        wide = lambda x: jnp.tile(x, (1, across))
        body = jnp.where(col[None] == 0, wide(l0), jnp.where(col[None] == 1, wide(l1), a2))
        case0 = jnp.where(col[None] == 0, rows0, u0)
        case1 = jnp.where(col[None] == 0, wide(lp), jnp.where(col[None] == 1, r1, u1))
        gb = b * nr + my_row
        outs.append(jnp.where(gb == 0, case0, jnp.where(gb == 1, case1, body)))
    return jnp.concatenate(outs, 0).reshape(shape)


def solution(mesh):
    in_specs = (P(None, "prow", None, "pcol"), P(), P(), P())
    out_specs = P(None, "prow", None, "pcol")
    return jax.shard_map(local, mesh=mesh, in_specs=in_specs, out_specs=out_specs, check_vma=False)
```

time: 361 us -> 110 us (0.30)
  the two profiles are of different devices: /device:TPU:0 before, /device:TPU:29 now
where the time goes in v1:
time: 110 us; the launch traced here: 109 us
  starting transfers between devices  28.7 us (26%)
  local copies, waits for them, and re-layouts  27 us (25%)
  other arithmetic  18.8 us (17%)
  matrix products  18.8 us (17%)
  waiting for transfers between devices  14.1 us (13%)
  between operations  1.25 us (1%)
    dot_general x29, matrix products, finish(): dot = lambda a, b: jnp.dot(a, b, preferred_element_type=f32)  18.8 us
    unnamed x124, local copies, waits for them, and re-layouts  16.9 us
    ppermute x5, starting transfers between devices, pair_up(): got = lax.ppermute(part, 'prow', twin(nr))  9.56 us
    ppermute x4, waiting for transfers between devices, local(): got = lax.ppermute(piece, 'pcol', pairs)  6.01 us
    ppermute x4, waiting for transfers between devices, local(): other.append(lax.ppermute(piece, 'pcol', twin(nc)))  5.72 us
    ppermute x4, starting transfers between devices, spread_rows(): got = lax.ppermute(part, 'prow', pairs)  5.39 us
    ppermute x4, starting transfers between devices, local(): got = lax.ppermute(piece, 'pcol', pairs)  5.12 us
    ppermute x4, starting transfers between devices, gather_rows(): total = total + lax.ppermute(total, 'prow', exchange_pairs(nr, level))  4.91 us
  transfers between devices with their start and end apart: 25, of which 9 were waited for; matrix products, arithmetic and copies ran while one was open for 41% of the time, Pallas kernels for 0%

profile of v1, /device:TPU:29, one launch (start us, length us, event | category | flops | bytes accessed | tf_op | source)
XLA Modules:
  0.0 108.6 jit_solution(4361784448412442178)
XLA Ops:
  1.5 0.9 compare_reduce_fusion.6
  3.2 2.1 %copy.21 = bf16[128,8,4,256]{3,1,2,0:T(8,128)(2,1)S(1)} copy(bf16[128,8,4,256]{3,2,1,0:T(4,128)(2,1)} %bitcast.174) | data formatting | bytes 4194304
  5.9 2.1 %gather_fusion = bf16[512,1024]{1,0:T(8,128)(2,1)S(1)} fusion(bf16[1024,1024]{1,0:T(8,128)(2,1)S(1)} %bitcast.173, s32[1024]{0:T(1024)S(1)} %pad_clamp_fusion), kind=kCustom, calls=%fused_computation | custom fusion | bytes 2099200 | tf_op jit(solution)/shard_map/gather | solution.py:76
  11.0 1.3 %collective-permute-start.14 = (bf16[256,256]{1,0:T(8,128)(2,1)}, bf16[256,256]{1,0:T(8,128)(2,1)}, u32[]{:S(2)}, u32[]{:S(2)}) collective-permute-start(bf16[256,256]{1,0:T(8,128)(2,1)} %bitcast.169), channel_id=1, source_target_pairs={{0,2},{1,3},{4,6},{5,7},{8,10},{9,11},{12,14},{13,15},{16,18},{17,... | collective-permute-start | bytes 393224 | tf_op jit(solution)/shard_map/ppermute | solution.py:83
  13.0 1.3 %collective-permute-start.13 = (bf16[256,256]{1,0:T(8,128)(2,1)}, bf16[256,256]{1,0:T(8,128)(2,1)}, u32[]{:S(2)}, u32[]{:S(2)}) collective-permute-start(bf16[256,256]{1,0:T(8,128)(2,1)} %bitcast.170), channel_id=1, source_target_pairs={{0,2},{1,3},{4,6},{5,7},{8,10},{9,11},{12,14},{13,15},{16,18},{17,... | collective-permute-start | bytes 393224 | tf_op jit(solution)/shard_map/ppermute | solution.py:83
  14.9 1.3 %collective-permute-start.12 = (bf16[256,256]{1,0:T(8,128)(2,1)}, bf16[256,256]{1,0:T(8,128)(2,1)}, u32[]{:S(2)}, u32[]{:S(2)}) collective-permute-start(bf16[256,256]{1,0:T(8,128)(2,1)} %bitcast.171), channel_id=1, source_target_pairs={{0,2},{1,3},{4,6},{5,7},{8,10},{9,11},{12,14},{13,15},{16,18},{17,... | collective-permute-start | bytes 393224 | tf_op jit(solution)/shard_map/ppermute | solution.py:83
  16.9 1.3 %collective-permute-start.11 = (bf16[256,256]{1,0:T(8,128)(2,1)}, bf16[256,256]{1,0:T(8,128)(2,1)}, u32[]{:S(2)}, u32[]{:S(2)}) collective-permute-start(bf16[256,256]{1,0:T(8,128)(2,1)} %bitcast.172), channel_id=1, source_target_pairs={{0,2},{1,3},{4,6},{5,7},{8,10},{9,11},{12,14},{13,15},{16,18},{17,... | collective-permute-start | bytes 393224 | tf_op jit(solution)/shard_map/ppermute | solution.py:83
  19.7 1.7 %fusion.139 = (bf16[1,256,4,256]{3,2,1,0:T(4,128)(2,1)S(1)}, bf16[1,256,4,256]{3,2,1,0:T(4,128)(2,1)}, bf16[1,256,4,256]{3,2,1,0:T(4,128)(2,1)}, bf16[1,256,4,256]{3,2,1,0:T(4,128)(2,1)S(1)}) fusion(bf16[4,256,4,256]{3,2,1,0:T(4,128)(2,1)S(1)} %copy-done), kind=kLoop, calls=%fused_computation.262 | loop fusion | bytes 4194304 | tf_op jit(solution)/shard_map/slice | solution.py:159
  23.8 1.9 %copy.34 = bf16[32,8,4,256]{3,1,2,0:T(8,128)(2,1)} copy(bf16[32,8,4,256]{3,2,1,0:T(4,128)(2,1)} %bitcast.199) | data formatting | bytes 1048576
  25.8 1.1 %copy.25 = bf16[32,8,4,256]{3,1,2,0:T(8,128)(2,1)S(1)} copy(bf16[32,8,4,256]{3,2,1,0:T(4,128)(2,1)} %bitcast.198) | data formatting | bytes 1048576
  26.9 1.0 copy.31
  28.8 0.9 select_add_fusion.1
  30.6 0.9 broadcast_select_fusion.14
  31.6 1.8 %collective-permute-done.13 = bf16[256,256]{1,0:T(8,128)(2,1)} collective-permute-done((bf16[256,256]{1,0:T(8,128)(2,1)}, bf16[256,256]{1,0:T(8,128)(2,1)}, u32[]{:S(2)}, u32[]{:S(2)}) %collective-permute-start.13) | collective-permute-done | bytes 131104 | tf_op jit(solution)/shard_map/ppermute | solution.py:83
  33.4 0.9 broadcast_select_fusion.15
  34.5 1.8 %collective-permute-done.12 = bf16[256,256]{1,0:T(8,128)(2,1)} collective-permute-done((bf16[256,256]{1,0:T(8,128)(2,1)}, bf16[256,256]{1,0:T(8,128)(2,1)}, u32[]{:S(2)}, u32[]{:S(2)}) %collective-permute-start.12) | collective-permute-done | bytes 131104 | tf_op jit(solution)/shard_map/ppermute | solution.py:83
  36.3 0.9 broadcast_select_fusion.16
  37.3 1.8 %collective-permute-done.11 = bf16[256,256]{1,0:T(8,128)(2,1)} collective-permute-done((bf16[256,256]{1,0:T(8,128)(2,1)}, bf16[256,256]{1,0:T(8,128)(2,1)}, u32[]{:S(2)}, u32[]{:S(2)}) %collective-permute-start.11) | collective-permute-done | bytes 131104 | tf_op jit(solution)/shard_map/ppermute | solution.py:83
  39.1 0.9 broadcast_select_fusion.17
  40.1 0.9 compare_reduce_fusion.3
  42.0 1.3 %collective-permute-start.22 = (bf16[256,1024]{1,0:T(8,128)(2,1)S(1)}, bf16[256,1024]{1,0:T(8,128)(2,1)S(1)}, u32[]{:S(2)}, u32[]{:S(2)}) collective-permute-start(bf16[256,1024]{1,0:T(8,128)(2,1)S(1)} %bitcast.193), channel_id=1, source_target_pairs={{0,8},{4,20},{1,9},{5,21},{2,10},{6,22},{3,11},{7,23}} | collective-permute-start | bytes 1572872 | tf_op jit(solution)/shard_map/ppermute | solution.py:129
  43.3 1.3 %collective-permute-done.17 = bf16[256,256]{1,0:T(8,128)(2,1)S(1)} collective-permute-done((bf16[256,256]{1,0:T(8,128)(2,1)S(1)}, bf16[256,256]{1,0:T(8,128)(2,1)S(1)}, u32[]{:S(2)}, u32[]{:S(2)}) %collective-permute-start.17) | collective-permute-done | bytes 131104 | tf_op jit(solution)/shard_map/ppermute | solution.py:86
  44.6 1.2 %collective-permute-start.2 = (bf16[256,256]{1,0:T(8,128)(2,1)S(1)}, bf16[256,256]{1,0:T(8,128)(2,1)S(1)}, u32[]{:S(2)}, u32[]{:S(2)}) collective-permute-start(bf16[256,256]{1,0:T(8,128)(2,1)S(1)} %add.288), channel_id=1, source_target_pairs={{0,16},{4,12},{8,24},{12,4},{16,0},{20,28},{24,8},{28,20},{1,17},{... | collective-permute-start | bytes 393224 | tf_op jit(solution)/shard_map/ppermute | solution.py:97
  45.8 1.6 %collective-permute-done.16 = bf16[256,256]{1,0:T(8,128)(2,1)S(1)} collective-permute-done((bf16[256,256]{1,0:T(8,128)(2,1)S(1)}, bf16[256,256]{1,0:T(8,128)(2,1)S(1)}, u32[]{:S(2)}, u32[]{:S(2)}) %collective-permute-start.16) | collective-permute-done | bytes 131104 | tf_op jit(solution)/shard_map/ppermute | solution.py:86
  47.4 2.8 %collective-permute-done.15 = bf16[256,256]{1,0:T(8,128)(2,1)S(1)} collective-permute-done((bf16[256,256]{1,0:T(8,128)(2,1)S(1)}, bf16[256,256]{1,0:T(8,128)(2,1)S(1)}, u32[]{:S(2)}, u32[]{:S(2)}) %collective-permute-start.15) | collective-permute-done | bytes 131104 | tf_op jit(solution)/shard_map/ppermute | solution.py:86
  50.4 1.3 %collective-permute-start.19 = (bf16[256,512]{1,0:T(8,128)(2,1)S(1)}, bf16[256,512]{1,0:T(8,128)(2,1)S(1)}, u32[]{:S(2)}, u32[]{:S(2)}) collective-permute-start(bf16[256,512]{1,0:T(8,128)(2,1)S(1)} %pad_maximum_fusion.7), channel_id=1, source_target_pairs={{0,8},{4,20},{1,9},{5,21},{2,10},{6,22},{3,11},{7,23}} | collective-permute-start | bytes 786440 | tf_op jit(solution)/shard_map/ppermute | solution.py:129
  52.6 2.9 %collective-permute-start.5 = (bf16[256,768]{1,0:T(8,128)(2,1)S(1)}, bf16[256,768]{1,0:T(8,128)(2,1)S(1)}, u32[]{:S(2)}, u32[]{:S(2)}) collective-permute-start(bf16[256,768]{1,0:T(8,128)(2,1)S(1)} %select_add_fusion), channel_id=1, source_target_pairs={{0,8},{4,20},{8,0},{12,28},{16,24},{20,4},{24,16},{28,12},{1,9},{5... | collective-permute-start | bytes 1179656 | tf_op jit(solution)/shard_map/ppermute | solution.py:97
  56.2 1.3 %collective-permute-start.9 = (bf16[256,256]{1,0:T(8,128)(2,1)S(1)}, bf16[256,256]{1,0:T(8,128)(2,1)S(1)}, u32[]{:S(2)}, u32[]{:S(2)}) collective-permute-start(bf16[256,256]{1,0:T(8,128)(2,1)S(1)} %get-tuple-element.39), channel_id=1, source_target_pairs={{1,0},{3,2},{4,5},{6,7},{9,8},{11,10},{12,13},{14,15},{17,16},{19,... | collective-permute-start | bytes 393224 | tf_op jit(solution)/shard_map/ppermute | solution.py:122
  57.9 1.3 %collective-permute-start.20 = (bf16[256,512]{1,0:T(8,128)(2,1)S(1)}, bf16[256,512]{1,0:T(8,128)(2,1)S(1)}, u32[]{:S(2)}, u32[]{:S(2)}) collective-permute-start(bf16[256,512]{1,0:T(8,128)(2,1)S(1)} %broadcast_select_fusion.10), channel_id=1, source_target_pairs={{0,16},{8,24},{4,12},{20,28},{1,17},{9,25},{5,13},{21,29},{2,18},{... | collective-permute-start | bytes 786440 | tf_op jit(solution)/shard_map/ppermute | solution.py:129
  59.3 1.5 %collective-permute-start.23 = (bf16[256,1024]{1,0:T(8,128)(2,1)S(1)}, bf16[256,1024]{1,0:T(8,128)(2,1)S(1)}, u32[]{:S(2)}, u32[]{:S(2)}) collective-permute-start(bf16[256,1024]{1,0:T(8,128)(2,1)S(1)} %broadcast_select_fusion.1), channel_id=1, source_target_pairs={{0,16},{8,24},{4,12},{20,28},{1,17},{9,25},{5,13},{21,29},{2,18},{... | collective-permute-start | bytes 1572872 | tf_op jit(solution)/shard_map/ppermute | solution.py:129
  60.8 2.0 %collective-permute-done.9 = bf16[256,256]{1,0:T(8,128)(2,1)S(1)} collective-permute-done((bf16[256,256]{1,0:T(8,128)(2,1)S(1)}, bf16[256,256]{1,0:T(8,128)(2,1)S(1)}, u32[]{:S(2)}, u32[]{:S(2)}) %collective-permute-start.9) | collective-permute-done | bytes 131104 | tf_op jit(solution)/shard_map/ppermute | solution.py:122
  62.8 2.5 %collective-permute-start.10 = (bf16[256,256]{1,0:T(8,128)(2,1)S(1)}, bf16[256,256]{1,0:T(8,128)(2,1)S(1)}, u32[]{:S(2)}, u32[]{:S(2)}) collective-permute-start(bf16[256,256]{1,0:T(8,128)(2,1)S(1)} %broadcast_select_fusion.19), channel_id=1, source_target_pairs={{0,4},{4,0},{8,12},{12,8},{16,20},{20,16},{24,28},{28,24},{1,5},{5... | collective-permute-start | bytes 393224 | tf_op jit(solution)/shard_map/ppermute | solution.py:101
  65.4 5.3 %collective-permute-start.21 = (bf16[256,512]{1,0:T(8,128)(2,1)S(1)}, bf16[256,512]{1,0:T(8,128)(2,1)S(1)}, u32[]{:S(2)}, u32[]{:S(2)}) collective-permute-start(bf16[256,512]{1,0:T(8,128)(2,1)S(1)} %broadcast_select_fusion.11), channel_id=1, source_target_pairs={{0,4},{4,0},{8,12},{12,8},{16,20},{20,16},{24,28},{28,24},{1,5},{5... | collective-permute-start | bytes 786440 | tf_op jit(solution)/shard_map/ppermute | solution.py:101
  72.5 1.1 convolution_convert_fusion.7
  73.6 1.1 convolution_convert_fusion.8
  75.5 1.6 %collective-permute-start.24 = (bf16[256,1024]{1,0:T(8,128)(2,1)}, bf16[256,1024]{1,0:T(8,128)(2,1)}, u32[]{:S(2)}, u32[]{:S(2)}) collective-permute-start(bf16[256,1024]{1,0:T(8,128)(2,1)} %broadcast_select_fusion.2), channel_id=1, source_target_pairs={{0,4},{4,0},{8,12},{12,8},{16,20},{20,16},{24,28},{28,24},{1,5},{5... | collective-permute-start | bytes 1572872 | tf_op jit(solution)/shard_map/ppermute | solution.py:101
  77.3 1.3 %convolution_convert_fusion.10 = bf16[256,256]{1,0:T(8,128)(2,1)S(1)} fusion(bf16[256,256]{1,0:T(8,128)(2,1)S(1)} %convolution_convert_fusion.11, bf16[256,256]{1,0:T(8,128)(2,1)S(1)} %convolution_convert_fusion.17, bf16[4,256,256]{2,1,0:T(8,128)(2,1)S(1)} %get-tuple-element.31, bf16[256,512]{1,0:T(8,128)(2,1)} %copy-done.52, pred[256]{0:T(512)(128)(4,1)} %copy-done.47, ...), kind=kOutput, calls=%fused_computation.64 | convolution fusion | flops 67436544 | bytes 786944 | tf_op jit(solution)/shard_map/dot_general | solution.py:147
  78.7 1.2 %convolution_convert_fusion.13 = bf16[256,256]{1,0:T(8,128)(2,1)S(1)} fusion(bf16[4,256,256]{2,1,0:T(8,128)(2,1)S(1)} %get-tuple-element.32, bf16[256,512]{1,0:T(8,128)(2,1)} %convolution_convert_fusion.7, pred[256]{0:T(512)(128)(4,1)S(1)} %copy-done.45, bf16[2,256,256]{2,1,0:T(8,128)(2,1)S(1)} %copy-done.34), kind=kOutput, calls=%fused_computation.67 | convolution fusion | flops 33685504 | bytes 524800 | tf_op jit(solution)/shard_map/dot_general | solution.py:147
  79.9 1.3 %convolution_convert_fusion.12 = bf16[256,256]{1,0:T(8,128)(2,1)S(1)} fusion(bf16[256,256]{1,0:T(8,128)(2,1)S(1)} %convolution_convert_fusion.13, bf16[256,256]{1,0:T(8,128)(2,1)S(1)} %convolution_convert_fusion.17, bf16[4,256,256]{2,1,0:T(8,128)(2,1)S(1)} %get-tuple-element.31, bf16[256,512]{1,0:T(8,128)(2,1)} %convolution_convert_fusion.7, ...), kind=kOutput, calls=%fused_computation.66 | convolution fusion | flops 67436544 | bytes 786944 | tf_op jit(solution)/shard_map/dot_general | solution.py:147
  81.2 1.2 %convolution_convert_fusion.15 = bf16[256,256]{1,0:T(8,128)(2,1)S(1)} fusion(bf16[4,256,256]{2,1,0:T(8,128)(2,1)S(1)} %get-tuple-element.32, bf16[256,512]{1,0:T(8,128)(2,1)} %convolution_convert_fusion.8, pred[256]{0:T(512)(128)(4,1)S(1)} %copy-done.43, bf16[2,256,256]{2,1,0:T(8,128)(2,1)} %param.7), kind=kOutput, calls=%fused_computation.69 | convolution fusion | flops 33685504 | bytes 524800 | tf_op jit(solution)/shard_map/dot_general | solution.py:147
  82.5 1.4 %convolution_convert_fusion.14 = bf16[256,256]{1,0:T(8,128)(2,1)S(1)} fusion(bf16[256,256]{1,0:T(8,128)(2,1)S(1)} %convolution_convert_fusion.15, bf16[256,256]{1,0:T(8,128)(2,1)S(1)} %convolution_convert_fusion.17, bf16[4,256,256]{2,1,0:T(8,128)(2,1)S(1)} %get-tuple-element.31, bf16[256,512]{1,0:T(8,128)(2,1)} %convolution_convert_fusion.8, ...), kind=kOutput, calls=%fused_computation.68 | convolution fusion | flops 67436544 | bytes 786944 | tf_op jit(solution)/shard_map/dot_general | solution.py:147
  86.0 0.9 copy.30
  87.5 1.1 %convolution_convert_fusion.18 = bf16[256,256]{1,0:T(8,128)(2,1)S(1)} fusion(bf16[256,512]{1,0:T(8,128)(2,1)S(1)} %convolution_convert_fusion.9, pred[256]{0:T(512)(128)(4,1)S(1)} %copy-done.49, bf16[2,256,256]{2,1,0:T(8,128)(2,1)S(1)} %copy-done.35, bf16[4,256,256]{2,1,0:T(8,128)(2,1)} %copy-done.9), kind=kOutput, calls=%fused_computation.72 | convolution fusion | flops 33685504 | bytes 524800 | tf_op jit(solution)/shard_map/dot_general | solution.py:147
  89.4 2.2 %convolution_convert_fusion.16 = bf16[256,256]{1,0:T(8,128)(2,1)} fusion(bf16[256,256]{1,0:T(8,128)(2,1)} %copy-done.28, bf16[256,256]{1,0:T(8,128)(2,1)} %copy-done.32, bf16[256,512]{1,0:T(8,128)(2,1)} %copy-done.51, pred[256]{0:T(512)(128)(4,1)} %get-tuple-element.11, bf16[2,256,256]{2,1,0:T(8,128)(2,1)} %param.7, bf16[4,256,256]{2,1,0:T(8,128)(2,1)} %copy-done.8), kind=kOutput, calls=%fused_computation.70 | convolution fusion | flops 67436544 | bytes 786944 | tf_op jit(solution)/shard_map/dot_general | solution.py:147
  91.5 1.0 tile.40
  92.7 1.1 %add.292 = bf16[256,768]{1,0:T(8,128)(2,1)S(1)} add(bf16[256,768]{1,0:T(8,128)(2,1)S(1)} %add.291, bf16[256,768]{1,0:T(8,128)(2,1)} %collective-permute-done.6) | non-fusion elementwise | flops 196608 | bytes 1179648 | tf_op jit(solution)/shard_map/add | solution.py:97
  94.0 1.3 %broadcast_select_fusion.4 = (bf16[256,1024]{1,0:T(8,128)(2,1)S(1)}, bf16[256,1024]{1,0:T(8,128)(2,1)S(1)}) fusion(bf16[256,1024]{1,0:T(8,128)(2,1)} %broadcast_select_fusion.2, bf16[256,1024]{1,0:T(8,128)(2,1)} %collective-permute-done.24, pred[]{:T(512)S(6)} %eq.331), kind=kLoop, calls=%fused_computation.99 | loop fusion | flops 524288 | bytes 2097153 | tf_op jit(solution)/shard_map/jit(_where)/select_n | solution.py:102
  105.9 2.8 %reshape.410 = bf16[4,256,4,256]{3,2,1,0:T(4,128)(2,1)} reshape(bf16[1024,1024]{1,0:T(8,128)(2,1)S(1)} %pad_maximum_fusion) | data formatting | bytes 4194304 | tf_op jit(solution)/shard_map/reshape | solution.py:174
  (213 shorter events, 33.5 us)
Async XLA Ops:
  8.8 20.0 %collective-permute-start = (bf16[256,256]{1,0:T(8,128)(2,1)}, bf16[256,256]{1,0:T(8,128)(2,1)}, u32[]{:S(2)}, u32[]{:S(2)}) collective-permute-start(bf16[256,256]{1,0:T(8,128)(2,1)} %broadcast_select_fusion.22), channel_id=1, source_target_pairs={{0,4},{4,0},{8,12},{12,8},{16,20},{20,16},{24,28},{28,24},{1,5},{5... | collective-permute-start | bytes 393224 | tf_op jit(solution)/shard_map/ppermute | solution.py:95
  11.0 19.6 %collective-permute-start.14 = (bf16[256,256]{1,0:T(8,128)(2,1)}, bf16[256,256]{1,0:T(8,128)(2,1)}, u32[]{:S(2)}, u32[]{:S(2)}) collective-permute-start(bf16[256,256]{1,0:T(8,128)(2,1)} %bitcast.169), channel_id=1, source_target_pairs={{0,2},{1,3},{4,6},{5,7},{8,10},{9,11},{12,14},{13,15},{16,18},{17,... | collective-permute-start | bytes 393224 | tf_op jit(solution)/shard_map/ppermute | solution.py:83
  13.0 20.5 %collective-permute-start.13 = (bf16[256,256]{1,0:T(8,128)(2,1)}, bf16[256,256]{1,0:T(8,128)(2,1)}, u32[]{:S(2)}, u32[]{:S(2)}) collective-permute-start(bf16[256,256]{1,0:T(8,128)(2,1)} %bitcast.170), channel_id=1, source_target_pairs={{0,2},{1,3},{4,6},{5,7},{8,10},{9,11},{12,14},{13,15},{16,18},{17,... | collective-permute-start | bytes 393224 | tf_op jit(solution)/shard_map/ppermute | solution.py:83
  14.9 21.4 %collective-permute-start.12 = (bf16[256,256]{1,0:T(8,128)(2,1)}, bf16[256,256]{1,0:T(8,128)(2,1)}, u32[]{:S(2)}, u32[]{:S(2)}) collective-permute-start(bf16[256,256]{1,0:T(8,128)(2,1)} %bitcast.171), channel_id=1, source_target_pairs={{0,2},{1,3},{4,6},{5,7},{8,10},{9,11},{12,14},{13,15},{16,18},{17,... | collective-permute-start | bytes 393224 | tf_op jit(solution)/shard_map/ppermute | solution.py:83
  16.9 22.2 %collective-permute-start.11 = (bf16[256,256]{1,0:T(8,128)(2,1)}, bf16[256,256]{1,0:T(8,128)(2,1)}, u32[]{:S(2)}, u32[]{:S(2)}) collective-permute-start(bf16[256,256]{1,0:T(8,128)(2,1)} %bitcast.172), channel_id=1, source_target_pairs={{0,2},{1,3},{4,6},{5,7},{8,10},{9,11},{12,14},{13,15},{16,18},{17,... | collective-permute-start | bytes 393224 | tf_op jit(solution)/shard_map/ppermute | solution.py:83
  26.9 32.3 %copy-start.3 = (bf16[32,8,4,256]{3,1,2,0:T(8,128)(2,1)}, bf16[32,8,4,256]{3,1,2,0:T(8,128)(2,1)S(1)}, u32[]{:S(2)}) copy-start(bf16[32,8,4,256]{3,1,2,0:T(8,128)(2,1)S(1)} %copy.25) | copy-start | bytes 1572868
  27.9 12.2 %copy-start.38 = (s32[256]{0:T(256)S(1)}, s32[256]{0:T(256)}, u32[]{:S(2)}) copy-start(s32[256]{0:T(256)} %iota_add_fusion.4) | copy-start | bytes 3076
  27.9 12.2 %copy-start.41 = (s32[256]{0:T(256)S(1)}, s32[256]{0:T(256)}, u32[]{:S(2)}) copy-start(s32[256]{0:T(256)} %iota_add_fusion.2) | copy-start | bytes 3076
  28.8 43.3 %copy-start.36 = (s32[256]{0:T(256)}, s32[256]{0:T(256)S(1)}, u32[]{:S(2)}) copy-start(s32[256]{0:T(256)S(1)} %get-tuple-element.51) | copy-start | bytes 3076
  29.8 11.3 %collective-permute-start.1 = (bf16[256,256]{1,0:T(8,128)(2,1)S(1)}, bf16[256,256]{1,0:T(8,128)(2,1)S(1)}, u32[]{:S(2)}, u32[]{:S(2)}) collective-permute-start(bf16[256,256]{1,0:T(8,128)(2,1)S(1)} %select_add_fusion.1), channel_id=1, source_target_pairs={{0,8},{4,20},{8,0},{12,28},{16,24},{20,4},{24,16},{28,12},{1,9},{5... | collective-permute-start | bytes 393224 | tf_op jit(solution)/shard_map/ppermute | solution.py:97
  31.6 10.4 %collective-permute-start.18 = (bf16[256,256]{1,0:T(8,128)(2,1)S(1)}, bf16[256,256]{1,0:T(8,128)(2,1)S(1)}, u32[]{:S(2)}, u32[]{:S(2)}) collective-permute-start(bf16[256,256]{1,0:T(8,128)(2,1)S(1)} %broadcast_select_fusion.14), channel_id=1, source_target_pairs={{0,1},{1,0},{2,3},{3,2},{4,5},{5,4},{6,7},{7,6},{8,9},{9,8},{10,11... | collective-permute-start | bytes 393224 | tf_op jit(solution)/shard_map/ppermute | solution.py:86
  34.4 10.2 %collective-permute-start.17 = (bf16[256,256]{1,0:T(8,128)(2,1)S(1)}, bf16[256,256]{1,0:T(8,128)(2,1)S(1)}, u32[]{:S(2)}, u32[]{:S(2)}) collective-permute-start(bf16[256,256]{1,0:T(8,128)(2,1)S(1)} %broadcast_select_fusion.15), channel_id=1, source_target_pairs={{0,1},{1,0},{2,3},{3,2},{4,5},{5,4},{6,7},{7,6},{8,9},{9,8},{10,11... | collective-permute-start | bytes 393224 | tf_op jit(solution)/shard_map/ppermute | solution.py:86
  37.2 10.2 %collective-permute-start.16 = (bf16[256,256]{1,0:T(8,128)(2,1)S(1)}, bf16[256,256]{1,0:T(8,128)(2,1)S(1)}, u32[]{:S(2)}, u32[]{:S(2)}) collective-permute-start(bf16[256,256]{1,0:T(8,128)(2,1)S(1)} %broadcast_select_fusion.16), channel_id=1, source_target_pairs={{0,1},{1,0},{2,3},{3,2},{4,5},{5,4},{6,7},{7,6},{8,9},{9,8},{10,11... | collective-permute-start | bytes 393224 | tf_op jit(solution)/shard_map/ppermute | solution.py:86
  40.0 10.2 %collective-permute-start.15 = (bf16[256,256]{1,0:T(8,128)(2,1)S(1)}, bf16[256,256]{1,0:T(8,128)(2,1)S(1)}, u32[]{:S(2)}, u32[]{:S(2)}) collective-permute-start(bf16[256,256]{1,0:T(8,128)(2,1)S(1)} %broadcast_select_fusion.17), channel_id=1, source_target_pairs={{0,1},{1,0},{2,3},{3,2},{4,5},{5,4},{6,7},{7,6},{8,9},{9,8},{10,11... | collective-permute-start | bytes 393224 | tf_op jit(solution)/shard_map/ppermute | solution.py:86
  41.1 36.0 %copy-start.47 = (pred[256]{0:T(512)(128)(4,1)}, pred[256]{0:T(512)(128)(4,1)S(1)}, u32[]{:S(2)}) copy-start(pred[256]{0:T(512)(128)(4,1)S(1)} %get-tuple-element.14) | copy-start | bytes 772
  41.1 11.4 %collective-permute-start.4 = (bf16[256,768]{1,0:T(8,128)(2,1)S(1)}, bf16[256,768]{1,0:T(8,128)(2,1)S(1)}, u32[]{:S(2)}, u32[]{:S(2)}) collective-permute-start(bf16[256,768]{1,0:T(8,128)(2,1)S(1)} %broadcast_select_fusion.9), channel_id=1, source_target_pairs={{0,4},{4,0},{8,12},{12,8},{16,20},{20,16},{24,28},{28,24},{1,5},{5... | collective-permute-start | bytes 1179656 | tf_op jit(solution)/shard_map/ppermute | solution.py:95
  42.0 17.2 %collective-permute-start.22 = (bf16[256,1024]{1,0:T(8,128)(2,1)S(1)}, bf16[256,1024]{1,0:T(8,128)(2,1)S(1)}, u32[]{:S(2)}, u32[]{:S(2)}) collective-permute-start(bf16[256,1024]{1,0:T(8,128)(2,1)S(1)} %bitcast.193), channel_id=1, source_target_pairs={{0,8},{4,20},{1,9},{5,21},{2,10},{6,22},{3,11},{7,23}} | collective-permute-start | bytes 1572872 | tf_op jit(solution)/shard_map/ppermute | solution.py:129
  44.6 7.1 %collective-permute-start.2 = (bf16[256,256]{1,0:T(8,128)(2,1)S(1)}, bf16[256,256]{1,0:T(8,128)(2,1)S(1)}, u32[]{:S(2)}, u32[]{:S(2)}) collective-permute-start(bf16[256,256]{1,0:T(8,128)(2,1)S(1)} %add.288), channel_id=1, source_target_pairs={{0,16},{4,12},{8,24},{12,4},{16,0},{20,28},{24,8},{28,20},{1,17},{... | collective-permute-start | bytes 393224 | tf_op jit(solution)/shard_map/ppermute | solution.py:97
  50.3 30.9 %copy-start.9 = (bf16[4,256,256]{2,1,0:T(8,128)(2,1)}, bf16[4,256,256]{2,1,0:T(8,128)(2,1)S(1)}, u32[]{:S(2)}) copy-start(bf16[4,256,256]{2,1,0:T(8,128)(2,1)S(1)} %get-tuple-element.32) | copy-start | bytes 1572868
  50.3 32.1 %copy-start.8 = (bf16[4,256,256]{2,1,0:T(8,128)(2,1)}, bf16[4,256,256]{2,1,0:T(8,128)(2,1)S(1)}, u32[]{:S(2)}) copy-start(bf16[4,256,256]{2,1,0:T(8,128)(2,1)S(1)} %get-tuple-element.31) | copy-start | bytes 1572868
  50.4 7.4 %collective-permute-start.19 = (bf16[256,512]{1,0:T(8,128)(2,1)S(1)}, bf16[256,512]{1,0:T(8,128)(2,1)S(1)}, u32[]{:S(2)}, u32[]{:S(2)}) collective-permute-start(bf16[256,512]{1,0:T(8,128)(2,1)S(1)} %pad_maximum_fusion.7), channel_id=1, source_target_pairs={{0,8},{4,20},{1,9},{5,21},{2,10},{6,22},{3,11},{7,23}} | collective-permute-start | bytes 786440 | tf_op jit(solution)/shard_map/ppermute | solution.py:129
  51.8 3.7 %collective-permute-start.3 = (bf16[256,256]{1,0:T(8,128)(2,1)S(1)}, bf16[256,256]{1,0:T(8,128)(2,1)S(1)}, u32[]{:S(2)}, u32[]{:S(2)}) collective-permute-start(bf16[256,256]{1,0:T(8,128)(2,1)S(1)} %add.289), channel_id=1, source_target_pairs={{0,4},{4,0},{8,12},{12,8},{16,20},{20,16},{24,28},{28,24},{1,5},{5... | collective-permute-start | bytes 393224 | tf_op jit(solution)/shard_map/ppermute | solution.py:101
  51.8 3.7 %collective-permute-start.8 = (bf16[256,256]{1,0:T(8,128)(2,1)S(1)}, bf16[256,256]{1,0:T(8,128)(2,1)S(1)}, u32[]{:S(2)}, u32[]{:S(2)}) collective-permute-start(bf16[256,256]{1,0:T(8,128)(2,1)S(1)} %add.289), channel_id=1, source_target_pairs={{1,3},{4,6},{9,11},{12,14},{17,19},{20,22},{25,27},{28,30}} | collective-permute-start | bytes 393224 | tf_op jit(solution)/shard_map/ppermute | solution.py:116
  52.6 18.1 %copy-start.33 = (bf16[2,256,256]{2,1,0:T(8,128)(2,1)S(1)}, bf16[2,256,256]{2,1,0:T(8,128)(2,1)}, u32[]{:S(2)}) copy-start(bf16[2,256,256]{2,1,0:T(8,128)(2,1)} %param.7) | copy-start | bytes 786436
  52.6 18.5 %collective-permute-start.5 = (bf16[256,768]{1,0:T(8,128)(2,1)S(1)}, bf16[256,768]{1,0:T(8,128)(2,1)S(1)}, u32[]{:S(2)}, u32[]{:S(2)}) collective-permute-start(bf16[256,768]{1,0:T(8,128)(2,1)S(1)} %select_add_fusion), channel_id=1, source_target_pairs={{0,8},{4,20},{8,0},{12,28},{16,24},{20,4},{24,16},{28,12},{1,9},{5... | collective-permute-start | bytes 1179656 | tf_op jit(solution)/shard_map/ppermute | solution.py:97
  56.2 6.6 %collective-permute-start.9 = (bf16[256,256]{1,0:T(8,128)(2,1)S(1)}, bf16[256,256]{1,0:T(8,128)(2,1)S(1)}, u32[]{:S(2)}, u32[]{:S(2)}) collective-permute-start(bf16[256,256]{1,0:T(8,128)(2,1)S(1)} %get-tuple-element.39), channel_id=1, source_target_pairs={{1,0},{3,2},{4,5},{6,7},{9,8},{11,10},{12,13},{14,15},{17,16},{19,... | collective-permute-start | bytes 393224 | tf_op jit(solution)/shard_map/ppermute | solution.py:122
  57.9 7.4 %collective-permute-start.20 = (bf16[256,512]{1,0:T(8,128)(2,1)S(1)}, bf16[256,512]{1,0:T(8,128)(2,1)S(1)}, u32[]{:S(2)}, u32[]{:S(2)}) collective-permute-start(bf16[256,512]{1,0:T(8,128)(2,1)S(1)} %broadcast_select_fusion.10), channel_id=1, source_target_pairs={{0,16},{8,24},{4,12},{20,28},{1,17},{9,25},{5,13},{21,29},{2,18},{... | collective-permute-start | bytes 786440 | tf_op jit(solution)/shard_map/ppermute | solution.py:129
  59.3 15.4 %collective-permute-start.23 = (bf16[256,1024]{1,0:T(8,128)(2,1)S(1)}, bf16[256,1024]{1,0:T(8,128)(2,1)S(1)}, u32[]{:S(2)}, u32[]{:S(2)}) collective-permute-start(bf16[256,1024]{1,0:T(8,128)(2,1)S(1)} %broadcast_select_fusion.1), channel_id=1, source_target_pairs={{0,16},{8,24},{4,12},{20,28},{1,17},{9,25},{5,13},{21,29},{2,18},{... | collective-permute-start | bytes 1572872 | tf_op jit(solution)/shard_map/ppermute | solution.py:129
  62.8 9.0 %copy-start.30 = (bf16[2,256,256]{2,1,0:T(8,128)(2,1)S(1)}, bf16[2,256,256]{2,1,0:T(8,128)(2,1)}, u32[]{:S(2)}) copy-start(bf16[2,256,256]{2,1,0:T(8,128)(2,1)} %param.6) | copy-start | bytes 786436
  62.8 7.9 %collective-permute-start.10 = (bf16[256,256]{1,0:T(8,128)(2,1)S(1)}, bf16[256,256]{1,0:T(8,128)(2,1)S(1)}, u32[]{:S(2)}, u32[]{:S(2)}) collective-permute-start(bf16[256,256]{1,0:T(8,128)(2,1)S(1)} %broadcast_select_fusion.19), channel_id=1, source_target_pairs={{0,4},{4,0},{8,12},{12,8},{16,20},{20,16},{24,28},{28,24},{1,5},{5... | collective-permute-start | bytes 393224 | tf_op jit(solution)/shard_map/ppermute | solution.py:101
  65.4 6.7 %collective-permute-start.21 = (bf16[256,512]{1,0:T(8,128)(2,1)S(1)}, bf16[256,512]{1,0:T(8,128)(2,1)S(1)}, u32[]{:S(2)}, u32[]{:S(2)}) collective-permute-start(bf16[256,512]{1,0:T(8,128)(2,1)S(1)} %broadcast_select_fusion.11), channel_id=1, source_target_pairs={{0,4},{4,0},{8,12},{12,8},{16,20},{20,16},{24,28},{28,24},{1,5},{5... | collective-permute-start | bytes 786440 | tf_op jit(solution)/shard_map/ppermute | solution.py:101
  71.3 21.4 %collective-permute-start.6 = (bf16[256,768]{1,0:T(8,128)(2,1)S(1)}, bf16[256,768]{1,0:T(8,128)(2,1)}, u32[]{:S(2)}, u32[]{:S(2)}) collective-permute-start(bf16[256,768]{1,0:T(8,128)(2,1)S(1)} %add.291), channel_id=1, source_target_pairs={{0,16},{4,12},{8,24},{12,4},{16,0},{20,28},{24,8},{28,20},{1,17},{... | collective-permute-start | bytes 1179656 | tf_op jit(solution)/shard_map/ppermute | solution.py:97
  72.0 10.5 %copy-start.32 = (bf16[256,256]{1,0:T(8,128)(2,1)}, bf16[256,256]{1,0:T(8,128)(2,1)S(1)}, u32[]{:S(2)}) copy-start(bf16[256,256]{1,0:T(8,128)(2,1)S(1)} %convolution_convert_fusion.17) | copy-start | bytes 393220
  72.5 4.6 %copy-start.52 = (bf16[256,512]{1,0:T(8,128)(2,1)}, bf16[256,512]{1,0:T(8,128)(2,1)S(1)}, u32[]{:S(2)}) copy-start(bf16[256,512]{1,0:T(8,128)(2,1)S(1)} %convolution_convert_fusion.6) | copy-start | bytes 786436
  72.5 4.8 %copy-start.34 = (bf16[2,256,256]{2,1,0:T(8,128)(2,1)S(1)}, bf16[2,256,256]{2,1,0:T(8,128)(2,1)}, u32[]{:S(2)}) copy-start(bf16[2,256,256]{2,1,0:T(8,128)(2,1)} %param.7) | copy-start | bytes 786436
  73.6 5.1 %copy-start.45 = (pred[256]{0:T(512)(128)(4,1)S(1)}, pred[256]{0:T(512)(128)(4,1)}, u32[]{:S(2)}) copy-start(pred[256]{0:T(512)(128)(4,1)} %get-tuple-element.13) | copy-start | bytes 772
  74.6 6.6 %copy-start.43 = (pred[256]{0:T(512)(128)(4,1)S(1)}, pred[256]{0:T(512)(128)(4,1)}, u32[]{:S(2)}) copy-start(pred[256]{0:T(512)(128)(4,1)} %get-tuple-element.12) | copy-start | bytes 772
  75.5 18.5 %collective-permute-start.24 = (bf16[256,1024]{1,0:T(8,128)(2,1)}, bf16[256,1024]{1,0:T(8,128)(2,1)}, u32[]{:S(2)}, u32[]{:S(2)}) collective-permute-start(bf16[256,1024]{1,0:T(8,128)(2,1)} %broadcast_select_fusion.2), channel_id=1, source_target_pairs={{0,4},{4,0},{8,12},{12,8},{16,20},{20,16},{24,28},{28,24},{1,5},{5... | collective-permute-start | bytes 1572872 | tf_op jit(solution)/shard_map/ppermute | solution.py:101
  77.3 7.0 %copy-start.21 = (bf16[256,256]{1,0:T(8,128)(2,1)}, bf16[256,256]{1,0:T(8,128)(2,1)S(1)}, u32[]{:S(2)}) copy-start(bf16[256,256]{1,0:T(8,128)(2,1)S(1)} %convolution_convert_fusion.11) | copy-start | bytes 393220
  77.3 6.6 %copy-start.39 = (s32[256]{0:T(256)S(1)}, s32[256]{0:T(256)}, u32[]{:S(2)}) copy-start(s32[256]{0:T(256)} %iota_add_fusion.4) | copy-start | bytes 3076
  78.7 5.9 %copy-start.14 = (bf16[256,256]{1,0:T(8,128)(2,1)}, bf16[256,256]{1,0:T(8,128)(2,1)S(1)}, u32[]{:S(2)}) copy-start(bf16[256,256]{1,0:T(8,128)(2,1)S(1)} %convolution_convert_fusion.10) | copy-start | bytes 393220
  79.9 5.7 %copy-start.23 = (bf16[256,256]{1,0:T(8,128)(2,1)}, bf16[256,256]{1,0:T(8,128)(2,1)S(1)}, u32[]{:S(2)}) copy-start(bf16[256,256]{1,0:T(8,128)(2,1)S(1)} %convolution_convert_fusion.13) | copy-start | bytes 393220
  81.2 4.6 %copy-start.12 = (bf16[256,256]{1,0:T(8,128)(2,1)}, bf16[256,256]{1,0:T(8,128)(2,1)S(1)}, u32[]{:S(2)}) copy-start(bf16[256,256]{1,0:T(8,128)(2,1)S(1)} %convolution_convert_fusion.12) | copy-start | bytes 393220
  83.9 3.3 %copy-start.10 = (bf16[256,256]{1,0:T(8,128)(2,1)}, bf16[256,256]{1,0:T(8,128)(2,1)S(1)}, u32[]{:S(2)}) copy-start(bf16[256,256]{1,0:T(8,128)(2,1)S(1)} %convolution_convert_fusion.14) | copy-start | bytes 393220
  84.3 3.1 %copy-start.51 = (bf16[256,512]{1,0:T(8,128)(2,1)}, bf16[256,512]{1,0:T(8,128)(2,1)S(1)}, u32[]{:S(2)}) copy-start(bf16[256,512]{1,0:T(8,128)(2,1)S(1)} %convolution_convert_fusion.9) | copy-start | bytes 786436
  92.6 2.7 %copy-start.4 = (bf16[32,8,4,256]{3,1,2,0:T(8,128)(2,1)S(1)}, bf16[32,8,4,256]{3,1,2,0:T(8,128)(2,1)}, u32[]{:S(2)}) copy-start(bf16[32,8,4,256]{3,1,2,0:T(8,128)(2,1)} %copy-done.3) | copy-start | bytes 1572868
  92.6 2.7 %copy-start.40 = (s32[256]{0:T(256)S(1)}, s32[256]{0:T(256)}, u32[]{:S(2)}) copy-start(s32[256]{0:T(256)} %iota_add_fusion.4) | copy-start | bytes 3076
  93.9 4.1 %collective-permute-start.7 = (bf16[256,768]{1,0:T(8,128)(2,1)S(1)}, bf16[256,768]{1,0:T(8,128)(2,1)S(1)}, u32[]{:S(2)}, u32[]{:S(2)}) collective-permute-start(bf16[256,768]{1,0:T(8,128)(2,1)S(1)} %add.292), channel_id=1, source_target_pairs={{0,4},{4,0},{8,12},{12,8},{16,20},{20,16},{24,28},{28,24},{1,5},{5... | collective-permute-start | bytes 1179656 | tf_op jit(solution)/shard_map/ppermute | solution.py:101
  (30 other events, 37.8 us)

commit v2 on v0

v2 whole, which is shorter than its diff:
```python
import functools

import jax
import jax.numpy as jnp
from jax import lax
from jax.experimental import pallas as pl
from jax.experimental.pallas import tpu as pltpu
from jax.sharding import PartitionSpec as P

BF, F32 = jnp.bfloat16, jnp.float32
VMEM = pl.BlockSpec(memory_space=pltpu.VMEM)
SMEM = pl.BlockSpec(memory_space=pltpu.SMEM)
ANY = pl.BlockSpec(memory_space=pl.ANY)
WEIGHT = 10**11


def bits_of(count):
    return list(range(1, count.bit_length() - 1))


def exchange_pairs(count, level):
    order = bits_of(count)
    return [(i, i ^ (1 << (order[level] if i % 2 == 0 else order[-1 - level]))) for i in range(count)]


def spread_pairs(count, levels):
    held, steps = [0, 1], []
    for level in levels:
        pairs = [pair for pair in exchange_pairs(count, level) if pair[0] in held]
        held = held + [target for _, target in pairs]
        steps.append(pairs)
    return steps


def far_steps(count):
    steps = []
    distance = count // 2
    while distance >= 2:
        steps.append([(i, i + distance) for i in range(count) if i % (2 * distance) < 2])
        distance //= 2
    return steps


def twin(count):
    return [(i, i ^ 1) for i in range(count)]


def member(index, pairs):
    return sum((index == t).astype(jnp.int32) for _, t in pairs) > 0


def after(value, *others):
    return lax.optimization_barrier((value, *others))[0]


def dot(a, b):
    return jnp.dot(a, b, preferred_element_type=F32)


def call(body, outs, args, in_specs, out_specs, scratch=(), flops=10**6):
    return pl.pallas_call(
        body,
        out_shape=outs,
        in_specs=in_specs,
        out_specs=out_specs,
        scratch_shapes=list(scratch),
        compiler_params=pltpu.CompilerParams(vmem_limit_bytes=24 << 20),
        cost_estimate=pl.CostEstimate(flops=flops, bytes_accessed=0, transcendentals=0),
    )(*args)


def first_kernel(a, piece, top, held, sem):
    copy = pltpu.make_async_copy(a.at[0], held, sem)
    copy.start()
    copy.wait()
    turned = jnp.transpose(held[...], (1, 0, 2))
    piece[...] = turned[0]
    top[...] = turned


def join_kernel(keep, got, top, out):
    across = keep.shape[0]
    out[:across] = keep[...] + got[...]
    out[across:] = top[...]


def merge_kernel(taken, part, got, out):
    across = part.shape[0] // 2
    out[:across] = part[:across] + got[:across]

    @pl.when(taken[0] > 0)
    def _():
        out[across:] = got[across:]

    @pl.when(taken[0] == 0)
    def _():
        out[across:] = part[across:]


def pick_kernel(nr, me, a, row, first_piece, flat, keep, give, middle, last, goes,
                raw, turned, hot, raw_sems, flat_sems):
    down, block, across, width = a.shape
    for b in range(down):
        pltpu.make_async_copy(a.at[b], raw.at[b], raw_sems.at[b]).start()
    my_row = me[0]
    even = my_row % 2 == 0
    first, second = row[0:1], row[1:2]
    i = lax.broadcasted_iota(jnp.int32, (block, block), 0)
    j = lax.broadcasted_iota(jnp.int32, (block, block), 1)

    def stand(line):
        line = jnp.where(i == j, line.astype(F32), 0.0)
        return jnp.sum(line, axis=1, keepdims=True).astype(jnp.int32)

    first_down, second_down = stand(first), stand(second)

    def found(mask, value, axis):
        value = jnp.where(mask, value.astype(F32), 0.0)
        count = jnp.sum(mask.astype(F32), axis=axis, keepdims=True)
        return count > 0.5, jnp.sum(value, axis=axis, keepdims=True).astype(jnp.int32)

    same = second_down == first
    hit, at = found(same, j, 1)
    second_source = jnp.where(hit, at, second_down)
    hit, at = found(first == block + i, jnp.broadcast_to(second_down, i.shape), 0)
    first_goes = jnp.where(hit, at, first)
    hit, at = found(same, i, 0)
    goes[0:1, :block] = jnp.where(hit, block + at, first_goes)
    hit, at = found(first_down == block + j, i, 0)
    goes[0:1, block:] = jnp.where(hit, at, second)

    kept = jnp.where(even, first_down, second_source)
    given = jnp.where(even, second_source, first_down)
    for b in range(down):
        base = (b * nr + my_row) * block
        hot[:block, b * block : (b + 1) * block] = (kept - base == j).astype(BF)
        hot[block:, b * block : (b + 1) * block] = (given - base == j).astype(BF)
    for b in range(down):
        pltpu.make_async_copy(a.at[b], raw.at[b], raw_sems.at[b]).wait()
        turned[:, b] = jnp.transpose(raw[b], (1, 0, 2))
        pltpu.make_async_copy(turned.at[:, b], flat.at[:, b], flat_sems.at[b]).start()
        if b == down - 1:
            last[...] = turned[0, b]
        elif b > 0:
            middle[b - 1] = turned[0, b]
    for c in range(across):
        picked = dot(hot[...], turned[c].reshape(down * block, width)).astype(BF)
        keep[c] = picked[:block]
        give[c] = picked[block:]
    for b in range(down):
        pltpu.make_async_copy(turned.at[:, b], flat.at[:, b], flat_sems.at[b]).wait()


def finish_kernel(nr, nc, parts, me, goes, lower, upper, *refs):
    across, down, block, width = refs[0].shape
    sources, rest = refs[:parts], refs[parts:]
    out = rest[0]
    held = rest[1 : 1 + parts]
    mix, u0, u1, r0, r1, result, in_sems, sems = rest[-8:]
    copies = [pltpu.make_async_copy(s, h, in_sems.at[k]) for k, (s, h) in enumerate(zip(sources, held))]
    for copy in copies:
        copy.start()
    flat, head_mine, head_other, tail_mine, tail_other, side_mine, side_other, top_mine, top_other = held[:9]
    rim_mine, rim_other = held[9:11]
    have, other = held[11:14], held[14:17]
    my_row, my_col = me[0], me[1]
    even = my_row % 2 == 0
    even_col = my_col % 2 == 0
    for k in range(1, 11):
        copies[k].wait()

    def both(mine, others):
        return jnp.where(even, mine, others), jnp.where(even, others, mine)

    side01, side10 = both(side_mine[...], side_other[...])
    u0p = dot(lower[0], side01).astype(BF)
    lp = dot(side10, upper[0]).astype(BF)
    for c in range(across):
        if c == 0:
            a0, a1 = both(head_mine[...], head_other[...])
        else:
            a0, a1 = both(tail_mine[c - 1], tail_other[c - 1])
        u = dot(lower[0], a0).astype(BF)
        a1 = (a1.astype(F32) - dot(lp, u)).astype(BF)
        if c == 0:
            r0[...] = a0
            r1[...] = a1
        t0, t1 = both(top_mine[c], top_other[c])
        mix[c, :block] = t0
        mix[c, block : 2 * block] = t1
        mix[c, 2 * block : 3 * block] = u
        mix[c, 3 * block :] = dot(lower[1], a1).astype(BF)
    rim = [jnp.concatenate(both(rim_mine[k], rim_other[k]), 0) for k in range(2)]
    for k in [0] + list(range(11, 17)):
        copies[k].wait()
    place = lax.broadcasted_iota(jnp.int32, (block, 2 * block), 0)
    for b in range(down):
        base = (b * nr + my_row) * block
        match = goes[...] - base == place
        onehot = match.astype(BF)
        hit = jnp.sum(match.astype(F32), axis=1, keepdims=True) > 0.5
        if b == 0:
            h, o = have[0][...], other[0][...]
        elif b == down - 1:
            h, o = have[2][...], other[2][...]
        else:
            h, o = have[1][b - 1], other[1][b - 1]
        z0 = jnp.where(hit, dot(onehot, rim[0]).astype(BF), jnp.where(even_col, h, o))
        z1 = jnp.where(hit, dot(onehot, rim[1]).astype(BF), jnp.where(even_col, o, h))
        l0 = dot(z0, upper[0]).astype(BF)
        l1 = dot((z1.astype(F32) - dot(l0, u0p)).astype(BF), upper[1]).astype(BF)
        factors = jnp.concatenate([onehot, -l0, -l1], 1)
        blocks = []
        for c in range(across):
            kept = jnp.where(hit, jnp.zeros((), BF), flat[c, b])
            s = (kept.astype(F32) + dot(factors, mix[c])).astype(BF)
            if c == 0:
                s = jnp.where(my_col == 0, l0, jnp.where(my_col == 1, l1, s))
            if b == 0:
                w0, w1 = mix[c, 2 * block : 3 * block], mix[c, 3 * block :]
                if c == 0:
                    w0 = jnp.where(my_col == 0, r0[...], w0)
                    w1 = jnp.where(my_col == 0, lp, jnp.where(my_col == 1, r1[...], w1))
                s = jnp.where(my_row == 0, w0, jnp.where(my_row == 1, w1, s))
            blocks.append(s)
        result[b] = jnp.transpose(jnp.stack(blocks), (1, 0, 2))
        pltpu.make_async_copy(result.at[b], out.at[b], sems.at[b]).start()
    for b in range(down):
        pltpu.make_async_copy(result.at[b], out.at[b], sems.at[b]).wait()


def local(matrix, pivots, lower_inverse, upper_inverse):
    nr = lax.axis_size("prow")
    nc = lax.axis_size("pcol")
    my_row = lax.axis_index("prow")
    my_col = lax.axis_index("pcol")
    down, block, across, width = matrix.shape
    joined = ("prow", "pcol")
    me = jnp.stack([my_row, my_col]).astype(jnp.int32)
    even_col = my_col % 2 == 0
    shape = lambda *s: jax.ShapeDtypeStruct(s, BF)
    depth = len(bits_of(nr))
    top_steps = spread_pairs(nr, [depth - 1] + list(range(depth - 1)) if depth else [])
    rim_steps = spread_pairs(nr, list(range(depth)))

    def far(piece):
        for pairs in far_steps(nc):
            got = lax.ppermute(piece, "pcol", pairs)
            piece = jnp.where(member(my_col, pairs), got, piece)
        return piece

    def near(piece):
        return lax.ppermute(piece, "pcol", twin(nc))

    def swap(part):
        return lax.ppermute(part, "prow", twin(nr))

    def pick(pairs, got, part):
        return jnp.where(member(my_row, pairs), got, part)

    first_piece, top = call(
        first_kernel, [shape(block, width), shape(across, block, width)], [matrix], [ANY], [VMEM] * 2,
        [pltpu.VMEM((block, across, width), BF), pltpu.SemaphoreType.DMA],
    )
    have0 = far(first_piece)
    for pairs in top_steps[:1]:
        top = pick(pairs, lax.ppermute(top, "prow", pairs), top)

    flat, keep, give, middle, last, goes = call(
        functools.partial(pick_kernel, nr),
        [shape(across, down, block, width), shape(across, block, width),
         shape(across, block, width), shape(down - 2, block, width), shape(block, width),
         jax.ShapeDtypeStruct((1, 2 * block), jnp.int32)],
        [me, matrix, pivots, first_piece],
        [SMEM, ANY, VMEM, ANY],
        [ANY] + [VMEM] * 5,
        [pltpu.VMEM(matrix.shape, BF), pltpu.VMEM((across, down, block, width), BF),
         pltpu.VMEM((2 * block, down * block), BF),
         pltpu.SemaphoreType.DMA((down,)), pltpu.SemaphoreType.DMA((down,))],
    )
    have1, have2 = far(middle), far(last)
    other0 = near(after(have0, keep))
    rim = jnp.stack([jnp.where(even_col, have0, other0), jnp.where(even_col, other0, have0)])

    part = call(
        join_kernel, shape(2 * across, block, width), [keep, swap(after(give, have0)), top], [VMEM] * 3, VMEM, flops=WEIGHT
    )
    for pairs in rim_steps[:-1]:
        rim = pick(pairs, lax.ppermute(after(rim, have1), "prow", pairs), rim)
    for level in range(depth - 1):
        pairs = exchange_pairs(nr, level)
        taken = member(my_row, top_steps[level + 1]).astype(jnp.int32)[None]
        part = call(
            merge_kernel, shape(2 * across, block, width), [taken, part, lax.ppermute(part, "prow", pairs)],
            [SMEM, VMEM, VMEM], VMEM, flops=WEIGHT,
        )
    head, tail, top = part[0], part[1:across], part[across:]
    if depth > 0:
        pairs = exchange_pairs(nr, depth - 1)
        head = head + lax.ppermute(head, "prow", pairs)
        got = lax.ppermute(jnp.concatenate([tail, rim]), "prow", pairs)
        tail = tail + got[: across - 1]
        rim = pick(rim_steps[-1], got[across - 1 :], rim)

    side = after(head, have2)
    for pairs in far_steps(nc):
        joint = [(i * nc + s, i * nc + t) for i in range(nr) for s, t in pairs if s % 2 != i % 2]
        got = lax.ppermute(side, joined, joint)
        right = member(my_col, pairs) & (my_col % 2 != my_row % 2)
        side = jnp.where(right, got, side)
    joint = [(i * nc + s, i * nc + (s ^ 1)) for i in range(nr) for s in range(nc) if s % 2 != i % 2]
    other1 = near(have1)
    side = jnp.where(my_col % 2 == my_row % 2, lax.ppermute(side, joined, joint), side)
    other2 = near(have2)

    args = [me, goes, lower_inverse, upper_inverse]
    parts = [flat, head, swap(head), tail, swap(tail), side, swap(side), top, swap(top), rim, swap(rim),
             have0, have1, have2, other0, other1, other2]
    return call(
        functools.partial(finish_kernel, nr, nc, len(parts)),
        shape(*matrix.shape),
        args + parts,
        [SMEM] + [VMEM] * 3 + [ANY] * len(parts),
        ANY,
        [pltpu.VMEM(p.shape, BF) for p in parts] +
        [pltpu.VMEM((across, 4 * block, width), BF)] + [pltpu.VMEM((block, width), BF)] * 4 +
        [pltpu.VMEM(matrix.shape, BF), pltpu.SemaphoreType.DMA((len(parts),)), pltpu.SemaphoreType.DMA((down,))],
    )


def solution(mesh):
    in_specs = (P(None, "prow", None, "pcol"), P(), P(), P())
    out_specs = P(None, "prow", None, "pcol")
    return jax.shard_map(local, mesh=mesh, in_specs=in_specs, out_specs=out_specs, check_vma=False)
```

time: 361 us -> 73.3 us (0.20)
  waiting for transfers between devices: 297 us -> 11.9 us
  starting transfers between devices: 0.39 us -> 35 us
  local copies, waits for them, and re-layouts: 20.3 us -> 5.48 us
  Pallas kernels: 0 us -> 14.5 us
  matrix products: 13.9 us -> 0 us
  between operations: 13.7 us -> 0.32 us
  other arithmetic: 15.3 us -> 5.64 us
    psum x6 -> x0, waiting for transfers between devices: 297 us -> none  [spread(): return lax.psum(block, axis)]
    ppermute x0 -> x19, starting transfers between devices: none -> 35 us  [the longest x3 12.4 us: far(): got = lax.ppermute(piece, 'pcol', pairs)]
    pallas_call x0 -> x5, Pallas kernels: none -> 14.5 us  [call(): pl.pallas_call(body, out_shape=outs, in_specs=in_specs, out_specs=out_spe...]
    dot_general x6 -> x0, matrix products: 13.9 us -> none  [the longest x2 7.27 us: local(): product = jnp.dot(lower, upper, preferred_element_type=jnp.float32)]
    ppermute x0 -> x19, waiting for transfers between devices: none -> 11.9 us  [the longest x3 5.48 us: near(): return lax.ppermute(piece, 'pcol', twin(nc))]
    scatter x3 -> x0, local copies, waits for them, and re-layouts: 8.77 us -> none  [the longest x2 8.71 us: local(): current = current.at[target].set(old_top, mode='drop')]
    scatter x4 -> x0, other arithmetic: 6.45 us -> none  [the longest x3 3.5 us: local(): current.at[top_first:top_first + block]]
    gather x2 -> x0, local copies, waits for them, and re-layouts: 4.58 us -> none  [local(): current[safe_index]]
  transfers between devices with their start and end apart: 6 -> 19, of which waited for: 6 -> 6; matrix products, arithmetic and copies ran while one was open for 2% -> 8% of each run, Pallas kernels for 0% -> 6%
where the time goes in v2:
time: 73.3 us; the launch traced here: 72.9 us
  starting transfers between devices  35 us (48%)
  Pallas kernels  14.5 us (20%)
  waiting for transfers between devices  11.9 us (16%)
  other arithmetic  5.64 us (8%)
  local copies, waits for them, and re-layouts  5.48 us (7%)
    pallas_call x5, Pallas kernels, call(): pl.pallas_call(body, out_shape=outs, in_specs=in_specs, out_specs=out_spe...  14.5 us
    ppermute x3, starting transfers between devices, far(): got = lax.ppermute(piece, 'pcol', pairs)  12.4 us
    ppermute x3, starting transfers between devices, near(): return lax.ppermute(piece, 'pcol', twin(nc))  8.28 us
    ppermute x3, waiting for transfers between devices, near(): return lax.ppermute(piece, 'pcol', twin(nc))  5.48 us
    unnamed x32, local copies, waits for them, and re-layouts  5.41 us
    ppermute x1, starting transfers between devices, local(): top = pick(pairs, lax.ppermute(top, 'prow', pairs), top)  4.22 us
    ppermute x6, starting transfers between devices, swap(): return lax.ppermute(part, 'prow', twin(nr))  3.63 us
    ppermute x1, waiting for transfers between devices, local(): rim = pick(pairs, lax.ppermute(after(rim, have1), 'prow', pairs), rim)  3.23 us
  transfers between devices with their start and end apart: 19, of which 6 were waited for; matrix products, arithmetic and copies ran while one was open for 8% of the time, Pallas kernels for 6%

profile of v2, /device:TPU:0, one launch (start us, length us, event | category | flops | bytes accessed | tf_op | source)
XLA Modules:
  0.0 72.9 jit_solution(5094341123590796099)
XLA Ops:
  0.0 1.6 %copy-done = bf16[4,256,4,256]{3,2,1,0:T(4,128)(2,1)S(1)} copy-done((bf16[4,256,4,256]{3,2,1,0:T(4,128)(2,1)S(1)}, bf16[4,256,4,256]{3,2,1,0:T(4,128)(2,1)}, u32[]{:S(2)}) %copy-start) | copy-done | bytes 2097176
  1.6 0.2 shard_map.46
  1.8 6.1 %collective-permute-start = (bf16[256,256]{1,0:T(8,128)(2,1)S(1)}, bf16[256,256]{1,0:T(8,128)(2,1)S(1)}, u32[]{:S(2)}, u32[]{:S(2)}) collective-permute-start(bf16[256,256]{1,0:T(8,128)(2,1)S(1)} %get-tuple-element.17.first_piece), channel_id=1, source_target_pairs={{0,2},{1,3},{4,6},{5,7},{8,10},{9,11},{12,14},{13,15},{16,18},{17,... | collective-permute-start | bytes 393224 | tf_op jit(solution)/shard_map/ppermute | solution.py:248
  7.9 4.2 %collective-permute-start.2 = (bf16[4,256,256]{2,1,0:T(8,128)(2,1)S(1)}, bf16[4,256,256]{2,1,0:T(8,128)(2,1)}, u32[]{:S(2)}, u32[]{:S(2)}) collective-permute-start(bf16[4,256,256]{2,1,0:T(8,128)(2,1)S(1)} %get-tuple-element.23), channel_id=1, source_target_pairs={{0,16},{4,12},{1,17},{5,13},{2,18},{6,14},{3,19},{7,15}} | collective-permute-start | bytes 1572872 | tf_op jit(solution)/shard_map/ppermute | solution.py:267
  12.1 0.1 pad_add_fusion.me
  12.2 4.2 %shard_map.47 = (bf16[4,4,256,256]{3,2,1,0:T(8,128)(2,1)S(1)}, bf16[4,256,256]{2,1,0:T(8,128)(2,1)S(1)}, bf16[4,256,256]{2,1,0:T(8,128)(2,1)}, bf16[2,256,256]{2...) custom-call(s32[2]{0:T(128)S(1)} %pad_add_fusion.me, bf16[4,256,4,256]{3,2,1,0:T(4,128)(2,1)S(1)} %copy-done.1, ...), custom_call_target="tpu_custom_call" | custom-call | flops 1000000 | tf_op jit(solution)/shard_map/pallas_call | solution.py:61
  16.4 0.0 copy-start.2
  16.4 1.3 %copy-done.2 = bf16[4,4,256,256]{3,2,1,0:T(8,128)(2,1)} copy-done((bf16[4,4,256,256]{3,2,1,0:T(8,128)(2,1)}, bf16[4,4,256,256]{3,2,1,0:T(8,128)(2,1)S(1)}, u32[]{:S(2)}) %copy-start.2) | copy-done | bytes 2097176
  17.7 0.8 %copy-done.11 = bf16[4,256,256]{2,1,0:T(8,128)(2,1)} copy-done((bf16[4,256,256]{2,1,0:T(8,128)(2,1)}, bf16[4,256,256]{2,1,0:T(8,128)(2,1)S(1)}, u32[]{:S(2)}) %copy-start.11) | copy-done | bytes 524312
  18.5 0.0 collective-permute-done
  18.5 0.1 collective-permute-start.1
  18.6 2.0 %collective-permute-start.7 = (bf16[2,256,256]{2,1,0:T(8,128)(2,1)S(1)}, bf16[2,256,256]{2,1,0:T(8,128)(2,1)}, u32[]{:S(2)}, u32[]{:S(2)}) collective-permute-start(bf16[2,256,256]{2,1,0:T(8,128)(2,1)S(1)} %get-tuple-element.25), channel_id=1, source_target_pairs={{0,2},{1,3},{4,6},{5,7},{8,10},{9,11},{12,14},{13,15},{16,18},{17,... | collective-permute-start | bytes 786440 | tf_op jit(solution)/shard_map/ppermute | solution.py:248
  20.6 1.6 %collective-permute-start.6 = (bf16[256,256]{1,0:T(8,128)(2,1)S(1)}, bf16[256,256]{1,0:T(8,128)(2,1)S(1)}, u32[]{:S(2)}, u32[]{:S(2)}) collective-permute-start(bf16[256,256]{1,0:T(8,128)(2,1)S(1)} %broadcast_select_fusion.6.refs_11_), channel_id=1, source_target_pairs={{0,1},{1,0},{2,3},{3,2},{4,5},{5,4},{6,7},{7,6},{8,9},{9,8},{10,11... | collective-permute-start | bytes 393224 | tf_op jit(solution)/shard_map/ppermute | solution.py:253
  22.2 0.0 collective-permute-done.2
  22.2 0.1 broadcast_select_fusion.top
  22.3 1.0 %copy-done.12 = bf16[4,256,256]{2,1,0:T(8,128)(2,1)S(1)} copy-done((bf16[4,256,256]{2,1,0:T(8,128)(2,1)S(1)}, bf16[4,256,256]{2,1,0:T(8,128)(2,1)}, u32[]{:S(2)}) %copy-start.12) | copy-done | bytes 524312
  23.3 0.1 shard_map.48.part
  23.4 0.4 collective-permute-start.3
  23.8 5.5 %collective-permute-done.6.refs_14_ = bf16[256,256]{1,0:T(8,128)(2,1)S(1)} collective-permute-done((bf16[256,256]{1,0:T(8,128)(2,1)S(1)}, bf16[256,256]{1,0:T(8,128)(2,1)S(1)}, u32[]{:S(2)}, u32[]{:S(2)}) %collective-permute-start.6) | collective-permute-done | bytes 131104 | tf_op jit(solution)/shard_map/ppermute | solution.py:253
  29.3 0.0 collective-permute-done.7
  29.3 0.7 %broadcast_select_fusion.1.refs_12_ = bf16[2,256,256]{2,1,0:T(8,128)(2,1)} fusion(bf16[2,256,256]{2,1,0:T(8,128)(2,1)} %collective-permute-done.7, bf16[2,256,256]{2,1,0:T(8,128)(2,1)S(1)} %get-tuple-element.25, pred[]{:T(512)S(6)} %gt.19), kind=kLoop, calls=%fused_computation.5 | loop fusion | flops 131072 | bytes 786433 | tf_op jit(solution)/shard_map/jit(_where)/select_n | solution.py:249
  30.1 1.3 %collective-permute-start.8 = (bf16[2,256,256]{2,1,0:T(8,128)(2,1)S(1)}, bf16[2,256,256]{2,1,0:T(8,128)(2,1)S(1)}, u32[]{:S(2)}, u32[]{:S(2)}) collective-permute-start(bf16[2,256,256]{2,1,0:T(8,128)(2,1)S(1)} %pad_maximum_fusion.1), channel_id=1, source_target_pairs={{0,8},{4,20},{1,9},{5,21},{2,10},{6,22},{3,11},{7,23}} | collective-permute-start | bytes 786440 | tf_op jit(solution)/shard_map/ppermute | solution.py:289
  31.4 4.3 %collective-permute-start.11 = (bf16[256,256]{1,0:T(8,128)(2,1)}, bf16[256,256]{1,0:T(8,128)(2,1)}, u32[]{:S(2)}, u32[]{:S(2)}) collective-permute-start(bf16[256,256]{1,0:T(8,128)(2,1)} %get-tuple-element.27), channel_id=1, source_target_pairs={{0,2},{1,3},{4,6},{5,7},{8,10},{9,11},{12,14},{13,15},{16,18},{17,... | collective-permute-start | bytes 393224 | tf_op jit(solution)/shard_map/ppermute | solution.py:248
  35.7 3.2 %collective-permute-done.8 = bf16[2,256,256]{2,1,0:T(8,128)(2,1)S(1)} collective-permute-done((bf16[2,256,256]{2,1,0:T(8,128)(2,1)S(1)}, bf16[2,256,256]{2,1,0:T(8,128)(2,1)S(1)}, u32[]{:S(2)}, u32[]{:S(2)}) %collective-permute-start.8) | collective-permute-done | bytes 262176 | tf_op jit(solution)/shard_map/ppermute | solution.py:289
  38.9 0.0 collective-permute-done.3.got
  39.0 0.6 copy-done.15
  39.6 0.1 shard_map.49
  39.7 0.1 collective-permute-start.4
  39.9 0.9 %pad_maximum_fusion = bf16[5,256,256]{2,1,0:T(8,128)(2,1)} fusion(bf16[2,256,256]{2,1,0:T(8,128)(2,1)S(1)} %broadcast_select_fusion.2, bf16[3,256,256]{2,1,0:T(8,128)(2,1)S(1)} %slice.21), kind=kLoop, calls=%fused_computation | loop fusion | flops 327680 | bytes 1310720 | tf_op jit(solution)/shard_map/concatenate | solution.py:301
  40.8 2.0 %collective-permute-start.9 = (bf16[5,256,256]{2,1,0:T(8,128)(2,1)}, bf16[5,256,256]{2,1,0:T(8,128)(2,1)}, u32[]{:S(2)}, u32[]{:S(2)}) collective-permute-start(bf16[5,256,256]{2,1,0:T(8,128)(2,1)} %pad_maximum_fusion), channel_id=1, source_target_pairs={{0,16},{4,12},{8,24},{12,4},{16,0},{20,28},{24,8},{28,20},{1,17},{... | collective-permute-start | bytes 1966088 | tf_op jit(solution)/shard_map/ppermute | solution.py:301
  42.8 1.6 %broadcast_select_fusion.5.refs_13_ = bf16[256,256]{1,0:T(8,128)(2,1)} fusion(bf16[256,256]{1,0:T(8,128)(2,1)} %collective-permute-done.11, bf16[256,256]{1,0:T(8,128)(2,1)} %get-tuple-element.27, pred[]{:T(512)S(6)} %gt.19), kind=kLoop, calls=%fused_computation.12 | loop fusion | flops 65536 | bytes 393217 | tf_op jit(solution)/shard_map/jit(_where)/select_n | solution.py:249
  44.3 0.5 collective-permute-done.4
  44.8 0.0 copy-start.3
  44.8 1.4 %collective-permute-start.12 = (bf16[256,256]{1,0:T(8,128)(2,1)S(1)}, bf16[256,256]{1,0:T(8,128)(2,1)}, u32[]{:S(2)}, u32[]{:S(2)}) collective-permute-start(bf16[256,256]{1,0:T(8,128)(2,1)S(1)} %fusion.refs_1_), channel_id=1, source_target_pairs={{1,3},{4,6},{9,11},{12,14},{17,19},{20,22},{25,27},{28,30}} | collective-permute-start | bytes 393224 | tf_op jit(solution)/shard_map/ppermute | solution.py:308
  46.3 6.6 %collective-permute-start.18 = (bf16[256,256]{1,0:T(8,128)(2,1)}, bf16[256,256]{1,0:T(8,128)(2,1)S(1)}, u32[]{:S(2)}, u32[]{:S(2)}) collective-permute-start(bf16[256,256]{1,0:T(8,128)(2,1)} %broadcast_select_fusion.5.refs_13_), channel_id=1, source_target_pairs={{0,1},{1,0},{2,3},{3,2},{4,5},{5,4},{6,7},{7,6},{8,9},{9,8},{10,11... | collective-permute-start | bytes 393224 | tf_op jit(solution)/shard_map/ppermute | solution.py:253
  52.9 0.1 collective-permute-start.17
  53.0 0.1 collective-permute-start.15
  53.1 0.0 collective-permute-done.12
  53.1 1.3 %collective-permute-start.13 = (bf16[256,256]{1,0:T(8,128)(2,1)S(1)}, bf16[256,256]{1,0:T(8,128)(2,1)S(1)}, u32[]{:S(2)}, u32[]{:S(2)}) collective-permute-start(bf16[256,256]{1,0:T(8,128)(2,1)S(1)} %broadcast_select_fusion.3), channel_id=1, source_target_pairs={{1,0},{3,2},{4,5},{6,7},{9,8},{11,10},{12,13},{14,15},{17,16},{19,... | collective-permute-start | bytes 393224 | tf_op jit(solution)/shard_map/ppermute | solution.py:313
  54.4 1.0 %slice_add_fusion.refs_3_ = bf16[3,256,256]{2,1,0:T(8,128)(2,1)S(1)} fusion(bf16[5,256,256]{2,1,0:T(8,128)(2,1)} %collective-permute-done.9, bf16[8,256,256]{2,1,0:T(8,128)(2,1)S(1)} %shard_map.49), kind=kLoop, calls=%fused_computation.2 | loop fusion | flops 196608 | bytes 1179648 | tf_op jit(solution)/shard_map/add | solution.py:302
  55.5 2.8 %collective-permute-start.10 = (bf16[3,256,256]{2,1,0:T(8,128)(2,1)S(1)}, bf16[3,256,256]{2,1,0:T(8,128)(2,1)S(1)}, u32[]{:S(2)}, u32[]{:S(2)}) collective-permute-start(bf16[3,256,256]{2,1,0:T(8,128)(2,1)S(1)} %slice_add_fusion.refs_3_), channel_id=1, source_target_pairs={{0,4},{4,0},{8,12},{12,8},{16,20},{20,16},{24,28},{28,24},{1,5},{5... | collective-permute-start | bytes 1179656 | tf_op jit(solution)/shard_map/ppermute | solution.py:256
  58.3 1.1 %slice_select_fusion.refs_9_ = bf16[2,256,256]{2,1,0:T(8,128)(2,1)S(1)} fusion(bf16[5,256,256]{2,1,0:T(8,128)(2,1)} %collective-permute-done.9, pred[]{:T(512)S(6)} %gt.22, bf16[2,256,256]{2,1,0:T(8,128)(2,1)} %copy-done.15, bf16[1,256,256]{2,1,0:T(8,128)(2,1)} %copy-done.14, bf16[1,256,256]{2,1,0:T(8,128)(2,1)} %copy-done.13, pred[]{:T(512)S(6)} %gt.21), kind=kLoop, calls=%fused_computation.3 | loop fusion | flops 393216 | bytes 1048578 | tf_op jit(solution)/shard_map/jit(_where)/select_n | solution.py:259
  59.4 1.5 %collective-permute-done.13 = bf16[256,256]{1,0:T(8,128)(2,1)S(1)} collective-permute-done((bf16[256,256]{1,0:T(8,128)(2,1)S(1)}, bf16[256,256]{1,0:T(8,128)(2,1)S(1)}, u32[]{:S(2)}, u32[]{:S(2)}) %collective-permute-start.13) | collective-permute-done | bytes 131104 | tf_op jit(solution)/shard_map/ppermute | solution.py:313
  60.9 0.6 collective-permute-start.5
  61.5 0.1 collective-permute-start.14
  61.6 1.0 %collective-permute-done.5.refs_2_ = bf16[256,256]{1,0:T(8,128)(2,1)S(1)} collective-permute-done((bf16[256,256]{1,0:T(8,128)(2,1)S(1)}, bf16[256,256]{1,0:T(8,128)(2,1)S(1)}, u32[]{:S(2)}, u32[]{:S(2)}) %collective-permute-start.5) | collective-permute-done | bytes 131104 | tf_op jit(solution)/shard_map/ppermute | solution.py:256
  62.6 0.2 collective-permute-done.14.refs_6_
  62.9 10.0 %shard_map.50 = bf16[4,256,4,256]{3,2,1,0:T(4,128)(2,1)} custom-call(s32[2]{0:T(128)S(1)} %copy-done.10, s32[1,512]{1,0:T(1,128)S(1)} %get-tuple-element.18.goes, bf16[2,256,256]{2,1,0:T(8,128)(2,1)S(1)} %copy-done.6, bf16[2,256,256]{2,1,0:T(8,128)(2,1)S(1)} %copy-done.7, bf16[4,4,256,256]{3,2,1,0:T(8,128)(2,1)S(1)} %copy-done.3, ...), custom_call_target="tpu_custom_call" | custom-call | flops 1000000 | tf_op jit(solution)/shard_map/pallas_call | solution.py:61
  (44 shorter events, 0.3 us)
Async XLA Ops:
  0.0 1.6 %copy-start = (bf16[4,256,4,256]{3,2,1,0:T(4,128)(2,1)S(1)}, bf16[4,256,4,256]{3,2,1,0:T(4,128)(2,1)}, u32[]{:S(2)}) copy-start(bf16[4,256,4,256]{3,2,1,0:T(4,128)(2,1)} %a.3) | copy-start | bytes 6291460
  1.6 10.6 %copy-start.1 = (bf16[4,256,4,256]{3,2,1,0:T(4,128)(2,1)S(1)}, bf16[4,256,4,256]{3,2,1,0:T(4,128)(2,1)}, u32[]{:S(2)}) copy-start(bf16[4,256,4,256]{3,2,1,0:T(4,128)(2,1)} %a.3) | copy-start | bytes 6291460
  1.6 10.6 %copy-start.8 = (s32[2,256]{1,0:T(2,128)S(1)}, s32[2,256]{1,0:T(2,128)}, u32[]{:S(2)}) copy-start(s32[2,256]{1,0:T(2,128)} %row.1) | copy-start | bytes 6148
  1.8 16.7 %collective-permute-start = (bf16[256,256]{1,0:T(8,128)(2,1)S(1)}, bf16[256,256]{1,0:T(8,128)(2,1)S(1)}, u32[]{:S(2)}, u32[]{:S(2)}) collective-permute-start(bf16[256,256]{1,0:T(8,128)(2,1)S(1)} %get-tuple-element.17.first_piece), channel_id=1, source_target_pairs={{0,2},{1,3},{4,6},{5,7},{8,10},{9,11},{12,14},{13,15},{16,18},{17,... | collective-permute-start | bytes 393224 | tf_op jit(solution)/shard_map/ppermute | solution.py:248
  7.9 14.3 %collective-permute-start.2 = (bf16[4,256,256]{2,1,0:T(8,128)(2,1)S(1)}, bf16[4,256,256]{2,1,0:T(8,128)(2,1)}, u32[]{:S(2)}, u32[]{:S(2)}) collective-permute-start(bf16[4,256,256]{2,1,0:T(8,128)(2,1)S(1)} %get-tuple-element.23), channel_id=1, source_target_pairs={{0,16},{4,12},{1,17},{5,13},{2,18},{6,14},{3,19},{7,15}} | collective-permute-start | bytes 1572872 | tf_op jit(solution)/shard_map/ppermute | solution.py:267
  12.2 4.2 %copy-start.9 = (s32[2]{0:T(128)}, s32[2]{0:T(128)S(1)}, u32[]{:S(2)}) copy-start(s32[2]{0:T(128)S(1)} %pad_add_fusion.me) | copy-start | bytes 28
  16.4 1.3 %copy-start.2 = (bf16[4,4,256,256]{3,2,1,0:T(8,128)(2,1)}, bf16[4,4,256,256]{3,2,1,0:T(8,128)(2,1)S(1)}, u32[]{:S(2)}) copy-start(bf16[4,4,256,256]{3,2,1,0:T(8,128)(2,1)S(1)} %get-tuple-element.19.refs_0_) | copy-start | bytes 6291460
  17.7 0.8 %copy-start.11 = (bf16[4,256,256]{2,1,0:T(8,128)(2,1)}, bf16[4,256,256]{2,1,0:T(8,128)(2,1)S(1)}, u32[]{:S(2)}) copy-start(bf16[4,256,256]{2,1,0:T(8,128)(2,1)S(1)} %get-tuple-element.20.keep) | copy-start | bytes 1572868
  18.5 3.7 %collective-permute-start.1 = (bf16[4,256,256]{2,1,0:T(8,128)(2,1)}, bf16[4,256,256]{2,1,0:T(8,128)(2,1)S(1)}, u32[]{:S(2)}, u32[]{:S(2)}) collective-permute-start(bf16[4,256,256]{2,1,0:T(8,128)(2,1)} %get-tuple-element.22), channel_id=1, source_target_pairs={{0,4},{4,0},{8,12},{12,8},{16,20},{20,16},{24,28},{28,24},{1,5},{5... | collective-permute-start | bytes 1572872 | tf_op jit(solution)/shard_map/ppermute | solution.py:256
  18.6 10.7 %collective-permute-start.7 = (bf16[2,256,256]{2,1,0:T(8,128)(2,1)S(1)}, bf16[2,256,256]{2,1,0:T(8,128)(2,1)}, u32[]{:S(2)}, u32[]{:S(2)}) collective-permute-start(bf16[2,256,256]{2,1,0:T(8,128)(2,1)S(1)} %get-tuple-element.25), channel_id=1, source_target_pairs={{0,2},{1,3},{4,6},{5,7},{8,10},{9,11},{12,14},{13,15},{16,18},{17,... | collective-permute-start | bytes 786440 | tf_op jit(solution)/shard_map/ppermute | solution.py:248
  20.6 8.6 %collective-permute-start.6 = (bf16[256,256]{1,0:T(8,128)(2,1)S(1)}, bf16[256,256]{1,0:T(8,128)(2,1)S(1)}, u32[]{:S(2)}, u32[]{:S(2)}) collective-permute-start(bf16[256,256]{1,0:T(8,128)(2,1)S(1)} %broadcast_select_fusion.6.refs_11_), channel_id=1, source_target_pairs={{0,1},{1,0},{2,3},{3,2},{4,5},{5,4},{6,7},{7,6},{8,9},{9,8},{10,11... | collective-permute-start | bytes 393224 | tf_op jit(solution)/shard_map/ppermute | solution.py:253
  22.3 1.0 %copy-start.12 = (bf16[4,256,256]{2,1,0:T(8,128)(2,1)S(1)}, bf16[4,256,256]{2,1,0:T(8,128)(2,1)}, u32[]{:S(2)}) copy-start(bf16[4,256,256]{2,1,0:T(8,128)(2,1)} %copy-done.11) | copy-start | bytes 1572868
  23.4 15.5 %collective-permute-start.3 = (bf16[8,256,256]{2,1,0:T(8,128)(2,1)S(1)}, bf16[8,256,256]{2,1,0:T(8,128)(2,1)S(1)}, u32[]{:S(2)}, u32[]{:S(2)}) collective-permute-start(bf16[8,256,256]{2,1,0:T(8,128)(2,1)S(1)} %shard_map.48.part), channel_id=1, source_target_pairs={{0,8},{4,20},{8,0},{12,28},{16,24},{20,4},{24,16},{28,12},{1,9},{5... | collective-permute-start | bytes 3145736 | tf_op jit(solution)/shard_map/ppermute | solution.py:294
  29.3 9.7 %copy-start.13 = (bf16[1,256,256]{2,1,0:T(8,128)(2,1)}, bf16[1,256,256]{2,1,0:T(8,128)(2,1)S(1)}, u32[]{:S(2)}) copy-start(bf16[1,256,256]{2,1,0:T(8,128)(2,1)S(1)} %get-tuple-element.29) | copy-start | bytes 393220
  29.3 9.7 %copy-start.14 = (bf16[1,256,256]{2,1,0:T(8,128)(2,1)}, bf16[1,256,256]{2,1,0:T(8,128)(2,1)S(1)}, u32[]{:S(2)}) copy-start(bf16[1,256,256]{2,1,0:T(8,128)(2,1)S(1)} %get-tuple-element.30) | copy-start | bytes 393220
  30.1 8.8 %collective-permute-start.8 = (bf16[2,256,256]{2,1,0:T(8,128)(2,1)S(1)}, bf16[2,256,256]{2,1,0:T(8,128)(2,1)S(1)}, u32[]{:S(2)}, u32[]{:S(2)}) collective-permute-start(bf16[2,256,256]{2,1,0:T(8,128)(2,1)S(1)} %pad_maximum_fusion.1), channel_id=1, source_target_pairs={{0,8},{4,20},{1,9},{5,21},{2,10},{6,22},{3,11},{7,23}} | collective-permute-start | bytes 786440 | tf_op jit(solution)/shard_map/ppermute | solution.py:289
  31.4 11.4 %collective-permute-start.11 = (bf16[256,256]{1,0:T(8,128)(2,1)}, bf16[256,256]{1,0:T(8,128)(2,1)}, u32[]{:S(2)}, u32[]{:S(2)}) collective-permute-start(bf16[256,256]{1,0:T(8,128)(2,1)} %get-tuple-element.27), channel_id=1, source_target_pairs={{0,2},{1,3},{4,6},{5,7},{8,10},{9,11},{12,14},{13,15},{16,18},{17,... | collective-permute-start | bytes 393224 | tf_op jit(solution)/shard_map/ppermute | solution.py:248
  38.9 0.7 copy-start.15
  39.7 5.0 %collective-permute-start.4 = (bf16[256,256]{1,0:T(8,128)(2,1)S(1)}, bf16[256,256]{1,0:T(8,128)(2,1)S(1)}, u32[]{:S(2)}, u32[]{:S(2)}) collective-permute-start(bf16[256,256]{1,0:T(8,128)(2,1)S(1)} %slice_bitcast_fusion), channel_id=1, source_target_pairs={{0,16},{4,12},{8,24},{12,4},{16,0},{20,28},{24,8},{28,20},{1,17},{... | collective-permute-start | bytes 393224 | tf_op jit(solution)/shard_map/ppermute | solution.py:300
  40.8 13.7 %collective-permute-start.9 = (bf16[5,256,256]{2,1,0:T(8,128)(2,1)}, bf16[5,256,256]{2,1,0:T(8,128)(2,1)}, u32[]{:S(2)}, u32[]{:S(2)}) collective-permute-start(bf16[5,256,256]{2,1,0:T(8,128)(2,1)} %pad_maximum_fusion), channel_id=1, source_target_pairs={{0,16},{4,12},{8,24},{12,4},{16,0},{20,28},{24,8},{28,20},{1,17},{... | collective-permute-start | bytes 1966088 | tf_op jit(solution)/shard_map/ppermute | solution.py:301
  44.8 18.1 %copy-start.3 = (bf16[4,4,256,256]{3,2,1,0:T(8,128)(2,1)S(1)}, bf16[4,4,256,256]{3,2,1,0:T(8,128)(2,1)}, u32[]{:S(2)}) copy-start(bf16[4,4,256,256]{3,2,1,0:T(8,128)(2,1)} %copy-done.2) | copy-start | bytes 6291460
  44.8 18.1 %copy-start.10 = (s32[2]{0:T(128)S(1)}, s32[2]{0:T(128)}, u32[]{:S(2)}) copy-start(s32[2]{0:T(128)} %copy-done.9) | copy-start | bytes 28
  44.8 8.3 %collective-permute-start.12 = (bf16[256,256]{1,0:T(8,128)(2,1)S(1)}, bf16[256,256]{1,0:T(8,128)(2,1)}, u32[]{:S(2)}, u32[]{:S(2)}) collective-permute-start(bf16[256,256]{1,0:T(8,128)(2,1)S(1)} %fusion.refs_1_), channel_id=1, source_target_pairs={{1,3},{4,6},{9,11},{12,14},{17,19},{20,22},{25,27},{28,30}} | collective-permute-start | bytes 393224 | tf_op jit(solution)/shard_map/ppermute | solution.py:308
  46.3 16.6 %copy-start.4 = (bf16[2,256,256]{2,1,0:T(8,128)(2,1)S(1)}, bf16[2,256,256]{2,1,0:T(8,128)(2,1)}, u32[]{:S(2)}) copy-start(bf16[2,256,256]{2,1,0:T(8,128)(2,1)} %broadcast_select_fusion.1.refs_12_) | copy-start | bytes 786436
  46.3 16.6 %copy-start.5 = (bf16[256,256]{1,0:T(8,128)(2,1)S(1)}, bf16[256,256]{1,0:T(8,128)(2,1)}, u32[]{:S(2)}) copy-start(bf16[256,256]{1,0:T(8,128)(2,1)} %broadcast_select_fusion.5.refs_13_) | copy-start | bytes 393220
  46.3 16.6 %copy-start.6 = (bf16[2,256,256]{2,1,0:T(8,128)(2,1)S(1)}, bf16[2,256,256]{2,1,0:T(8,128)(2,1)}, u32[]{:S(2)}) copy-start(bf16[2,256,256]{2,1,0:T(8,128)(2,1)} %lower.1) | copy-start | bytes 786436
  46.3 16.6 %copy-start.7 = (bf16[2,256,256]{2,1,0:T(8,128)(2,1)S(1)}, bf16[2,256,256]{2,1,0:T(8,128)(2,1)}, u32[]{:S(2)}) copy-start(bf16[2,256,256]{2,1,0:T(8,128)(2,1)} %upper.1) | copy-start | bytes 786436
  46.3 14.6 %collective-permute-start.18 = (bf16[256,256]{1,0:T(8,128)(2,1)}, bf16[256,256]{1,0:T(8,128)(2,1)S(1)}, u32[]{:S(2)}, u32[]{:S(2)}) collective-permute-start(bf16[256,256]{1,0:T(8,128)(2,1)} %broadcast_select_fusion.5.refs_13_), channel_id=1, source_target_pairs={{0,1},{1,0},{2,3},{3,2},{4,5},{5,4},{6,7},{7,6},{8,9},{9,8},{10,11... | collective-permute-start | bytes 393224 | tf_op jit(solution)/shard_map/ppermute | solution.py:253
  52.9 8.6 %collective-permute-start.17 = (bf16[2,256,256]{2,1,0:T(8,128)(2,1)}, bf16[2,256,256]{2,1,0:T(8,128)(2,1)S(1)}, u32[]{:S(2)}, u32[]{:S(2)}) collective-permute-start(bf16[2,256,256]{2,1,0:T(8,128)(2,1)} %broadcast_select_fusion.1.refs_12_), channel_id=1, source_target_pairs={{0,1},{1,0},{2,3},{3,2},{4,5},{5,4},{6,7},{7,6},{8,9},{9,8},{10,11... | collective-permute-start | bytes 786440 | tf_op jit(solution)/shard_map/ppermute | solution.py:253
  53.0 9.6 %collective-permute-start.15 = (bf16[4,256,256]{2,1,0:T(8,128)(2,1)S(1)}, bf16[4,256,256]{2,1,0:T(8,128)(2,1)S(1)}, u32[]{:S(2)}, u32[]{:S(2)}) collective-permute-start(bf16[4,256,256]{2,1,0:T(8,128)(2,1)S(1)} %slice.23.refs_7_), channel_id=1, source_target_pairs={{0,4},{4,0},{8,12},{12,8},{16,20},{20,16},{24,28},{28,24},{1,5},{5... | collective-permute-start | bytes 1572872 | tf_op jit(solution)/shard_map/ppermute | solution.py:256
  53.1 7.7 %collective-permute-start.13 = (bf16[256,256]{1,0:T(8,128)(2,1)S(1)}, bf16[256,256]{1,0:T(8,128)(2,1)S(1)}, u32[]{:S(2)}, u32[]{:S(2)}) collective-permute-start(bf16[256,256]{1,0:T(8,128)(2,1)S(1)} %broadcast_select_fusion.3), channel_id=1, source_target_pairs={{1,0},{3,2},{4,5},{6,7},{9,8},{11,10},{12,13},{14,15},{17,16},{19,... | collective-permute-start | bytes 393224 | tf_op jit(solution)/shard_map/ppermute | solution.py:313
  55.5 7.4 %collective-permute-start.10 = (bf16[3,256,256]{2,1,0:T(8,128)(2,1)S(1)}, bf16[3,256,256]{2,1,0:T(8,128)(2,1)S(1)}, u32[]{:S(2)}, u32[]{:S(2)}) collective-permute-start(bf16[3,256,256]{2,1,0:T(8,128)(2,1)S(1)} %slice_add_fusion.refs_3_), channel_id=1, source_target_pairs={{0,4},{4,0},{8,12},{12,8},{16,20},{20,16},{24,28},{28,24},{1,5},{5... | collective-permute-start | bytes 1179656 | tf_op jit(solution)/shard_map/ppermute | solution.py:256
  60.9 2.0 %collective-permute-start.16 = (bf16[2,256,256]{2,1,0:T(8,128)(2,1)S(1)}, bf16[2,256,256]{2,1,0:T(8,128)(2,1)S(1)}, u32[]{:S(2)}, u32[]{:S(2)}) collective-permute-start(bf16[2,256,256]{2,1,0:T(8,128)(2,1)S(1)} %slice_select_fusion.refs_9_), channel_id=1, source_target_pairs={{0,4},{4,0},{8,12},{12,8},{16,20},{20,16},{24,28},{28,24},{1,5},{5... | collective-permute-start | bytes 786440 | tf_op jit(solution)/shard_map/ppermute | solution.py:256
  60.9 1.7 %collective-permute-start.5 = (bf16[256,256]{1,0:T(8,128)(2,1)S(1)}, bf16[256,256]{1,0:T(8,128)(2,1)S(1)}, u32[]{:S(2)}, u32[]{:S(2)}) collective-permute-start(bf16[256,256]{1,0:T(8,128)(2,1)S(1)} %fusion.refs_1_), channel_id=1, source_target_pairs={{0,4},{4,0},{8,12},{12,8},{16,20},{20,16},{24,28},{28,24},{1,5},{5... | collective-permute-start | bytes 393224 | tf_op jit(solution)/shard_map/ppermute | solution.py:256
  61.5 1.3 %collective-permute-start.14 = (bf16[256,256]{1,0:T(8,128)(2,1)S(1)}, bf16[256,256]{1,0:T(8,128)(2,1)S(1)}, u32[]{:S(2)}, u32[]{:S(2)}) collective-permute-start(bf16[256,256]{1,0:T(8,128)(2,1)S(1)} %broadcast_select_fusion.4.refs_5_), channel_id=1, source_target_pairs={{0,4},{4,0},{8,12},{12,8},{16,20},{20,16},{24,28},{28,24},{1,5},{5... | collective-permute-start | bytes 393224 | tf_op jit(solution)/shard_map/ppermute | solution.py:256

commit v3 on v2

--- a/solution.py
+++ b/solution.py
@@ -11,6 +11,7 @@
 VMEM = pl.BlockSpec(memory_space=pltpu.VMEM)
 SMEM = pl.BlockSpec(memory_space=pltpu.SMEM)
 ANY = pl.BlockSpec(memory_space=pl.ANY)
+HBM = pl.BlockSpec(memory_space=pltpu.HBM)
 WEIGHT = 10**11
 
 
@@ -57,14 +58,14 @@
     return jnp.dot(a, b, preferred_element_type=F32)
 
 
-def call(body, outs, args, in_specs, out_specs, scratch=(), flops=10**6):
+def call(body, outs, args, in_specs, out_specs, scratch=(), flops=10**6, limit=10):
     return pl.pallas_call(
         body,
         out_shape=outs,
         in_specs=in_specs,
         out_specs=out_specs,
         scratch_shapes=list(scratch),
-        compiler_params=pltpu.CompilerParams(vmem_limit_bytes=24 << 20),
+        compiler_params=pltpu.CompilerParams(vmem_limit_bytes=limit << 20),
         cost_estimate=pl.CostEstimate(flops=flops, bytes_accessed=0, transcendentals=0),
     )(*args)
 
@@ -97,8 +98,8 @@
         out[across:] = part[across:]
 
 
-def pick_kernel(nr, me, a, row, first_piece, flat, keep, give, middle, last, goes,
-                raw, turned, hot, raw_sems, flat_sems):
+def pick_kernel(nr, me, a, row, first_piece, keep, give, middle, last, goes,
+                raw, turned, hot, raw_sems):
     down, block, across, width = a.shape
     for b in range(down):
         pltpu.make_async_copy(a.at[b], raw.at[b], raw_sems.at[b]).start()
@@ -138,7 +139,6 @@
     for b in range(down):
         pltpu.make_async_copy(a.at[b], raw.at[b], raw_sems.at[b]).wait()
         turned[:, b] = jnp.transpose(raw[b], (1, 0, 2))
-        pltpu.make_async_copy(turned.at[:, b], flat.at[:, b], flat_sems.at[b]).start()
         if b == down - 1:
             last[...] = turned[0, b]
         elif b > 0:
@@ -147,27 +147,33 @@
         picked = dot(hot[...], turned[c].reshape(down * block, width)).astype(BF)
         keep[c] = picked[:block]
         give[c] = picked[block:]
-    for b in range(down):
-        pltpu.make_async_copy(turned.at[:, b], flat.at[:, b], flat_sems.at[b]).wait()
+
+
+def turn_kernel(a, gate, out, raw, turned, raw_sems, sems):
+    down = a.shape[0]
+    for b in range(down):
+        pltpu.make_async_copy(a.at[b], raw.at[b], raw_sems.at[b]).start()
+    for b in range(down):
+        pltpu.make_async_copy(a.at[b], raw.at[b], raw_sems.at[b]).wait()
+        turned[:, b] = jnp.transpose(raw[b], (1, 0, 2))
+        pltpu.make_async_copy(turned.at[:, b], out.at[:, b], sems.at[b]).start()
+    for b in range(down):
+        pltpu.make_async_copy(turned.at[:, b], out.at[:, b], sems.at[b]).wait()
 
 
 def finish_kernel(nr, nc, parts, me, goes, lower, upper, *refs):
-    across, down, block, width = refs[0].shape
-    sources, rest = refs[:parts], refs[parts:]
-    out = rest[0]
-    held = rest[1 : 1 + parts]
-    mix, u0, u1, r0, r1, result, in_sems, sems = rest[-8:]
+    flat, head_mine, head_other, tail_mine, tail_other, side_mine, side_other, top_mine, top_other, rim_mine, rim_other, have0, have1, have2, other0, other1, other2 = refs[:17]
+    sources, rest = refs[17 : 17 + parts], refs[17 + parts :]
+    out, held = rest[0], rest[1 : 1 + parts]
+    mix, r0, r1, result, in_sems, sems = rest[1 + parts :]
     copies = [pltpu.make_async_copy(s, h, in_sems.at[k]) for k, (s, h) in enumerate(zip(sources, held))]
     for copy in copies:
         copy.start()
-    flat, head_mine, head_other, tail_mine, tail_other, side_mine, side_other, top_mine, top_other = held[:9]
-    rim_mine, rim_other = held[9:11]
-    have, other = held[11:14], held[14:17]
+    have, other = (have0, have1, have2), (other0, other1, other2)
+    across, down, block, width = flat.shape
     my_row, my_col = me[0], me[1]
     even = my_row % 2 == 0
     even_col = my_col % 2 == 0
-    for k in range(1, 11):
-        copies[k].wait()
 
     def both(mine, others):
         return jnp.where(even, mine, others), jnp.where(even, others, mine)
@@ -191,40 +197,47 @@
         mix[c, 2 * block : 3 * block] = u
         mix[c, 3 * block :] = dot(lower[1], a1).astype(BF)
     rim = [jnp.concatenate(both(rim_mine[k], rim_other[k]), 0) for k in range(2)]
-    for k in [0] + list(range(11, 17)):
-        copies[k].wait()
+    for copy in copies:
+        copy.wait()
     place = lax.broadcasted_iota(jnp.int32, (block, 2 * block), 0)
-    for b in range(down):
-        base = (b * nr + my_row) * block
-        match = goes[...] - base == place
+    half = max(down // 2, 1)
+    for h in range(0, down, half):
+        match = jnp.concatenate([goes[...] - (b * nr + my_row) * block == place for b in range(h, h + half)], 0)
         onehot = match.astype(BF)
         hit = jnp.sum(match.astype(F32), axis=1, keepdims=True) > 0.5
-        if b == 0:
-            h, o = have[0][...], other[0][...]
-        elif b == down - 1:
-            h, o = have[2][...], other[2][...]
-        else:
-            h, o = have[1][b - 1], other[1][b - 1]
-        z0 = jnp.where(hit, dot(onehot, rim[0]).astype(BF), jnp.where(even_col, h, o))
-        z1 = jnp.where(hit, dot(onehot, rim[1]).astype(BF), jnp.where(even_col, o, h))
+
+        def rows_of(three):
+            first, middle, last = three
+            picked = []
+            for b in range(h, h + half):
+                picked.append(first[...] if b == 0 else last[...] if b == down - 1 else middle[b - 1])
+            return jnp.concatenate(picked, 0)
+
+        mine, others = rows_of(have), rows_of(other)
+        z0 = jnp.where(hit, dot(onehot, rim[0]).astype(BF), jnp.where(even_col, mine, others))
+        z1 = jnp.where(hit, dot(onehot, rim[1]).astype(BF), jnp.where(even_col, others, mine))
         l0 = dot(z0, upper[0]).astype(BF)
         l1 = dot((z1.astype(F32) - dot(l0, u0p)).astype(BF), upper[1]).astype(BF)
         factors = jnp.concatenate([onehot, -l0, -l1], 1)
         blocks = []
         for c in range(across):
-            kept = jnp.where(hit, jnp.zeros((), BF), flat[c, b])
+            kept = jnp.where(hit, jnp.zeros((), BF), flat[c, h : h + half].reshape(half * block, width))
             s = (kept.astype(F32) + dot(factors, mix[c])).astype(BF)
             if c == 0:
                 s = jnp.where(my_col == 0, l0, jnp.where(my_col == 1, l1, s))
+            blocks.append(s)
+        for b in range(h, h + half):
+            held_rows = slice((b - h) * block, (b - h + 1) * block)
+            tiles = [s[held_rows] for s in blocks]
             if b == 0:
-                w0, w1 = mix[c, 2 * block : 3 * block], mix[c, 3 * block :]
-                if c == 0:
-                    w0 = jnp.where(my_col == 0, r0[...], w0)
-                    w1 = jnp.where(my_col == 0, lp, jnp.where(my_col == 1, r1[...], w1))
-                s = jnp.where(my_row == 0, w0, jnp.where(my_row == 1, w1, s))
-            blocks.append(s)
-        result[b] = jnp.transpose(jnp.stack(blocks), (1, 0, 2))
-        pltpu.make_async_copy(result.at[b], out.at[b], sems.at[b]).start()
+                for c in range(across):
+                    w0, w1 = mix[c, 2 * block : 3 * block], mix[c, 3 * block :]
+                    if c == 0:
+                        w0 = jnp.where(my_col == 0, r0[...], w0)
+                        w1 = jnp.where(my_col == 0, lp, jnp.where(my_col == 1, r1[...], w1))
+                    tiles[c] = jnp.where(my_row == 0, w0, jnp.where(my_row == 1, w1, tiles[c]))
+            result[b] = jnp.transpose(jnp.stack(tiles), (1, 0, 2))
+            pltpu.make_async_copy(result.at[b], out.at[b], sems.at[b]).start()
     for b in range(down):
         pltpu.make_async_copy(result.at[b], out.at[b], sems.at[b]).wait()
 
@@ -259,24 +272,24 @@
         return jnp.where(member(my_row, pairs), got, part)
 
     first_piece, top = call(
-        first_kernel, [shape(block, width), shape(across, block, width)], [matrix], [ANY], [VMEM] * 2,
-        [pltpu.VMEM((block, across, width), BF), pltpu.SemaphoreType.DMA],
+        first_kernel, [shape(block, width), shape(across, block, width)], [matrix], [HBM], [VMEM] * 2,
+        [pltpu.VMEM((block, across, width), BF), pltpu.SemaphoreType.DMA], limit=4,
     )
     have0 = far(first_piece)
     for pairs in top_steps[:1]:
         top = pick(pairs, lax.ppermute(top, "prow", pairs), top)
 
-    flat, keep, give, middle, last, goes = call(
+    keep, give, middle, last, goes = call(
         functools.partial(pick_kernel, nr),
-        [shape(across, down, block, width), shape(across, block, width),
+        [shape(across, block, width),
          shape(across, block, width), shape(down - 2, block, width), shape(block, width),
          jax.ShapeDtypeStruct((1, 2 * block), jnp.int32)],
         [me, matrix, pivots, first_piece],
-        [SMEM, ANY, VMEM, ANY],
-        [ANY] + [VMEM] * 5,
+        [SMEM, HBM, VMEM, ANY],
+        [VMEM] * 5,
         [pltpu.VMEM(matrix.shape, BF), pltpu.VMEM((across, down, block, width), BF),
          pltpu.VMEM((2 * block, down * block), BF),
-         pltpu.SemaphoreType.DMA((down,)), pltpu.SemaphoreType.DMA((down,))],
+         pltpu.SemaphoreType.DMA((down,))],
     )
     have1, have2 = far(middle), far(last)
     other0 = near(after(have0, keep))
@@ -285,8 +298,13 @@
     part = call(
         join_kernel, shape(2 * across, block, width), [keep, swap(after(give, have0)), top], [VMEM] * 3, VMEM, flops=WEIGHT
     )
+    flat = call(
+        turn_kernel, shape(across, down, block, width), [matrix, other0], [HBM, ANY], HBM,
+        [pltpu.VMEM(matrix.shape, BF), pltpu.VMEM((across, down, block, width), BF),
+         pltpu.SemaphoreType.DMA((down,)), pltpu.SemaphoreType.DMA((down,))], flops=10**9, limit=16,
+    )
     for pairs in rim_steps[:-1]:
-        rim = pick(pairs, lax.ppermute(after(rim, have1), "prow", pairs), rim)
+        rim = pick(pairs, lax.ppermute(after(rim, have1, flat), "prow", pairs), rim)
     for level in range(depth - 1):
         pairs = exchange_pairs(nr, level)
         taken = member(my_row, top_steps[level + 1]).astype(jnp.int32)[None]
@@ -302,29 +320,30 @@
         tail = tail + got[: across - 1]
         rim = pick(rim_steps[-1], got[across - 1 :], rim)
 
-    side = after(head, have2)
+    other1 = near(have1)
+    side = after(head, have2, other1)
     for pairs in far_steps(nc):
         joint = [(i * nc + s, i * nc + t) for i in range(nr) for s, t in pairs if s % 2 != i % 2]
         got = lax.ppermute(side, joined, joint)
         right = member(my_col, pairs) & (my_col % 2 != my_row % 2)
         side = jnp.where(right, got, side)
     joint = [(i * nc + s, i * nc + (s ^ 1)) for i in range(nr) for s in range(nc) if s % 2 != i % 2]
-    other1 = near(have1)
     side = jnp.where(my_col % 2 == my_row % 2, lax.ppermute(side, joined, joint), side)
     other2 = near(have2)
 
     args = [me, goes, lower_inverse, upper_inverse]
-    parts = [flat, head, swap(head), tail, swap(tail), side, swap(side), top, swap(top), rim, swap(rim),
-             have0, have1, have2, other0, other1, other2]
+    ready = [flat, head, swap(head), tail, swap(tail), side, swap(side), top, swap(top), rim, swap(rim), have0, have1, have2, other0, other1, other2]
+    parts = []
     return call(
         functools.partial(finish_kernel, nr, nc, len(parts)),
         shape(*matrix.shape),
-        args + parts,
-        [SMEM] + [VMEM] * 3 + [ANY] * len(parts),
+        args + ready + parts,
+        [SMEM] + [VMEM] * (3 + len(ready)) + [ANY] * len(parts),
         ANY,
         [pltpu.VMEM(p.shape, BF) for p in parts] +
-        [pltpu.VMEM((across, 4 * block, width), BF)] + [pltpu.VMEM((block, width), BF)] * 4 +
-        [pltpu.VMEM(matrix.shape, BF), pltpu.SemaphoreType.DMA((len(parts),)), pltpu.SemaphoreType.DMA((down,))],
+        [pltpu.VMEM((across, 4 * block, width), BF)] + [pltpu.VMEM((block, width), BF)] * 2 +
+        [pltpu.VMEM(matrix.shape, BF), pltpu.SemaphoreType.DMA((max(len(parts), 1),)), pltpu.SemaphoreType.DMA((down,))],
+        limit=12,
     )
 
 

time: 73.3 us -> 70.5 us (0.962)
  waiting for transfers between devices: 11.9 us -> 8.2 us
  Pallas kernels: 14.5 us -> 16.3 us
  starting transfers between devices: 35 us -> 33.9 us
    ppermute x3, starting transfers between devices: 12.4 us -> 8.68 us  [far(): got = lax.ppermute(piece, 'pcol', pairs)]
    ppermute x3, starting transfers between devices: 8.28 us -> 11.8 us  [near(): return lax.ppermute(piece, 'pcol', twin(nc))]
    ppermute x3, waiting for transfers between devices: 5.48 us -> 2.49 us  [near(): return lax.ppermute(piece, 'pcol', twin(nc))]
    ppermute x1, waiting for transfers between devices: 3.23 us -> 1.21 us  [local(): rim = pick(pairs, lax.ppermute(after(rim, have1, flat), 'prow', pairs), rim)]
    ppermute x6, starting transfers between devices: 3.63 us -> 1.72 us  [swap(): return lax.ppermute(part, 'prow', twin(nr))]
    pallas_call x5 -> x6, Pallas kernels: 14.5 us -> 16.3 us  [call(): pl.pallas_call(body, out_shape=outs, in_specs=in_specs, out_specs=out_spe...]
    ppermute x1, waiting for transfers between devices: 1.47 us -> 2.91 us  [local(): lax.ppermute(side, joined, joint)]
    ppermute x1, starting transfers between devices: 0.35 us -> 1.49 us  [local(): lax.ppermute(part, 'prow', pairs)]
  transfers between devices with their start and end apart: 19 -> 19, of which waited for: 6 -> 5; matrix products, arithmetic and copies ran while one was open for 8% -> 8% of each run, Pallas kernels for 6% -> 12%
where the time goes in v3:
time: 70.5 us; the launch traced here: 70 us
  starting transfers between devices  33.9 us (48%)
  Pallas kernels  16.3 us (23%)
  waiting for transfers between devices  8.2 us (12%)
  other arithmetic  5.67 us (8%)
  local copies, waits for them, and re-layouts  5.55 us (8%)
    pallas_call x6, Pallas kernels, call(): pl.pallas_call(body, out_shape=outs, in_specs=in_specs, out_specs=out_spe...  16.3 us
    ppermute x3, starting transfers between devices, near(): return lax.ppermute(piece, 'pcol', twin(nc))  11.8 us
    ppermute x3, starting transfers between devices, far(): got = lax.ppermute(piece, 'pcol', pairs)  8.68 us
    unnamed x34, local copies, waits for them, and re-layouts  5.48 us
    ppermute x1, starting transfers between devices, local(): top = pick(pairs, lax.ppermute(top, 'prow', pairs), top)  4.23 us
    ppermute x1, waiting for transfers between devices, local(): lax.ppermute(side, joined, joint)  2.91 us
    ppermute x3, waiting for transfers between devices, near(): return lax.ppermute(piece, 'pcol', twin(nc))  2.49 us
    select_n x3, other arithmetic, far(): piece = jnp.where(member(my_col, pairs), got, piece)  2.32 us
  transfers between devices with their start and end apart: 19, of which 5 were waited for; matrix products, arithmetic and copies ran while one was open for 8% of the time, Pallas kernels for 12%

profile of v3, /device:TPU:0, one launch (start us, length us, event | category | flops | bytes accessed | tf_op | source)
XLA Modules:
  0.0 70.0 jit_solution(6849494597080809231)
XLA Ops:
  0.0 1.6 %copy-done = bf16[4,256,4,256]{3,2,1,0:T(4,128)(2,1)S(1)} copy-done((bf16[4,256,4,256]{3,2,1,0:T(4,128)(2,1)S(1)}, bf16[4,256,4,256]{3,2,1,0:T(4,128)(2,1)}, u32[]{:S(2)}) %copy-start) | copy-done | bytes 2097176
  1.6 0.2 shard_map.46
  1.8 6.1 %collective-permute-start = (bf16[256,256]{1,0:T(8,128)(2,1)S(1)}, bf16[256,256]{1,0:T(8,128)(2,1)S(1)}, u32[]{:S(2)}, u32[]{:S(2)}) collective-permute-start(bf16[256,256]{1,0:T(8,128)(2,1)S(1)} %get-tuple-element.16.first_piece), channel_id=1, source_target_pairs={{0,2},{1,3},{4,6},{5,7},{8,10},{9,11},{12,14},{13,15},{16,18},{17,... | collective-permute-start | bytes 393224 | tf_op jit(solution)/shard_map/ppermute | solution.py:261
  7.9 4.2 %collective-permute-start.3 = (bf16[4,256,256]{2,1,0:T(8,128)(2,1)S(1)}, bf16[4,256,256]{2,1,0:T(8,128)(2,1)}, u32[]{:S(2)}, u32[]{:S(2)}) collective-permute-start(bf16[4,256,256]{2,1,0:T(8,128)(2,1)S(1)} %get-tuple-element.22), channel_id=1, source_target_pairs={{0,16},{4,12},{1,17},{5,13},{2,18},{6,14},{3,19},{7,15}} | collective-permute-start | bytes 1572872 | tf_op jit(solution)/shard_map/ppermute | solution.py:280
  12.1 0.1 pad_add_fusion.me
  12.2 3.9 %shard_map.47 = (bf16[4,256,256]{2,1,0:T(8,128)(2,1)S(1)}, bf16[4,256,256]{2,1,0:T(8,128)(2,1)}, bf16[2,256,256]{2,1,0:T(8,128)(2,1)S(1)}, bf16[256,256]{1,0:T(8,128)(2,1)}, s32[1,512]{1,0:T(1,128)S(1)}) custom-call(s32[2]{0:T(128)S(1)} %pad_add_fusion.me, bf16[4,256,4,256]{3,2,1,0:T(4,128)(2,1)S(1)} %copy-done.1, s32[2,256]{1,0:T(2,128)S(1)} %copy-done.9, ...), custom_call_target="tpu_custom_call" | custom-call | flops 1000000 | tf_op jit(solution)/shard_map/pallas_call | solution.py:62
  16.1 0.8 %copy-done.12 = bf16[4,256,256]{2,1,0:T(8,128)(2,1)} copy-done((bf16[4,256,256]{2,1,0:T(8,128)(2,1)}, bf16[4,256,256]{2,1,0:T(8,128)(2,1)S(1)}, u32[]{:S(2)}) %copy-start.12) | copy-done | bytes 524312
  16.9 0.0 collective-permute-done
  16.9 0.1 collective-permute-start.2
  17.0 1.3 %collective-permute-start.7 = (bf16[2,256,256]{2,1,0:T(8,128)(2,1)S(1)}, bf16[2,256,256]{2,1,0:T(8,128)(2,1)S(1)}, u32[]{:S(2)}, u32[]{:S(2)}) collective-permute-start(bf16[2,256,256]{2,1,0:T(8,128)(2,1)S(1)} %get-tuple-element.23), channel_id=1, source_target_pairs={{0,2},{1,3},{4,6},{5,7},{8,10},{9,11},{12,14},{13,15},{16,18},{17,... | collective-permute-start | bytes 786440 | tf_op jit(solution)/shard_map/ppermute | solution.py:261
  18.3 2.1 %collective-permute-start.1 = (bf16[256,256]{1,0:T(8,128)(2,1)S(1)}, bf16[256,256]{1,0:T(8,128)(2,1)S(1)}, u32[]{:S(2)}, u32[]{:S(2)}) collective-permute-start(bf16[256,256]{1,0:T(8,128)(2,1)S(1)} %broadcast_select_fusion.6.refs_11_), channel_id=1, source_target_pairs={{0,1},{1,0},{2,3},{3,2},{4,5},{5,4},{6,7},{7,6},{8,9},{9,8},{10,11... | collective-permute-start | bytes 393224 | tf_op jit(solution)/shard_map/ppermute | solution.py:266
  20.4 0.0 collective-permute-done.3
  20.4 0.1 broadcast_select_fusion.top
  20.5 0.0 collective-permute-done.2.got
  20.5 1.0 %copy-done.13 = bf16[4,256,256]{2,1,0:T(8,128)(2,1)S(1)} copy-done((bf16[4,256,256]{2,1,0:T(8,128)(2,1)S(1)}, bf16[4,256,256]{2,1,0:T(8,128)(2,1)}, u32[]{:S(2)}) %copy-start.13) | copy-done | bytes 524312
  21.5 2.1 %shard_map.49.part = bf16[8,256,256]{2,1,0:T(8,128)(2,1)} custom-call(bf16[4,256,256]{2,1,0:T(8,128)(2,1)S(1)} %copy-done.13, bf16[4,256,256]{2,1,0:T(8,128)(2,1)} %collective-permute-done.2.got, bf16[4,256,256]{2,1,0:T(8,128)(2,1)S(1)} %broadcast_select_fusion.top), custom_call_target="tpu_custom_call" | custom-call | flops 99999997952 | tf_op jit(solution)/shard_map/pallas_call | solution.py:62
  23.6 1.5 %collective-permute-start.4 = (bf16[8,256,256]{2,1,0:T(8,128)(2,1)}, bf16[8,256,256]{2,1,0:T(8,128)(2,1)}, u32[]{:S(2)}, u32[]{:S(2)}) collective-permute-start(bf16[8,256,256]{2,1,0:T(8,128)(2,1)} %shard_map.49.part), channel_id=1, source_target_pairs={{0,8},{4,20},{8,0},{12,28},{16,24},{20,4},{24,16},{28,12},{1,9},{5... | collective-permute-start | bytes 3145736 | tf_op jit(solution)/shard_map/ppermute | solution.py:312
  25.1 2.5 %collective-permute-done.1.gate.refs_14_ = bf16[256,256]{1,0:T(8,128)(2,1)S(1)} collective-permute-done((bf16[256,256]{1,0:T(8,128)(2,1)S(1)}, bf16[256,256]{1,0:T(8,128)(2,1)S(1)}, u32[]{:S(2)}, u32[]{:S(2)}) %collective-permute-start.1) | collective-permute-done | bytes 131104 | tf_op jit(solution)/shard_map/ppermute | solution.py:266
  27.7 1.0 %shard_map.48.refs_0_ = bf16[4,4,256,256]{3,2,1,0:T(8,128)(2,1)S(1)} custom-call(bf16[4,256,4,256]{3,2,1,0:T(4,128)(2,1)S(1)} %copy-done.1, bf16[256,256]{1,0:T(8,128)(2,1)S(1)} %collective-permute-done.1.gate.refs_14_), custom_call_target="tpu_custom_call" | custom-call | flops 1000000000 | tf_op jit(solution)/shard_map/pallas_call | solution.py:62
  28.6 0.0 copy-start.2
  28.6 1.3 %copy-done.2 = bf16[4,4,256,256]{3,2,1,0:T(8,128)(2,1)} copy-done((bf16[4,4,256,256]{3,2,1,0:T(8,128)(2,1)}, bf16[4,4,256,256]{3,2,1,0:T(8,128)(2,1)S(1)}, u32[]{:S(2)}) %copy-start.2) | copy-done | bytes 2097176
  30.0 0.7 %broadcast_select_fusion.1.refs_12_ = bf16[2,256,256]{2,1,0:T(8,128)(2,1)} fusion(bf16[2,256,256]{2,1,0:T(8,128)(2,1)S(1)} %collective-permute-done.7, bf16[2,256,256]{2,1,0:T(8,128)(2,1)S(1)} %get-tuple-element.23, pred[]{:T(512)S(6)} %gt.18), kind=kLoop, calls=%fused_computation.5 | loop fusion | flops 131072 | bytes 786433 | tf_op jit(solution)/shard_map/jit(_where)/select_n | solution.py:262
  30.7 1.3 %collective-permute-start.8 = (bf16[2,256,256]{2,1,0:T(8,128)(2,1)S(1)}, bf16[2,256,256]{2,1,0:T(8,128)(2,1)S(1)}, u32[]{:S(2)}, u32[]{:S(2)}) collective-permute-start(bf16[2,256,256]{2,1,0:T(8,128)(2,1)S(1)} %pad_maximum_fusion.1), channel_id=1, source_target_pairs={{0,8},{4,20},{1,9},{5,21},{2,10},{6,22},{3,11},{7,23}} | collective-permute-start | bytes 786440 | tf_op jit(solution)/shard_map/ppermute | solution.py:307
  32.0 1.3 %collective-permute-start.11 = (bf16[256,256]{1,0:T(8,128)(2,1)}, bf16[256,256]{1,0:T(8,128)(2,1)S(1)}, u32[]{:S(2)}, u32[]{:S(2)}) collective-permute-start(bf16[256,256]{1,0:T(8,128)(2,1)} %get-tuple-element.25), channel_id=1, source_target_pairs={{0,2},{1,3},{4,6},{5,7},{8,10},{9,11},{12,14},{13,15},{16,18},{17,... | collective-permute-start | bytes 393224 | tf_op jit(solution)/shard_map/ppermute | solution.py:261
  33.3 5.9 %collective-permute-start.12 = (bf16[2,256,256]{2,1,0:T(8,128)(2,1)}, bf16[2,256,256]{2,1,0:T(8,128)(2,1)S(1)}, u32[]{:S(2)}, u32[]{:S(2)}) collective-permute-start(bf16[2,256,256]{2,1,0:T(8,128)(2,1)} %broadcast_select_fusion.1.refs_12_), channel_id=1, source_target_pairs={{0,1},{1,0},{2,3},{3,2},{4,5},{5,4},{6,7},{7,6},{8,9},{9,8},{10,11... | collective-permute-start | bytes 786440 | tf_op jit(solution)/shard_map/ppermute | solution.py:266
  39.3 1.2 %collective-permute-done.8 = bf16[2,256,256]{2,1,0:T(8,128)(2,1)S(1)} collective-permute-done((bf16[2,256,256]{2,1,0:T(8,128)(2,1)S(1)}, bf16[2,256,256]{2,1,0:T(8,128)(2,1)S(1)}, u32[]{:S(2)}, u32[]{:S(2)}) %collective-permute-start.8) | collective-permute-done | bytes 262176 | tf_op jit(solution)/shard_map/ppermute | solution.py:307
  40.5 1.7 %shard_map.50 = bf16[8,256,256]{2,1,0:T(8,128)(2,1)S(1)} custom-call(s32[1]{0:T(128)} %bitcast.2.taken, bf16[8,256,256]{2,1,0:T(8,128)(2,1)} %shard_map.49.part, bf16[8,256,256]{2,1,0:T(8,128)(2,1)} %collective-permute-done.4.got), custom_call_target="tpu_custom_call" | custom-call | flops 99999997952 | tf_op jit(solution)/shard_map/pallas_call | solution.py:62
  42.3 0.8 %collective-permute-start.5 = (bf16[256,256]{1,0:T(8,128)(2,1)S(1)}, bf16[256,256]{1,0:T(8,128)(2,1)S(1)}, u32[]{:S(2)}, u32[]{:S(2)}) collective-permute-start(bf16[256,256]{1,0:T(8,128)(2,1)S(1)} %slice_bitcast_fusion), channel_id=1, source_target_pairs={{0,16},{4,12},{8,24},{12,4},{16,0},{20,28},{24,8},{28,20},{1,17},{... | collective-permute-start | bytes 393224 | tf_op jit(solution)/shard_map/ppermute | solution.py:318
  43.1 0.9 %pad_maximum_fusion = bf16[5,256,256]{2,1,0:T(8,128)(2,1)} fusion(bf16[2,256,256]{2,1,0:T(8,128)(2,1)S(1)} %broadcast_select_fusion.2, bf16[3,256,256]{2,1,0:T(8,128)(2,1)S(1)} %slice.21), kind=kLoop, calls=%fused_computation | loop fusion | flops 327680 | bytes 1310720 | tf_op jit(solution)/shard_map/concatenate | solution.py:319
  44.0 1.3 %collective-permute-start.9 = (bf16[5,256,256]{2,1,0:T(8,128)(2,1)}, bf16[5,256,256]{2,1,0:T(8,128)(2,1)}, u32[]{:S(2)}, u32[]{:S(2)}) collective-permute-start(bf16[5,256,256]{2,1,0:T(8,128)(2,1)} %pad_maximum_fusion), channel_id=1, source_target_pairs={{0,16},{4,12},{8,24},{12,4},{16,0},{20,28},{24,8},{28,20},{1,17},{... | collective-permute-start | bytes 1966088 | tf_op jit(solution)/shard_map/ppermute | solution.py:319
  45.3 0.0 collective-permute-done.11
  45.3 1.6 %broadcast_select_fusion.5.refs_13_ = bf16[256,256]{1,0:T(8,128)(2,1)} fusion(bf16[256,256]{1,0:T(8,128)(2,1)S(1)} %collective-permute-done.11, bf16[256,256]{1,0:T(8,128)(2,1)} %get-tuple-element.25, pred[]{:T(512)S(6)} %gt.18), kind=kLoop, calls=%fused_computation.12 | loop fusion | flops 65536 | bytes 393217 | tf_op jit(solution)/shard_map/jit(_where)/select_n | solution.py:262
  46.9 0.5 collective-permute-done.5
  47.3 0.0 copy-start.3
  47.4 0.7 copy-done.7
  48.1 1.3 %collective-permute-start.13 = (bf16[256,256]{1,0:T(8,128)(2,1)S(1)}, bf16[256,256]{1,0:T(8,128)(2,1)}, u32[]{:S(2)}, u32[]{:S(2)}) collective-permute-start(bf16[256,256]{1,0:T(8,128)(2,1)S(1)} %fusion.refs_1_), channel_id=1, source_target_pairs={{1,3},{4,6},{9,11},{12,14},{17,19},{20,22},{25,27},{28,30}} | collective-permute-start | bytes 393224 | tf_op jit(solution)/shard_map/ppermute | solution.py:327
  49.4 3.9 %collective-permute-start.18 = (bf16[256,256]{1,0:T(8,128)(2,1)}, bf16[256,256]{1,0:T(8,128)(2,1)S(1)}, u32[]{:S(2)}, u32[]{:S(2)}) collective-permute-start(bf16[256,256]{1,0:T(8,128)(2,1)} %broadcast_select_fusion.5.refs_13_), channel_id=1, source_target_pairs={{0,1},{1,0},{2,3},{3,2},{4,5},{5,4},{6,7},{7,6},{8,9},{9,8},{10,11... | collective-permute-start | bytes 393224 | tf_op jit(solution)/shard_map/ppermute | solution.py:266
  53.3 0.1 collective-permute-start.16
  53.4 0.5 collective-permute-start.6
  53.9 0.0 collective-permute-done.13
  53.9 1.3 %collective-permute-start.14 = (bf16[256,256]{1,0:T(8,128)(2,1)S(1)}, bf16[256,256]{1,0:T(8,128)(2,1)S(1)}, u32[]{:S(2)}, u32[]{:S(2)}) collective-permute-start(bf16[256,256]{1,0:T(8,128)(2,1)S(1)} %broadcast_select_fusion.3), channel_id=1, source_target_pairs={{1,0},{3,2},{4,5},{6,7},{9,8},{11,10},{12,13},{14,15},{17,16},{19,... | collective-permute-start | bytes 393224 | tf_op jit(solution)/shard_map/ppermute | solution.py:331
  55.2 1.0 %slice_add_fusion.refs_3_ = bf16[3,256,256]{2,1,0:T(8,128)(2,1)S(1)} fusion(bf16[5,256,256]{2,1,0:T(8,128)(2,1)} %collective-permute-done.9, bf16[8,256,256]{2,1,0:T(8,128)(2,1)S(1)} %shard_map.50), kind=kLoop, calls=%fused_computation.2 | loop fusion | flops 196608 | bytes 1179648 | tf_op jit(solution)/shard_map/add | solution.py:320
  56.3 0.5 collective-permute-start.10
  56.8 1.1 %slice_select_fusion.refs_9_ = bf16[2,256,256]{2,1,0:T(8,128)(2,1)S(1)} fusion(bf16[5,256,256]{2,1,0:T(8,128)(2,1)} %collective-permute-done.9, pred[]{:T(512)S(6)} %gt.22, bf16[2,256,256]{2,1,0:T(8,128)(2,1)} %copy-done.16, bf16[1,256,256]{2,1,0:T(8,128)(2,1)} %copy-done.15, bf16[1,256,256]{2,1,0:T(8,128)(2,1)} %copy-done.14, pred[]{:T(512)S(6)} %gt.21), kind=kLoop, calls=%fused_computation.3 | loop fusion | flops 393216 | bytes 1048578 | tf_op jit(solution)/shard_map/jit(_where)/select_n | solution.py:272
  57.9 2.9 %collective-permute-done.14 = bf16[256,256]{1,0:T(8,128)(2,1)S(1)} collective-permute-done((bf16[256,256]{1,0:T(8,128)(2,1)S(1)}, bf16[256,256]{1,0:T(8,128)(2,1)S(1)}, u32[]{:S(2)}, u32[]{:S(2)}) %collective-permute-start.14) | collective-permute-done | bytes 131104 | tf_op jit(solution)/shard_map/ppermute | solution.py:331
  60.8 0.6 collective-permute-start.15
  61.4 1.1 %collective-permute-done.15.refs_6_ = bf16[256,256]{1,0:T(8,128)(2,1)S(1)} collective-permute-done((bf16[256,256]{1,0:T(8,128)(2,1)S(1)}, bf16[256,256]{1,0:T(8,128)(2,1)S(1)}, u32[]{:S(2)}, u32[]{:S(2)}) %collective-permute-start.15) | collective-permute-done | bytes 131104 | tf_op jit(solution)/shard_map/ppermute | solution.py:269
  62.6 7.5 %shard_map.51 = bf16[4,256,4,256]{3,2,1,0:T(4,128)(2,1)} custom-call(s32[2]{0:T(128)S(1)} %copy-done.11, s32[1,512]{1,0:T(1,128)S(1)} %get-tuple-element.17.goes, bf16[2,256,256]{2,1,0:T(8,128)(2,1)S(1)} %copy-done.5, bf16[2,256,256]{2,1,0:T(8,128)(2,1)S(1)} %copy-done.6, bf16[4,4,256,256]{3,2,1,0:T(8,128)(2,1)S(1)} %copy-done.3, ...), custom_call_target="tpu_custom_call" | custom-call | flops 1000000 | tf_op jit(solution)/shard_map/pallas_call | solution.py:62
  (47 shorter events, 0.3 us)
Async XLA Ops:
  0.0 1.6 %copy-start = (bf16[4,256,4,256]{3,2,1,0:T(4,128)(2,1)S(1)}, bf16[4,256,4,256]{3,2,1,0:T(4,128)(2,1)}, u32[]{:S(2)}) copy-start(bf16[4,256,4,256]{3,2,1,0:T(4,128)(2,1)} %a.5) | copy-start | bytes 6291460
  1.6 10.6 %copy-start.1 = (bf16[4,256,4,256]{3,2,1,0:T(4,128)(2,1)S(1)}, bf16[4,256,4,256]{3,2,1,0:T(4,128)(2,1)}, u32[]{:S(2)}) copy-start(bf16[4,256,4,256]{3,2,1,0:T(4,128)(2,1)} %a.5) | copy-start | bytes 6291460
  1.6 10.6 %copy-start.9 = (s32[2,256]{1,0:T(2,128)S(1)}, s32[2,256]{1,0:T(2,128)}, u32[]{:S(2)}) copy-start(s32[2,256]{1,0:T(2,128)} %row.1) | copy-start | bytes 6148
  1.8 15.1 %collective-permute-start = (bf16[256,256]{1,0:T(8,128)(2,1)S(1)}, bf16[256,256]{1,0:T(8,128)(2,1)S(1)}, u32[]{:S(2)}, u32[]{:S(2)}) collective-permute-start(bf16[256,256]{1,0:T(8,128)(2,1)S(1)} %get-tuple-element.16.first_piece), channel_id=1, source_target_pairs={{0,2},{1,3},{4,6},{5,7},{8,10},{9,11},{12,14},{13,15},{16,18},{17,... | collective-permute-start | bytes 393224 | tf_op jit(solution)/shard_map/ppermute | solution.py:261
  7.9 12.5 %collective-permute-start.3 = (bf16[4,256,256]{2,1,0:T(8,128)(2,1)S(1)}, bf16[4,256,256]{2,1,0:T(8,128)(2,1)}, u32[]{:S(2)}, u32[]{:S(2)}) collective-permute-start(bf16[4,256,256]{2,1,0:T(8,128)(2,1)S(1)} %get-tuple-element.22), channel_id=1, source_target_pairs={{0,16},{4,12},{1,17},{5,13},{2,18},{6,14},{3,19},{7,15}} | collective-permute-start | bytes 1572872 | tf_op jit(solution)/shard_map/ppermute | solution.py:280
  12.2 3.9 %copy-start.10 = (s32[2]{0:T(128)}, s32[2]{0:T(128)S(1)}, u32[]{:S(2)}) copy-start(s32[2]{0:T(128)S(1)} %pad_add_fusion.me) | copy-start | bytes 28
  16.1 0.8 %copy-start.12 = (bf16[4,256,256]{2,1,0:T(8,128)(2,1)}, bf16[4,256,256]{2,1,0:T(8,128)(2,1)S(1)}, u32[]{:S(2)}) copy-start(bf16[4,256,256]{2,1,0:T(8,128)(2,1)S(1)} %get-tuple-element.18.keep) | copy-start | bytes 1572868
  16.9 3.6 %collective-permute-start.2 = (bf16[4,256,256]{2,1,0:T(8,128)(2,1)}, bf16[4,256,256]{2,1,0:T(8,128)(2,1)}, u32[]{:S(2)}, u32[]{:S(2)}) collective-permute-start(bf16[4,256,256]{2,1,0:T(8,128)(2,1)} %get-tuple-element.21), channel_id=1, source_target_pairs={{0,4},{4,0},{8,12},{12,8},{16,20},{20,16},{24,28},{28,24},{1,5},{5... | collective-permute-start | bytes 1572872 | tf_op jit(solution)/shard_map/ppermute | solution.py:269
  17.0 13.0 %collective-permute-start.7 = (bf16[2,256,256]{2,1,0:T(8,128)(2,1)S(1)}, bf16[2,256,256]{2,1,0:T(8,128)(2,1)S(1)}, u32[]{:S(2)}, u32[]{:S(2)}) collective-permute-start(bf16[2,256,256]{2,1,0:T(8,128)(2,1)S(1)} %get-tuple-element.23), channel_id=1, source_target_pairs={{0,2},{1,3},{4,6},{5,7},{8,10},{9,11},{12,14},{13,15},{16,18},{17,... | collective-permute-start | bytes 786440 | tf_op jit(solution)/shard_map/ppermute | solution.py:261
  18.3 9.3 %collective-permute-start.1 = (bf16[256,256]{1,0:T(8,128)(2,1)S(1)}, bf16[256,256]{1,0:T(8,128)(2,1)S(1)}, u32[]{:S(2)}, u32[]{:S(2)}) collective-permute-start(bf16[256,256]{1,0:T(8,128)(2,1)S(1)} %broadcast_select_fusion.6.refs_11_), channel_id=1, source_target_pairs={{0,1},{1,0},{2,3},{3,2},{4,5},{5,4},{6,7},{7,6},{8,9},{9,8},{10,11... | collective-permute-start | bytes 393224 | tf_op jit(solution)/shard_map/ppermute | solution.py:266
  20.5 1.0 %copy-start.13 = (bf16[4,256,256]{2,1,0:T(8,128)(2,1)S(1)}, bf16[4,256,256]{2,1,0:T(8,128)(2,1)}, u32[]{:S(2)}) copy-start(bf16[4,256,256]{2,1,0:T(8,128)(2,1)} %copy-done.12) | copy-start | bytes 1572868
  23.6 16.9 %collective-permute-start.4 = (bf16[8,256,256]{2,1,0:T(8,128)(2,1)}, bf16[8,256,256]{2,1,0:T(8,128)(2,1)}, u32[]{:S(2)}, u32[]{:S(2)}) collective-permute-start(bf16[8,256,256]{2,1,0:T(8,128)(2,1)} %shard_map.49.part), channel_id=1, source_target_pairs={{0,8},{4,20},{8,0},{12,28},{16,24},{20,4},{24,16},{28,12},{1,9},{5... | collective-permute-start | bytes 3145736 | tf_op jit(solution)/shard_map/ppermute | solution.py:312
  27.6 12.8 %copy-start.14 = (bf16[1,256,256]{2,1,0:T(8,128)(2,1)}, bf16[1,256,256]{2,1,0:T(8,128)(2,1)S(1)}, u32[]{:S(2)}) copy-start(bf16[1,256,256]{2,1,0:T(8,128)(2,1)S(1)} %get-tuple-element.27) | copy-start | bytes 393220
  27.7 12.8 %copy-start.15 = (bf16[1,256,256]{2,1,0:T(8,128)(2,1)}, bf16[1,256,256]{2,1,0:T(8,128)(2,1)S(1)}, u32[]{:S(2)}) copy-start(bf16[1,256,256]{2,1,0:T(8,128)(2,1)S(1)} %get-tuple-element.28) | copy-start | bytes 393220
  28.6 1.3 %copy-start.2 = (bf16[4,4,256,256]{3,2,1,0:T(8,128)(2,1)}, bf16[4,4,256,256]{3,2,1,0:T(8,128)(2,1)S(1)}, u32[]{:S(2)}) copy-start(bf16[4,4,256,256]{3,2,1,0:T(8,128)(2,1)S(1)} %shard_map.48.refs_0_) | copy-start | bytes 6291460
  30.7 9.7 %collective-permute-start.8 = (bf16[2,256,256]{2,1,0:T(8,128)(2,1)S(1)}, bf16[2,256,256]{2,1,0:T(8,128)(2,1)S(1)}, u32[]{:S(2)}, u32[]{:S(2)}) collective-permute-start(bf16[2,256,256]{2,1,0:T(8,128)(2,1)S(1)} %pad_maximum_fusion.1), channel_id=1, source_target_pairs={{0,8},{4,20},{1,9},{5,21},{2,10},{6,22},{3,11},{7,23}} | collective-permute-start | bytes 786440 | tf_op jit(solution)/shard_map/ppermute | solution.py:307
  32.0 13.3 %collective-permute-start.11 = (bf16[256,256]{1,0:T(8,128)(2,1)}, bf16[256,256]{1,0:T(8,128)(2,1)S(1)}, u32[]{:S(2)}, u32[]{:S(2)}) collective-permute-start(bf16[256,256]{1,0:T(8,128)(2,1)} %get-tuple-element.25), channel_id=1, source_target_pairs={{0,2},{1,3},{4,6},{5,7},{8,10},{9,11},{12,14},{13,15},{16,18},{17,... | collective-permute-start | bytes 393224 | tf_op jit(solution)/shard_map/ppermute | solution.py:261
  33.3 14.0 %collective-permute-start.12 = (bf16[2,256,256]{2,1,0:T(8,128)(2,1)}, bf16[2,256,256]{2,1,0:T(8,128)(2,1)S(1)}, u32[]{:S(2)}, u32[]{:S(2)}) collective-permute-start(bf16[2,256,256]{2,1,0:T(8,128)(2,1)} %broadcast_select_fusion.1.refs_12_), channel_id=1, source_target_pairs={{0,1},{1,0},{2,3},{3,2},{4,5},{5,4},{6,7},{7,6},{8,9},{9,8},{10,11... | collective-permute-start | bytes 786440 | tf_op jit(solution)/shard_map/ppermute | solution.py:266
  40.5 1.8 %copy-start.16 = (bf16[2,256,256]{2,1,0:T(8,128)(2,1)}, bf16[2,256,256]{2,1,0:T(8,128)(2,1)S(1)}, u32[]{:S(2)}) copy-start(bf16[2,256,256]{2,1,0:T(8,128)(2,1)S(1)} %collective-permute-done.8) | copy-start | bytes 786436
  42.3 5.0 %collective-permute-start.5 = (bf16[256,256]{1,0:T(8,128)(2,1)S(1)}, bf16[256,256]{1,0:T(8,128)(2,1)S(1)}, u32[]{:S(2)}, u32[]{:S(2)}) collective-permute-start(bf16[256,256]{1,0:T(8,128)(2,1)S(1)} %slice_bitcast_fusion), channel_id=1, source_target_pairs={{0,16},{4,12},{8,24},{12,4},{16,0},{20,28},{24,8},{28,20},{1,17},{... | collective-permute-start | bytes 393224 | tf_op jit(solution)/shard_map/ppermute | solution.py:318
  44.0 11.2 %collective-permute-start.9 = (bf16[5,256,256]{2,1,0:T(8,128)(2,1)}, bf16[5,256,256]{2,1,0:T(8,128)(2,1)}, u32[]{:S(2)}, u32[]{:S(2)}) collective-permute-start(bf16[5,256,256]{2,1,0:T(8,128)(2,1)} %pad_maximum_fusion), channel_id=1, source_target_pairs={{0,16},{4,12},{8,24},{12,4},{16,0},{20,28},{24,8},{28,20},{1,17},{... | collective-permute-start | bytes 1966088 | tf_op jit(solution)/shard_map/ppermute | solution.py:319
  47.3 15.2 %copy-start.3 = (bf16[4,4,256,256]{3,2,1,0:T(8,128)(2,1)S(1)}, bf16[4,4,256,256]{3,2,1,0:T(8,128)(2,1)}, u32[]{:S(2)}) copy-start(bf16[4,4,256,256]{3,2,1,0:T(8,128)(2,1)} %copy-done.2) | copy-start | bytes 6291460
  47.4 15.2 %copy-start.11 = (s32[2]{0:T(128)S(1)}, s32[2]{0:T(128)}, u32[]{:S(2)}) copy-start(s32[2]{0:T(128)} %copy-done.10) | copy-start | bytes 28
  47.4 0.7 %copy-start.7 = (bf16[2,256,256]{2,1,0:T(8,128)(2,1)}, bf16[2,256,256]{2,1,0:T(8,128)(2,1)S(1)}, u32[]{:S(2)}) copy-start(bf16[2,256,256]{2,1,0:T(8,128)(2,1)S(1)} %collective-permute-done.12.refs_15_) | copy-start | bytes 786436
  48.1 5.8 %collective-permute-start.13 = (bf16[256,256]{1,0:T(8,128)(2,1)S(1)}, bf16[256,256]{1,0:T(8,128)(2,1)}, u32[]{:S(2)}, u32[]{:S(2)}) collective-permute-start(bf16[256,256]{1,0:T(8,128)(2,1)S(1)} %fusion.refs_1_), channel_id=1, source_target_pairs={{1,3},{4,6},{9,11},{12,14},{17,19},{20,22},{25,27},{28,30}} | collective-permute-start | bytes 393224 | tf_op jit(solution)/shard_map/ppermute | solution.py:327
  49.4 13.1 %copy-start.4 = (bf16[256,256]{1,0:T(8,128)(2,1)S(1)}, bf16[256,256]{1,0:T(8,128)(2,1)}, u32[]{:S(2)}) copy-start(bf16[256,256]{1,0:T(8,128)(2,1)} %broadcast_select_fusion.5.refs_13_) | copy-start | bytes 393220
  49.4 13.1 %copy-start.5 = (bf16[2,256,256]{2,1,0:T(8,128)(2,1)S(1)}, bf16[2,256,256]{2,1,0:T(8,128)(2,1)}, u32[]{:S(2)}) copy-start(bf16[2,256,256]{2,1,0:T(8,128)(2,1)} %lower.1) | copy-start | bytes 786436
  49.4 13.2 %copy-start.6 = (bf16[2,256,256]{2,1,0:T(8,128)(2,1)S(1)}, bf16[2,256,256]{2,1,0:T(8,128)(2,1)}, u32[]{:S(2)}) copy-start(bf16[2,256,256]{2,1,0:T(8,128)(2,1)} %upper.1) | copy-start | bytes 786436
  49.4 13.2 %copy-start.8 = (bf16[2,256,256]{2,1,0:T(8,128)(2,1)S(1)}, bf16[2,256,256]{2,1,0:T(8,128)(2,1)}, u32[]{:S(2)}) copy-start(bf16[2,256,256]{2,1,0:T(8,128)(2,1)} %copy-done.7) | copy-start | bytes 786436
  49.4 11.4 %collective-permute-start.18 = (bf16[256,256]{1,0:T(8,128)(2,1)}, bf16[256,256]{1,0:T(8,128)(2,1)S(1)}, u32[]{:S(2)}, u32[]{:S(2)}) collective-permute-start(bf16[256,256]{1,0:T(8,128)(2,1)} %broadcast_select_fusion.5.refs_13_), channel_id=1, source_target_pairs={{0,1},{1,0},{2,3},{3,2},{4,5},{5,4},{6,7},{7,6},{8,9},{9,8},{10,11... | collective-permute-start | bytes 393224 | tf_op jit(solution)/shard_map/ppermute | solution.py:266
  53.3 8.1 %collective-permute-start.16 = (bf16[4,256,256]{2,1,0:T(8,128)(2,1)S(1)}, bf16[4,256,256]{2,1,0:T(8,128)(2,1)S(1)}, u32[]{:S(2)}, u32[]{:S(2)}) collective-permute-start(bf16[4,256,256]{2,1,0:T(8,128)(2,1)S(1)} %slice.23.refs_7_), channel_id=1, source_target_pairs={{0,4},{4,0},{8,12},{12,8},{16,20},{20,16},{24,28},{28,24},{1,5},{5... | collective-permute-start | bytes 1572872 | tf_op jit(solution)/shard_map/ppermute | solution.py:269
  53.4 8.0 %collective-permute-start.6 = (bf16[256,256]{1,0:T(8,128)(2,1)S(1)}, bf16[256,256]{1,0:T(8,128)(2,1)S(1)}, u32[]{:S(2)}, u32[]{:S(2)}) collective-permute-start(bf16[256,256]{1,0:T(8,128)(2,1)S(1)} %fusion.refs_1_), channel_id=1, source_target_pairs={{0,4},{4,0},{8,12},{12,8},{16,20},{20,16},{24,28},{28,24},{1,5},{5... | collective-permute-start | bytes 393224 | tf_op jit(solution)/shard_map/ppermute | solution.py:269
  53.9 6.9 %collective-permute-start.14 = (bf16[256,256]{1,0:T(8,128)(2,1)S(1)}, bf16[256,256]{1,0:T(8,128)(2,1)S(1)}, u32[]{:S(2)}, u32[]{:S(2)}) collective-permute-start(bf16[256,256]{1,0:T(8,128)(2,1)S(1)} %broadcast_select_fusion.3), channel_id=1, source_target_pairs={{1,0},{3,2},{4,5},{6,7},{9,8},{11,10},{12,13},{14,15},{17,16},{19,... | collective-permute-start | bytes 393224 | tf_op jit(solution)/shard_map/ppermute | solution.py:331
  56.3 6.2 %collective-permute-start.10 = (bf16[3,256,256]{2,1,0:T(8,128)(2,1)S(1)}, bf16[3,256,256]{2,1,0:T(8,128)(2,1)S(1)}, u32[]{:S(2)}, u32[]{:S(2)}) collective-permute-start(bf16[3,256,256]{2,1,0:T(8,128)(2,1)S(1)} %slice_add_fusion.refs_3_), channel_id=1, source_target_pairs={{0,4},{4,0},{8,12},{12,8},{16,20},{20,16},{24,28},{28,24},{1,5},{5... | collective-permute-start | bytes 1179656 | tf_op jit(solution)/shard_map/ppermute | solution.py:269
  60.8 1.7 %collective-permute-start.17 = (bf16[2,256,256]{2,1,0:T(8,128)(2,1)S(1)}, bf16[2,256,256]{2,1,0:T(8,128)(2,1)S(1)}, u32[]{:S(2)}, u32[]{:S(2)}) collective-permute-start(bf16[2,256,256]{2,1,0:T(8,128)(2,1)S(1)} %slice_select_fusion.refs_9_), channel_id=1, source_target_pairs={{0,4},{4,0},{8,12},{12,8},{16,20},{20,16},{24,28},{28,24},{1,5},{5... | collective-permute-start | bytes 786440 | tf_op jit(solution)/shard_map/ppermute | solution.py:269
  60.8 1.7 %collective-permute-start.15 = (bf16[256,256]{1,0:T(8,128)(2,1)S(1)}, bf16[256,256]{1,0:T(8,128)(2,1)S(1)}, u32[]{:S(2)}, u32[]{:S(2)}) collective-permute-start(bf16[256,256]{1,0:T(8,128)(2,1)S(1)} %broadcast_select_fusion.4.refs_5_), channel_id=1, source_target_pairs={{0,4},{4,0},{8,12},{12,8},{16,20},{20,16},{24,28},{28,24},{1,5},{5... | collective-permute-start | bytes 393224 | tf_op jit(solution)/shard_map/ppermute | solution.py:269

commit v4 on v3

--- a/solution.py
+++ b/solution.py
@@ -181,26 +181,23 @@
     side01, side10 = both(side_mine[...], side_other[...])
     u0p = dot(lower[0], side01).astype(BF)
     lp = dot(side10, upper[0]).astype(BF)
+    heads = [both(head_mine[...], head_other[...])]
+    heads += [both(tail_mine[c], tail_other[c]) for c in range(across - 1)]
+    firsts = [dot(lower[0], a0).astype(BF) for a0, _ in heads]
+    seconds = [(a1.astype(F32) - dot(lp, u)).astype(BF) for (_, a1), u in zip(heads, firsts)]
+    r0[...] = heads[0][0]
+    r1[...] = seconds[0]
     for c in range(across):
-        if c == 0:
-            a0, a1 = both(head_mine[...], head_other[...])
-        else:
-            a0, a1 = both(tail_mine[c - 1], tail_other[c - 1])
-        u = dot(lower[0], a0).astype(BF)
-        a1 = (a1.astype(F32) - dot(lp, u)).astype(BF)
-        if c == 0:
-            r0[...] = a0
-            r1[...] = a1
         t0, t1 = both(top_mine[c], top_other[c])
         mix[c, :block] = t0
         mix[c, block : 2 * block] = t1
-        mix[c, 2 * block : 3 * block] = u
-        mix[c, 3 * block :] = dot(lower[1], a1).astype(BF)
+        mix[c, 2 * block : 3 * block] = firsts[c]
+        mix[c, 3 * block :] = dot(lower[1], seconds[c]).astype(BF)
     rim = [jnp.concatenate(both(rim_mine[k], rim_other[k]), 0) for k in range(2)]
     for copy in copies:
         copy.wait()
     place = lax.broadcasted_iota(jnp.int32, (block, 2 * block), 0)
-    half = max(down // 2, 1)
+    half = down
     for h in range(0, down, half):
         match = jnp.concatenate([goes[...] - (b * nr + my_row) * block == place for b in range(h, h + half)], 0)
         onehot = match.astype(BF)
@@ -327,9 +324,10 @@
         got = lax.ppermute(side, joined, joint)
         right = member(my_col, pairs) & (my_col % 2 != my_row % 2)
         side = jnp.where(right, got, side)
+    far_side = side
     joint = [(i * nc + s, i * nc + (s ^ 1)) for i in range(nr) for s in range(nc) if s % 2 != i % 2]
     side = jnp.where(my_col % 2 == my_row % 2, lax.ppermute(side, joined, joint), side)
-    other2 = near(have2)
+    other2 = near(after(have2, far_side))
 
     args = [me, goes, lower_inverse, upper_inverse]
     ready = [flat, head, swap(head), tail, swap(tail), side, swap(side), top, swap(top), rim, swap(rim), have0, have1, have2, other0, other1, other2]

time: 70.5 us -> 69.4 us (0.984)
  waiting for transfers between devices: 8.2 us -> 7.01 us
  starting transfers between devices: 33.9 us -> 34.8 us
  Pallas kernels: 16.3 us -> 15.5 us
    ppermute x1, waiting for transfers between devices: 2.91 us -> 1.55 us  [local(): lax.ppermute(side, joined, joint)]
    ppermute x3, waiting for transfers between devices: 2.49 us -> 3.76 us  [near(): return lax.ppermute(piece, 'pcol', twin(nc))]
    ppermute x3, starting transfers between devices: 11.8 us -> 13.1 us  [near(): return lax.ppermute(piece, 'pcol', twin(nc))]
    ppermute x6, waiting for transfers between devices: 1.12 us -> 0.02 us  [swap(): return lax.ppermute(part, 'prow', twin(nr))]
    pallas_call x6, Pallas kernels: 16.3 us -> 15.5 us  [call(): pl.pallas_call(body, out_shape=outs, in_specs=in_specs, out_specs=out_spe...]
  transfers between devices with their start and end apart: 19 -> 19, of which waited for: 5 -> 5; matrix products, arithmetic and copies ran while one was open for 8% -> 8% of each run, Pallas kernels for 12% -> 13%
where the time goes in v4:
time: 69.4 us; the launch traced here: 68.9 us
  starting transfers between devices  34.8 us (50%)
  Pallas kernels  15.5 us (22%)
  waiting for transfers between devices  7.01 us (10%)
  other arithmetic  5.67 us (8%)
  local copies, waits for them, and re-layouts  5.55 us (8%)
    pallas_call x6, Pallas kernels, call(): pl.pallas_call(body, out_shape=outs, in_specs=in_specs, out_specs=out_spe...  15.5 us
    ppermute x3, starting transfers between devices, near(): return lax.ppermute(piece, 'pcol', twin(nc))  13.1 us
    ppermute x3, starting transfers between devices, far(): got = lax.ppermute(piece, 'pcol', pairs)  8.68 us
    unnamed x34, local copies, waits for them, and re-layouts  5.48 us
    ppermute x1, starting transfers between devices, local(): top = pick(pairs, lax.ppermute(top, 'prow', pairs), top)  4.23 us
    ppermute x3, waiting for transfers between devices, near(): return lax.ppermute(piece, 'pcol', twin(nc))  3.76 us
    select_n x3, other arithmetic, far(): piece = jnp.where(member(my_col, pairs), got, piece)  2.32 us
    ppermute x1, waiting for transfers between devices, local(): lax.ppermute(side, joined, joint)  1.55 us
  transfers between devices with their start and end apart: 19, of which 5 were waited for; matrix products, arithmetic and copies ran while one was open for 8% of the time, Pallas kernels for 13%

profile of v4, /device:TPU:0, one launch (start us, length us, event | category | flops | bytes accessed | tf_op | source)
XLA Modules:
  0.0 68.9 jit_solution(16893812748871696175)
XLA Ops:
  0.0 1.6 %copy-done = bf16[4,256,4,256]{3,2,1,0:T(4,128)(2,1)S(1)} copy-done((bf16[4,256,4,256]{3,2,1,0:T(4,128)(2,1)S(1)}, bf16[4,256,4,256]{3,2,1,0:T(4,128)(2,1)}, u32[]{:S(2)}) %copy-start) | copy-done | bytes 2097176
  1.6 0.2 shard_map.46
  1.8 6.1 %collective-permute-start = (bf16[256,256]{1,0:T(8,128)(2,1)S(1)}, bf16[256,256]{1,0:T(8,128)(2,1)S(1)}, u32[]{:S(2)}, u32[]{:S(2)}) collective-permute-start(bf16[256,256]{1,0:T(8,128)(2,1)S(1)} %get-tuple-element.17.first_piece), channel_id=1, source_target_pairs={{0,2},{1,3},{4,6},{5,7},{8,10},{9,11},{12,14},{13,15},{16,18},{17,... | collective-permute-start | bytes 393224 | tf_op jit(solution)/shard_map/ppermute | solution.py:258
  7.9 4.2 %collective-permute-start.3 = (bf16[4,256,256]{2,1,0:T(8,128)(2,1)S(1)}, bf16[4,256,256]{2,1,0:T(8,128)(2,1)}, u32[]{:S(2)}, u32[]{:S(2)}) collective-permute-start(bf16[4,256,256]{2,1,0:T(8,128)(2,1)S(1)} %get-tuple-element.23), channel_id=1, source_target_pairs={{0,16},{4,12},{1,17},{5,13},{2,18},{6,14},{3,19},{7,15}} | collective-permute-start | bytes 1572872 | tf_op jit(solution)/shard_map/ppermute | solution.py:277
  12.1 0.1 pad_add_fusion.me
  12.2 3.9 %shard_map.47 = (bf16[4,256,256]{2,1,0:T(8,128)(2,1)S(1)}, bf16[4,256,256]{2,1,0:T(8,128)(2,1)}, bf16[2,256,256]{2,1,0:T(8,128)(2,1)S(1)}, bf16[256,256]{1,0:T(8,128)(2,1)}, s32[1,512]{1,0:T(1,128)S(1)}) custom-call(s32[2]{0:T(128)S(1)} %pad_add_fusion.me, bf16[4,256,4,256]{3,2,1,0:T(4,128)(2,1)S(1)} %copy-done.1, s32[2,256]{1,0:T(2,128)S(1)} %copy-done.9, ...), custom_call_target="tpu_custom_call" | custom-call | flops 1000000 | tf_op jit(solution)/shard_map/pallas_call | solution.py:62
  16.1 0.8 %copy-done.12 = bf16[4,256,256]{2,1,0:T(8,128)(2,1)} copy-done((bf16[4,256,256]{2,1,0:T(8,128)(2,1)}, bf16[4,256,256]{2,1,0:T(8,128)(2,1)S(1)}, u32[]{:S(2)}) %copy-start.12) | copy-done | bytes 524312
  16.9 0.0 collective-permute-done
  16.9 0.1 collective-permute-start.2
  17.0 1.3 %collective-permute-start.7 = (bf16[2,256,256]{2,1,0:T(8,128)(2,1)S(1)}, bf16[2,256,256]{2,1,0:T(8,128)(2,1)S(1)}, u32[]{:S(2)}, u32[]{:S(2)}) collective-permute-start(bf16[2,256,256]{2,1,0:T(8,128)(2,1)S(1)} %get-tuple-element.24), channel_id=1, source_target_pairs={{0,2},{1,3},{4,6},{5,7},{8,10},{9,11},{12,14},{13,15},{16,18},{17,... | collective-permute-start | bytes 786440 | tf_op jit(solution)/shard_map/ppermute | solution.py:258
  18.3 2.1 %collective-permute-start.1 = (bf16[256,256]{1,0:T(8,128)(2,1)S(1)}, bf16[256,256]{1,0:T(8,128)(2,1)S(1)}, u32[]{:S(2)}, u32[]{:S(2)}) collective-permute-start(bf16[256,256]{1,0:T(8,128)(2,1)S(1)} %broadcast_select_fusion.6.refs_11_), channel_id=1, source_target_pairs={{0,1},{1,0},{2,3},{3,2},{4,5},{5,4},{6,7},{7,6},{8,9},{9,8},{10,11... | collective-permute-start | bytes 393224 | tf_op jit(solution)/shard_map/ppermute | solution.py:263
  20.4 0.0 collective-permute-done.3
  20.4 0.1 broadcast_select_fusion.top
  20.5 1.0 %copy-done.13 = bf16[4,256,256]{2,1,0:T(8,128)(2,1)S(1)} copy-done((bf16[4,256,256]{2,1,0:T(8,128)(2,1)S(1)}, bf16[4,256,256]{2,1,0:T(8,128)(2,1)}, u32[]{:S(2)}) %copy-start.13) | copy-done | bytes 524312
  21.5 2.1 %shard_map.49.part = bf16[8,256,256]{2,1,0:T(8,128)(2,1)} custom-call(bf16[4,256,256]{2,1,0:T(8,128)(2,1)S(1)} %copy-done.13, bf16[4,256,256]{2,1,0:T(8,128)(2,1)} %collective-permute-done.2.got, bf16[4,256,256]{2,1,0:T(8,128)(2,1)S(1)} %broadcast_select_fusion.top), custom_call_target="tpu_custom_call" | custom-call | flops 99999997952 | tf_op jit(solution)/shard_map/pallas_call | solution.py:62
  23.6 1.5 %collective-permute-start.4 = (bf16[8,256,256]{2,1,0:T(8,128)(2,1)}, bf16[8,256,256]{2,1,0:T(8,128)(2,1)}, u32[]{:S(2)}, u32[]{:S(2)}) collective-permute-start(bf16[8,256,256]{2,1,0:T(8,128)(2,1)} %shard_map.49.part), channel_id=1, source_target_pairs={{0,8},{4,20},{8,0},{12,28},{16,24},{20,4},{24,16},{28,12},{1,9},{5... | collective-permute-start | bytes 3145736 | tf_op jit(solution)/shard_map/ppermute | solution.py:309
  25.1 2.5 %collective-permute-done.1.gate.refs_14_ = bf16[256,256]{1,0:T(8,128)(2,1)S(1)} collective-permute-done((bf16[256,256]{1,0:T(8,128)(2,1)S(1)}, bf16[256,256]{1,0:T(8,128)(2,1)S(1)}, u32[]{:S(2)}, u32[]{:S(2)}) %collective-permute-start.1) | collective-permute-done | bytes 131104 | tf_op jit(solution)/shard_map/ppermute | solution.py:263
  27.7 1.0 %shard_map.48.refs_0_ = bf16[4,4,256,256]{3,2,1,0:T(8,128)(2,1)S(1)} custom-call(bf16[4,256,4,256]{3,2,1,0:T(4,128)(2,1)S(1)} %copy-done.1, bf16[256,256]{1,0:T(8,128)(2,1)S(1)} %collective-permute-done.1.gate.refs_14_), custom_call_target="tpu_custom_call" | custom-call | flops 1000000000 | tf_op jit(solution)/shard_map/pallas_call | solution.py:62
  28.6 0.0 copy-start.2
  28.6 1.3 %copy-done.2 = bf16[4,4,256,256]{3,2,1,0:T(8,128)(2,1)} copy-done((bf16[4,4,256,256]{3,2,1,0:T(8,128)(2,1)}, bf16[4,4,256,256]{3,2,1,0:T(8,128)(2,1)S(1)}, u32[]{:S(2)}) %copy-start.2) | copy-done | bytes 2097176
  30.0 0.0 collective-permute-done.7
  30.0 0.7 %broadcast_select_fusion.1.refs_12_ = bf16[2,256,256]{2,1,0:T(8,128)(2,1)} fusion(bf16[2,256,256]{2,1,0:T(8,128)(2,1)S(1)} %collective-permute-done.7, bf16[2,256,256]{2,1,0:T(8,128)(2,1)S(1)} %get-tuple-element.24, pred[]{:T(512)S(6)} %gt.18), kind=kLoop, calls=%fused_computation.5 | loop fusion | flops 131072 | bytes 786433 | tf_op jit(solution)/shard_map/jit(_where)/select_n | solution.py:259
  30.7 1.3 %collective-permute-start.8 = (bf16[2,256,256]{2,1,0:T(8,128)(2,1)S(1)}, bf16[2,256,256]{2,1,0:T(8,128)(2,1)S(1)}, u32[]{:S(2)}, u32[]{:S(2)}) collective-permute-start(bf16[2,256,256]{2,1,0:T(8,128)(2,1)S(1)} %pad_maximum_fusion.1), channel_id=1, source_target_pairs={{0,8},{4,20},{1,9},{5,21},{2,10},{6,22},{3,11},{7,23}} | collective-permute-start | bytes 786440 | tf_op jit(solution)/shard_map/ppermute | solution.py:304
  32.0 1.3 %collective-permute-start.11 = (bf16[256,256]{1,0:T(8,128)(2,1)}, bf16[256,256]{1,0:T(8,128)(2,1)S(1)}, u32[]{:S(2)}, u32[]{:S(2)}) collective-permute-start(bf16[256,256]{1,0:T(8,128)(2,1)} %get-tuple-element.26), channel_id=1, source_target_pairs={{0,2},{1,3},{4,6},{5,7},{8,10},{9,11},{12,14},{13,15},{16,18},{17,... | collective-permute-start | bytes 393224 | tf_op jit(solution)/shard_map/ppermute | solution.py:258
  33.3 5.9 %collective-permute-start.12 = (bf16[2,256,256]{2,1,0:T(8,128)(2,1)}, bf16[2,256,256]{2,1,0:T(8,128)(2,1)S(1)}, u32[]{:S(2)}, u32[]{:S(2)}) collective-permute-start(bf16[2,256,256]{2,1,0:T(8,128)(2,1)} %broadcast_select_fusion.1.refs_12_), channel_id=1, source_target_pairs={{0,1},{1,0},{2,3},{3,2},{4,5},{5,4},{6,7},{7,6},{8,9},{9,8},{10,11... | collective-permute-start | bytes 786440 | tf_op jit(solution)/shard_map/ppermute | solution.py:263
  39.3 1.2 %collective-permute-done.8 = bf16[2,256,256]{2,1,0:T(8,128)(2,1)S(1)} collective-permute-done((bf16[2,256,256]{2,1,0:T(8,128)(2,1)S(1)}, bf16[2,256,256]{2,1,0:T(8,128)(2,1)S(1)}, u32[]{:S(2)}, u32[]{:S(2)}) %collective-permute-start.8) | collective-permute-done | bytes 262176 | tf_op jit(solution)/shard_map/ppermute | solution.py:304
  40.5 0.0 collective-permute-done.4.got
  40.5 1.7 %shard_map.50 = bf16[8,256,256]{2,1,0:T(8,128)(2,1)S(1)} custom-call(s32[1]{0:T(128)} %bitcast.2.taken, bf16[8,256,256]{2,1,0:T(8,128)(2,1)} %shard_map.49.part, bf16[8,256,256]{2,1,0:T(8,128)(2,1)} %collective-permute-done.4.got), custom_call_target="tpu_custom_call" | custom-call | flops 99999997952 | tf_op jit(solution)/shard_map/pallas_call | solution.py:62
  42.3 0.8 %collective-permute-start.5 = (bf16[256,256]{1,0:T(8,128)(2,1)S(1)}, bf16[256,256]{1,0:T(8,128)(2,1)S(1)}, u32[]{:S(2)}, u32[]{:S(2)}) collective-permute-start(bf16[256,256]{1,0:T(8,128)(2,1)S(1)} %slice_bitcast_fusion), channel_id=1, source_target_pairs={{0,16},{4,12},{8,24},{12,4},{16,0},{20,28},{24,8},{28,20},{1,17},{... | collective-permute-start | bytes 393224 | tf_op jit(solution)/shard_map/ppermute | solution.py:315
  43.1 0.9 %pad_maximum_fusion = bf16[5,256,256]{2,1,0:T(8,128)(2,1)} fusion(bf16[2,256,256]{2,1,0:T(8,128)(2,1)S(1)} %broadcast_select_fusion.2, bf16[3,256,256]{2,1,0:T(8,128)(2,1)S(1)} %slice.21), kind=kLoop, calls=%fused_computation | loop fusion | flops 327680 | bytes 1310720 | tf_op jit(solution)/shard_map/concatenate | solution.py:316
  44.0 1.3 %collective-permute-start.9 = (bf16[5,256,256]{2,1,0:T(8,128)(2,1)}, bf16[5,256,256]{2,1,0:T(8,128)(2,1)}, u32[]{:S(2)}, u32[]{:S(2)}) collective-permute-start(bf16[5,256,256]{2,1,0:T(8,128)(2,1)} %pad_maximum_fusion), channel_id=1, source_target_pairs={{0,16},{4,12},{8,24},{12,4},{16,0},{20,28},{24,8},{28,20},{1,17},{... | collective-permute-start | bytes 1966088 | tf_op jit(solution)/shard_map/ppermute | solution.py:316
  45.3 0.0 collective-permute-done.11
  45.3 1.6 %broadcast_select_fusion.5.refs_13_ = bf16[256,256]{1,0:T(8,128)(2,1)} fusion(bf16[256,256]{1,0:T(8,128)(2,1)S(1)} %collective-permute-done.11, bf16[256,256]{1,0:T(8,128)(2,1)} %get-tuple-element.26, pred[]{:T(512)S(6)} %gt.18), kind=kLoop, calls=%fused_computation.12 | loop fusion | flops 65536 | bytes 393217 | tf_op jit(solution)/shard_map/jit(_where)/select_n | solution.py:259
  46.9 0.5 collective-permute-done.5
  47.3 0.0 copy-start.3
  47.4 0.7 %copy-done.7 = bf16[2,256,256]{2,1,0:T(8,128)(2,1)} copy-done((bf16[2,256,256]{2,1,0:T(8,128)(2,1)}, bf16[2,256,256]{2,1,0:T(8,128)(2,1)S(1)}, u32[]{:S(2)}) %copy-start.7) | copy-done | bytes 262168
  48.1 1.3 %collective-permute-start.13 = (bf16[256,256]{1,0:T(8,128)(2,1)S(1)}, bf16[256,256]{1,0:T(8,128)(2,1)}, u32[]{:S(2)}, u32[]{:S(2)}) collective-permute-start(bf16[256,256]{1,0:T(8,128)(2,1)S(1)} %fusion.refs_1_), channel_id=1, source_target_pairs={{1,3},{4,6},{9,11},{12,14},{17,19},{20,22},{25,27},{28,30}} | collective-permute-start | bytes 393224 | tf_op jit(solution)/shard_map/ppermute | solution.py:324
  49.4 0.5 collective-permute-start.16
  49.9 0.1 collective-permute-start.6
  50.0 1.3 %collective-permute-start.14 = (bf16[256,256]{1,0:T(8,128)(2,1)S(1)}, bf16[256,256]{1,0:T(8,128)(2,1)S(1)}, u32[]{:S(2)}, u32[]{:S(2)}) collective-permute-start(bf16[256,256]{1,0:T(8,128)(2,1)S(1)} %broadcast_select_fusion.3), channel_id=1, source_target_pairs={{1,0},{3,2},{4,5},{6,7},{9,8},{11,10},{12,13},{14,15},{17,16},{19,... | collective-permute-start | bytes 393224 | tf_op jit(solution)/shard_map/ppermute | solution.py:329
  51.3 5.1 %collective-permute-start.18 = (bf16[256,256]{1,0:T(8,128)(2,1)}, bf16[256,256]{1,0:T(8,128)(2,1)S(1)}, u32[]{:S(2)}, u32[]{:S(2)}) collective-permute-start(bf16[256,256]{1,0:T(8,128)(2,1)} %broadcast_select_fusion.5.refs_13_), channel_id=1, source_target_pairs={{0,1},{1,0},{2,3},{3,2},{4,5},{5,4},{6,7},{7,6},{8,9},{9,8},{10,11... | collective-permute-start | bytes 393224 | tf_op jit(solution)/shard_map/ppermute | solution.py:263
  56.5 1.0 %slice_add_fusion.refs_3_ = bf16[3,256,256]{2,1,0:T(8,128)(2,1)S(1)} fusion(bf16[5,256,256]{2,1,0:T(8,128)(2,1)} %collective-permute-done.9, bf16[8,256,256]{2,1,0:T(8,128)(2,1)S(1)} %shard_map.50), kind=kLoop, calls=%fused_computation.2 | loop fusion | flops 196608 | bytes 1179648 | tf_op jit(solution)/shard_map/add | solution.py:317
  57.5 0.1 collective-permute-start.10
  57.6 1.1 %slice_select_fusion.refs_9_ = bf16[2,256,256]{2,1,0:T(8,128)(2,1)S(1)} fusion(bf16[5,256,256]{2,1,0:T(8,128)(2,1)} %collective-permute-done.9, pred[]{:T(512)S(6)} %gt.22, bf16[2,256,256]{2,1,0:T(8,128)(2,1)} %copy-done.16, bf16[1,256,256]{2,1,0:T(8,128)(2,1)} %copy-done.15, bf16[1,256,256]{2,1,0:T(8,128)(2,1)} %copy-done.14, pred[]{:T(512)S(6)} %gt.21), kind=kLoop, calls=%fused_computation.3 | loop fusion | flops 393216 | bytes 1048578 | tf_op jit(solution)/shard_map/jit(_where)/select_n | solution.py:269
  58.7 1.5 %collective-permute-done.14 = bf16[256,256]{1,0:T(8,128)(2,1)S(1)} collective-permute-done((bf16[256,256]{1,0:T(8,128)(2,1)S(1)}, bf16[256,256]{1,0:T(8,128)(2,1)S(1)}, u32[]{:S(2)}, u32[]{:S(2)}) %collective-permute-start.14) | collective-permute-done | bytes 131104 | tf_op jit(solution)/shard_map/ppermute | solution.py:329
  60.3 0.6 collective-permute-start.15
  60.8 1.3 %collective-permute-done.18.refs_16_ = bf16[256,256]{1,0:T(8,128)(2,1)S(1)} collective-permute-done((bf16[256,256]{1,0:T(8,128)(2,1)}, bf16[256,256]{1,0:T(8,128)(2,1)S(1)}, u32[]{:S(2)}, u32[]{:S(2)}) %collective-permute-start.18) | collective-permute-done | bytes 131104 | tf_op jit(solution)/shard_map/ppermute | solution.py:263
  62.2 6.7 %shard_map.51 = bf16[4,256,4,256]{3,2,1,0:T(4,128)(2,1)} custom-call(s32[2]{0:T(128)S(1)} %copy-done.11, s32[1,512]{1,0:T(1,128)S(1)} %get-tuple-element.18.goes, bf16[2,256,256]{2,1,0:T(8,128)(2,1)S(1)} %copy-done.5, bf16[2,256,256]{2,1,0:T(8,128)(2,1)S(1)} %copy-done.6, bf16[4,4,256,256]{3,2,1,0:T(8,128)(2,1)S(1)} %copy-done.3, ...), custom_call_target="tpu_custom_call" | custom-call | flops 1000000 | tf_op jit(solution)/shard_map/pallas_call | solution.py:62
  (47 shorter events, 0.3 us)
Async XLA Ops:
  0.0 1.6 %copy-start = (bf16[4,256,4,256]{3,2,1,0:T(4,128)(2,1)S(1)}, bf16[4,256,4,256]{3,2,1,0:T(4,128)(2,1)}, u32[]{:S(2)}) copy-start(bf16[4,256,4,256]{3,2,1,0:T(4,128)(2,1)} %a.5) | copy-start | bytes 6291460
  1.6 10.6 %copy-start.1 = (bf16[4,256,4,256]{3,2,1,0:T(4,128)(2,1)S(1)}, bf16[4,256,4,256]{3,2,1,0:T(4,128)(2,1)}, u32[]{:S(2)}) copy-start(bf16[4,256,4,256]{3,2,1,0:T(4,128)(2,1)} %a.5) | copy-start | bytes 6291460
  1.6 10.6 %copy-start.9 = (s32[2,256]{1,0:T(2,128)S(1)}, s32[2,256]{1,0:T(2,128)}, u32[]{:S(2)}) copy-start(s32[2,256]{1,0:T(2,128)} %row.1) | copy-start | bytes 6148
  1.8 15.1 %collective-permute-start = (bf16[256,256]{1,0:T(8,128)(2,1)S(1)}, bf16[256,256]{1,0:T(8,128)(2,1)S(1)}, u32[]{:S(2)}, u32[]{:S(2)}) collective-permute-start(bf16[256,256]{1,0:T(8,128)(2,1)S(1)} %get-tuple-element.17.first_piece), channel_id=1, source_target_pairs={{0,2},{1,3},{4,6},{5,7},{8,10},{9,11},{12,14},{13,15},{16,18},{17,... | collective-permute-start | bytes 393224 | tf_op jit(solution)/shard_map/ppermute | solution.py:258
  7.9 12.5 %collective-permute-start.3 = (bf16[4,256,256]{2,1,0:T(8,128)(2,1)S(1)}, bf16[4,256,256]{2,1,0:T(8,128)(2,1)}, u32[]{:S(2)}, u32[]{:S(2)}) collective-permute-start(bf16[4,256,256]{2,1,0:T(8,128)(2,1)S(1)} %get-tuple-element.23), channel_id=1, source_target_pairs={{0,16},{4,12},{1,17},{5,13},{2,18},{6,14},{3,19},{7,15}} | collective-permute-start | bytes 1572872 | tf_op jit(solution)/shard_map/ppermute | solution.py:277
  12.2 3.9 %copy-start.10 = (s32[2]{0:T(128)}, s32[2]{0:T(128)S(1)}, u32[]{:S(2)}) copy-start(s32[2]{0:T(128)S(1)} %pad_add_fusion.me) | copy-start | bytes 28
  16.1 0.8 %copy-start.12 = (bf16[4,256,256]{2,1,0:T(8,128)(2,1)}, bf16[4,256,256]{2,1,0:T(8,128)(2,1)S(1)}, u32[]{:S(2)}) copy-start(bf16[4,256,256]{2,1,0:T(8,128)(2,1)S(1)} %get-tuple-element.19.keep) | copy-start | bytes 1572868
  16.9 3.6 %collective-permute-start.2 = (bf16[4,256,256]{2,1,0:T(8,128)(2,1)}, bf16[4,256,256]{2,1,0:T(8,128)(2,1)}, u32[]{:S(2)}, u32[]{:S(2)}) collective-permute-start(bf16[4,256,256]{2,1,0:T(8,128)(2,1)} %get-tuple-element.22), channel_id=1, source_target_pairs={{0,4},{4,0},{8,12},{12,8},{16,20},{20,16},{24,28},{28,24},{1,5},{5... | collective-permute-start | bytes 1572872 | tf_op jit(solution)/shard_map/ppermute | solution.py:266
  17.0 13.0 %collective-permute-start.7 = (bf16[2,256,256]{2,1,0:T(8,128)(2,1)S(1)}, bf16[2,256,256]{2,1,0:T(8,128)(2,1)S(1)}, u32[]{:S(2)}, u32[]{:S(2)}) collective-permute-start(bf16[2,256,256]{2,1,0:T(8,128)(2,1)S(1)} %get-tuple-element.24), channel_id=1, source_target_pairs={{0,2},{1,3},{4,6},{5,7},{8,10},{9,11},{12,14},{13,15},{16,18},{17,... | collective-permute-start | bytes 786440 | tf_op jit(solution)/shard_map/ppermute | solution.py:258
  18.3 9.3 %collective-permute-start.1 = (bf16[256,256]{1,0:T(8,128)(2,1)S(1)}, bf16[256,256]{1,0:T(8,128)(2,1)S(1)}, u32[]{:S(2)}, u32[]{:S(2)}) collective-permute-start(bf16[256,256]{1,0:T(8,128)(2,1)S(1)} %broadcast_select_fusion.6.refs_11_), channel_id=1, source_target_pairs={{0,1},{1,0},{2,3},{3,2},{4,5},{5,4},{6,7},{7,6},{8,9},{9,8},{10,11... | collective-permute-start | bytes 393224 | tf_op jit(solution)/shard_map/ppermute | solution.py:263
  20.5 1.0 %copy-start.13 = (bf16[4,256,256]{2,1,0:T(8,128)(2,1)S(1)}, bf16[4,256,256]{2,1,0:T(8,128)(2,1)}, u32[]{:S(2)}) copy-start(bf16[4,256,256]{2,1,0:T(8,128)(2,1)} %copy-done.12) | copy-start | bytes 1572868
  23.6 16.9 %collective-permute-start.4 = (bf16[8,256,256]{2,1,0:T(8,128)(2,1)}, bf16[8,256,256]{2,1,0:T(8,128)(2,1)}, u32[]{:S(2)}, u32[]{:S(2)}) collective-permute-start(bf16[8,256,256]{2,1,0:T(8,128)(2,1)} %shard_map.49.part), channel_id=1, source_target_pairs={{0,8},{4,20},{8,0},{12,28},{16,24},{20,4},{24,16},{28,12},{1,9},{5... | collective-permute-start | bytes 3145736 | tf_op jit(solution)/shard_map/ppermute | solution.py:309
  27.6 12.8 %copy-start.14 = (bf16[1,256,256]{2,1,0:T(8,128)(2,1)}, bf16[1,256,256]{2,1,0:T(8,128)(2,1)S(1)}, u32[]{:S(2)}) copy-start(bf16[1,256,256]{2,1,0:T(8,128)(2,1)S(1)} %get-tuple-element.29) | copy-start | bytes 393220
  27.7 12.8 %copy-start.15 = (bf16[1,256,256]{2,1,0:T(8,128)(2,1)}, bf16[1,256,256]{2,1,0:T(8,128)(2,1)S(1)}, u32[]{:S(2)}) copy-start(bf16[1,256,256]{2,1,0:T(8,128)(2,1)S(1)} %get-tuple-element.30) | copy-start | bytes 393220
  28.6 1.3 %copy-start.2 = (bf16[4,4,256,256]{3,2,1,0:T(8,128)(2,1)}, bf16[4,4,256,256]{3,2,1,0:T(8,128)(2,1)S(1)}, u32[]{:S(2)}) copy-start(bf16[4,4,256,256]{3,2,1,0:T(8,128)(2,1)S(1)} %shard_map.48.refs_0_) | copy-start | bytes 6291460
  30.7 9.7 %collective-permute-start.8 = (bf16[2,256,256]{2,1,0:T(8,128)(2,1)S(1)}, bf16[2,256,256]{2,1,0:T(8,128)(2,1)S(1)}, u32[]{:S(2)}, u32[]{:S(2)}) collective-permute-start(bf16[2,256,256]{2,1,0:T(8,128)(2,1)S(1)} %pad_maximum_fusion.1), channel_id=1, source_target_pairs={{0,8},{4,20},{1,9},{5,21},{2,10},{6,22},{3,11},{7,23}} | collective-permute-start | bytes 786440 | tf_op jit(solution)/shard_map/ppermute | solution.py:304
  32.0 13.3 %collective-permute-start.11 = (bf16[256,256]{1,0:T(8,128)(2,1)}, bf16[256,256]{1,0:T(8,128)(2,1)S(1)}, u32[]{:S(2)}, u32[]{:S(2)}) collective-permute-start(bf16[256,256]{1,0:T(8,128)(2,1)} %get-tuple-element.26), channel_id=1, source_target_pairs={{0,2},{1,3},{4,6},{5,7},{8,10},{9,11},{12,14},{13,15},{16,18},{17,... | collective-permute-start | bytes 393224 | tf_op jit(solution)/shard_map/ppermute | solution.py:258
  33.3 14.0 %collective-permute-start.12 = (bf16[2,256,256]{2,1,0:T(8,128)(2,1)}, bf16[2,256,256]{2,1,0:T(8,128)(2,1)S(1)}, u32[]{:S(2)}, u32[]{:S(2)}) collective-permute-start(bf16[2,256,256]{2,1,0:T(8,128)(2,1)} %broadcast_select_fusion.1.refs_12_), channel_id=1, source_target_pairs={{0,1},{1,0},{2,3},{3,2},{4,5},{5,4},{6,7},{7,6},{8,9},{9,8},{10,11... | collective-permute-start | bytes 786440 | tf_op jit(solution)/shard_map/ppermute | solution.py:263
  40.5 1.8 %copy-start.16 = (bf16[2,256,256]{2,1,0:T(8,128)(2,1)}, bf16[2,256,256]{2,1,0:T(8,128)(2,1)S(1)}, u32[]{:S(2)}) copy-start(bf16[2,256,256]{2,1,0:T(8,128)(2,1)S(1)} %collective-permute-done.8) | copy-start | bytes 786436
  42.3 5.0 %collective-permute-start.5 = (bf16[256,256]{1,0:T(8,128)(2,1)S(1)}, bf16[256,256]{1,0:T(8,128)(2,1)S(1)}, u32[]{:S(2)}, u32[]{:S(2)}) collective-permute-start(bf16[256,256]{1,0:T(8,128)(2,1)S(1)} %slice_bitcast_fusion), channel_id=1, source_target_pairs={{0,16},{4,12},{8,24},{12,4},{16,0},{20,28},{24,8},{28,20},{1,17},{... | collective-permute-start | bytes 393224 | tf_op jit(solution)/shard_map/ppermute | solution.py:315
  44.0 12.5 %collective-permute-start.9 = (bf16[5,256,256]{2,1,0:T(8,128)(2,1)}, bf16[5,256,256]{2,1,0:T(8,128)(2,1)}, u32[]{:S(2)}, u32[]{:S(2)}) collective-permute-start(bf16[5,256,256]{2,1,0:T(8,128)(2,1)} %pad_maximum_fusion), channel_id=1, source_target_pairs={{0,16},{4,12},{8,24},{12,4},{16,0},{20,28},{24,8},{28,20},{1,17},{... | collective-permute-start | bytes 1966088 | tf_op jit(solution)/shard_map/ppermute | solution.py:316
  47.3 14.8 %copy-start.3 = (bf16[4,4,256,256]{3,2,1,0:T(8,128)(2,1)S(1)}, bf16[4,4,256,256]{3,2,1,0:T(8,128)(2,1)}, u32[]{:S(2)}) copy-start(bf16[4,4,256,256]{3,2,1,0:T(8,128)(2,1)} %copy-done.2) | copy-start | bytes 6291460
  47.4 14.8 %copy-start.11 = (s32[2]{0:T(128)S(1)}, s32[2]{0:T(128)}, u32[]{:S(2)}) copy-start(s32[2]{0:T(128)} %copy-done.10) | copy-start | bytes 28
  47.4 0.7 %copy-start.7 = (bf16[2,256,256]{2,1,0:T(8,128)(2,1)}, bf16[2,256,256]{2,1,0:T(8,128)(2,1)S(1)}, u32[]{:S(2)}) copy-start(bf16[2,256,256]{2,1,0:T(8,128)(2,1)S(1)} %collective-permute-done.12.refs_15_) | copy-start | bytes 786436
  48.1 1.9 %collective-permute-start.13 = (bf16[256,256]{1,0:T(8,128)(2,1)S(1)}, bf16[256,256]{1,0:T(8,128)(2,1)}, u32[]{:S(2)}, u32[]{:S(2)}) collective-permute-start(bf16[256,256]{1,0:T(8,128)(2,1)S(1)} %fusion.refs_1_), channel_id=1, source_target_pairs={{1,3},{4,6},{9,11},{12,14},{17,19},{20,22},{25,27},{28,30}} | collective-permute-start | bytes 393224 | tf_op jit(solution)/shard_map/ppermute | solution.py:324
  49.4 12.8 %copy-start.4 = (bf16[256,256]{1,0:T(8,128)(2,1)S(1)}, bf16[256,256]{1,0:T(8,128)(2,1)}, u32[]{:S(2)}) copy-start(bf16[256,256]{1,0:T(8,128)(2,1)} %broadcast_select_fusion.5.refs_13_) | copy-start | bytes 393220
  49.4 12.8 %copy-start.5 = (bf16[2,256,256]{2,1,0:T(8,128)(2,1)S(1)}, bf16[2,256,256]{2,1,0:T(8,128)(2,1)}, u32[]{:S(2)}) copy-start(bf16[2,256,256]{2,1,0:T(8,128)(2,1)} %lower.1) | copy-start | bytes 786436
  49.4 12.8 %copy-start.6 = (bf16[2,256,256]{2,1,0:T(8,128)(2,1)S(1)}, bf16[2,256,256]{2,1,0:T(8,128)(2,1)}, u32[]{:S(2)}) copy-start(bf16[2,256,256]{2,1,0:T(8,128)(2,1)} %upper.1) | copy-start | bytes 786436
  49.4 12.8 %copy-start.8 = (bf16[2,256,256]{2,1,0:T(8,128)(2,1)S(1)}, bf16[2,256,256]{2,1,0:T(8,128)(2,1)}, u32[]{:S(2)}) copy-start(bf16[2,256,256]{2,1,0:T(8,128)(2,1)} %copy-done.7) | copy-start | bytes 786436
  49.4 12.7 %collective-permute-start.16 = (bf16[4,256,256]{2,1,0:T(8,128)(2,1)S(1)}, bf16[4,256,256]{2,1,0:T(8,128)(2,1)S(1)}, u32[]{:S(2)}, u32[]{:S(2)}) collective-permute-start(bf16[4,256,256]{2,1,0:T(8,128)(2,1)S(1)} %slice.23.refs_7_), channel_id=1, source_target_pairs={{0,4},{4,0},{8,12},{12,8},{16,20},{20,16},{24,28},{28,24},{1,5},{5... | collective-permute-start | bytes 1572872 | tf_op jit(solution)/shard_map/ppermute | solution.py:266
  49.9 10.4 %collective-permute-start.6 = (bf16[256,256]{1,0:T(8,128)(2,1)S(1)}, bf16[256,256]{1,0:T(8,128)(2,1)S(1)}, u32[]{:S(2)}, u32[]{:S(2)}) collective-permute-start(bf16[256,256]{1,0:T(8,128)(2,1)S(1)} %fusion.refs_1_), channel_id=1, source_target_pairs={{0,4},{4,0},{8,12},{12,8},{16,20},{20,16},{24,28},{28,24},{1,5},{5... | collective-permute-start | bytes 393224 | tf_op jit(solution)/shard_map/ppermute | solution.py:266
  50.0 10.2 %collective-permute-start.14 = (bf16[256,256]{1,0:T(8,128)(2,1)S(1)}, bf16[256,256]{1,0:T(8,128)(2,1)S(1)}, u32[]{:S(2)}, u32[]{:S(2)}) collective-permute-start(bf16[256,256]{1,0:T(8,128)(2,1)S(1)} %broadcast_select_fusion.3), channel_id=1, source_target_pairs={{1,0},{3,2},{4,5},{6,7},{9,8},{11,10},{12,13},{14,15},{17,16},{19,... | collective-permute-start | bytes 393224 | tf_op jit(solution)/shard_map/ppermute | solution.py:329
  51.3 10.8 %collective-permute-start.18 = (bf16[256,256]{1,0:T(8,128)(2,1)}, bf16[256,256]{1,0:T(8,128)(2,1)S(1)}, u32[]{:S(2)}, u32[]{:S(2)}) collective-permute-start(bf16[256,256]{1,0:T(8,128)(2,1)} %broadcast_select_fusion.5.refs_13_), channel_id=1, source_target_pairs={{0,1},{1,0},{2,3},{3,2},{4,5},{5,4},{6,7},{7,6},{8,9},{9,8},{10,11... | collective-permute-start | bytes 393224 | tf_op jit(solution)/shard_map/ppermute | solution.py:263
  57.5 4.6 %collective-permute-start.10 = (bf16[3,256,256]{2,1,0:T(8,128)(2,1)S(1)}, bf16[3,256,256]{2,1,0:T(8,128)(2,1)S(1)}, u32[]{:S(2)}, u32[]{:S(2)}) collective-permute-start(bf16[3,256,256]{2,1,0:T(8,128)(2,1)S(1)} %slice_add_fusion.refs_3_), channel_id=1, source_target_pairs={{0,4},{4,0},{8,12},{12,8},{16,20},{20,16},{24,28},{28,24},{1,5},{5... | collective-permute-start | bytes 1179656 | tf_op jit(solution)/shard_map/ppermute | solution.py:266
  60.2 1.9 %collective-permute-start.17 = (bf16[2,256,256]{2,1,0:T(8,128)(2,1)S(1)}, bf16[2,256,256]{2,1,0:T(8,128)(2,1)S(1)}, u32[]{:S(2)}, u32[]{:S(2)}) collective-permute-start(bf16[2,256,256]{2,1,0:T(8,128)(2,1)S(1)} %slice_select_fusion.refs_9_), channel_id=1, source_target_pairs={{0,4},{4,0},{8,12},{12,8},{16,20},{20,16},{24,28},{28,24},{1,5},{5... | collective-permute-start | bytes 786440 | tf_op jit(solution)/shard_map/ppermute | solution.py:266
  60.3 1.9 %collective-permute-start.15 = (bf16[256,256]{1,0:T(8,128)(2,1)S(1)}, bf16[256,256]{1,0:T(8,128)(2,1)S(1)}, u32[]{:S(2)}, u32[]{:S(2)}) collective-permute-start(bf16[256,256]{1,0:T(8,128)(2,1)S(1)} %broadcast_select_fusion.4.refs_5_), channel_id=1, source_target_pairs={{0,4},{4,0},{8,12},{12,8},{16,20},{20,16},{24,28},{28,24},{1,5},{5... | collective-permute-start | bytes 393224 | tf_op jit(solution)/shard_map/ppermute | solution.py:266

commit v5 on v4

--- a/solution.py
+++ b/solution.py
@@ -99,10 +99,8 @@
 
 
 def pick_kernel(nr, me, a, row, first_piece, keep, give, middle, last, goes,
-                raw, turned, hot, raw_sems):
+                turned, hot):
     down, block, across, width = a.shape
-    for b in range(down):
-        pltpu.make_async_copy(a.at[b], raw.at[b], raw_sems.at[b]).start()
     my_row = me[0]
     even = my_row % 2 == 0
     first, second = row[0:1], row[1:2]
@@ -137,8 +135,7 @@
         hot[:block, b * block : (b + 1) * block] = (kept - base == j).astype(BF)
         hot[block:, b * block : (b + 1) * block] = (given - base == j).astype(BF)
     for b in range(down):
-        pltpu.make_async_copy(a.at[b], raw.at[b], raw_sems.at[b]).wait()
-        turned[:, b] = jnp.transpose(raw[b], (1, 0, 2))
+        turned[:, b] = jnp.transpose(a[b], (1, 0, 2))
         if b == down - 1:
             last[...] = turned[0, b]
         elif b > 0:
@@ -282,11 +279,10 @@
          shape(across, block, width), shape(down - 2, block, width), shape(block, width),
          jax.ShapeDtypeStruct((1, 2 * block), jnp.int32)],
         [me, matrix, pivots, first_piece],
-        [SMEM, HBM, VMEM, ANY],
+        [SMEM, VMEM, VMEM, ANY],
         [VMEM] * 5,
-        [pltpu.VMEM(matrix.shape, BF), pltpu.VMEM((across, down, block, width), BF),
-         pltpu.VMEM((2 * block, down * block), BF),
-         pltpu.SemaphoreType.DMA((down,))],
+        [pltpu.VMEM((across, down, block, width), BF),
+         pltpu.VMEM((2 * block, down * block), BF)],
     )
     have1, have2 = far(middle), far(last)
     other0 = near(after(have0, keep))

time: 69.4 us -> 68.8 us (level)
  Pallas kernels: 15.5 us -> 14.8 us
    ppermute x3, waiting for transfers between devices: 3.76 us -> 2.98 us  [near(): return lax.ppermute(piece, 'pcol', twin(nc))]
    pallas_call x6, Pallas kernels: 15.5 us -> 14.8 us  [call(): pl.pallas_call(body, out_shape=outs, in_specs=in_specs, out_specs=out_spe...]
  transfers between devices with their start and end apart: 19 -> 19, of which waited for: 5 -> 5; matrix products, arithmetic and copies ran while one was open for 8% -> 8% of each run, Pallas kernels for 13% -> 12%
where the time goes in v5:
time: 68.8 us; the launch traced here: 68.3 us
  starting transfers between devices  35.4 us (51%)
  Pallas kernels  14.8 us (22%)
  waiting for transfers between devices  6.58 us (10%)
  other arithmetic  5.67 us (8%)
  local copies, waits for them, and re-layouts  5.56 us (8%)
    pallas_call x6, Pallas kernels, call(): pl.pallas_call(body, out_shape=outs, in_specs=in_specs, out_specs=out_spe...  14.8 us
    ppermute x3, starting transfers between devices, near(): return lax.ppermute(piece, 'pcol', twin(nc))  13.3 us
    ppermute x3, starting transfers between devices, far(): got = lax.ppermute(piece, 'pcol', pairs)  8.68 us
    unnamed x34, local copies, waits for them, and re-layouts  5.49 us
    ppermute x1, starting transfers between devices, local(): top = pick(pairs, lax.ppermute(top, 'prow', pairs), top)  4.23 us
    ppermute x3, waiting for transfers between devices, near(): return lax.ppermute(piece, 'pcol', twin(nc))  2.98 us
    select_n x3, other arithmetic, far(): piece = jnp.where(member(my_col, pairs), got, piece)  2.32 us
    ppermute x1, starting transfers between devices, local(): rim = pick(pairs, lax.ppermute(after(rim, have1, flat), 'prow', pairs), rim)  1.72 us
  transfers between devices with their start and end apart: 19, of which 5 were waited for; matrix products, arithmetic and copies ran while one was open for 8% of the time, Pallas kernels for 12%

profile of v5, /device:TPU:0, one launch (start us, length us, event | category | flops | bytes accessed | tf_op | source)
XLA Modules:
  0.0 68.3 jit_solution(5249610831145972701)
XLA Ops:
  0.0 1.6 %copy-done = bf16[4,256,4,256]{3,2,1,0:T(4,128)(2,1)S(1)} copy-done((bf16[4,256,4,256]{3,2,1,0:T(4,128)(2,1)S(1)}, bf16[4,256,4,256]{3,2,1,0:T(4,128)(2,1)}, u32[]{:S(2)}) %copy-start) | copy-done | bytes 2097176
  1.6 0.2 shard_map.46
  1.8 6.1 %collective-permute-start = (bf16[256,256]{1,0:T(8,128)(2,1)S(1)}, bf16[256,256]{1,0:T(8,128)(2,1)S(1)}, u32[]{:S(2)}, u32[]{:S(2)}) collective-permute-start(bf16[256,256]{1,0:T(8,128)(2,1)S(1)} %get-tuple-element.17.first_piece), channel_id=1, source_target_pairs={{0,2},{1,3},{4,6},{5,7},{8,10},{9,11},{12,14},{13,15},{16,18},{17,... | collective-permute-start | bytes 393224 | tf_op jit(solution)/shard_map/ppermute | solution.py:255
  7.9 4.2 %collective-permute-start.3 = (bf16[4,256,256]{2,1,0:T(8,128)(2,1)S(1)}, bf16[4,256,256]{2,1,0:T(8,128)(2,1)}, u32[]{:S(2)}, u32[]{:S(2)}) collective-permute-start(bf16[4,256,256]{2,1,0:T(8,128)(2,1)S(1)} %get-tuple-element.23), channel_id=1, source_target_pairs={{0,16},{4,12},{1,17},{5,13},{2,18},{6,14},{3,19},{7,15}} | collective-permute-start | bytes 1572872 | tf_op jit(solution)/shard_map/ppermute | solution.py:274
  12.1 0.1 pad_add_fusion.me
  12.2 3.1 %shard_map.47 = (bf16[4,256,256]{2,1,0:T(8,128)(2,1)S(1)}, bf16[4,256,256]{2,1,0:T(8,128)(2,1)}, bf16[2,256,256]{2,1,0:T(8,128)(2,1)S(1)}, bf16[256,256]{1,0:T(8,128)(2,1)}, s32[1,512]{1,0:T(1,128)S(1)}) custom-call(s32[2]{0:T(128)S(1)} %pad_add_fusion.me, bf16[4,256,4,256]{3,2,1,0:T(4,128)(2,1)S(1)} %copy-done.1, s32[2,256]{1,0:T(2,128)S(1)} %copy-done.9, ...), custom_call_target="tpu_custom_call" | custom-call | flops 1000000 | tf_op jit(solution)/shard_map/pallas_call | solution.py:62
  15.3 0.8 %copy-done.12 = bf16[4,256,256]{2,1,0:T(8,128)(2,1)} copy-done((bf16[4,256,256]{2,1,0:T(8,128)(2,1)}, bf16[4,256,256]{2,1,0:T(8,128)(2,1)S(1)}, u32[]{:S(2)}) %copy-start.12) | copy-done | bytes 524312
  16.1 0.0 collective-permute-done
  16.1 0.1 collective-permute-start.2
  16.2 1.3 %collective-permute-start.7 = (bf16[2,256,256]{2,1,0:T(8,128)(2,1)S(1)}, bf16[2,256,256]{2,1,0:T(8,128)(2,1)S(1)}, u32[]{:S(2)}, u32[]{:S(2)}) collective-permute-start(bf16[2,256,256]{2,1,0:T(8,128)(2,1)S(1)} %get-tuple-element.24), channel_id=1, source_target_pairs={{0,2},{1,3},{4,6},{5,7},{8,10},{9,11},{12,14},{13,15},{16,18},{17,... | collective-permute-start | bytes 786440 | tf_op jit(solution)/shard_map/ppermute | solution.py:255
  17.5 2.8 %collective-permute-start.1 = (bf16[256,256]{1,0:T(8,128)(2,1)S(1)}, bf16[256,256]{1,0:T(8,128)(2,1)S(1)}, u32[]{:S(2)}, u32[]{:S(2)}) collective-permute-start(bf16[256,256]{1,0:T(8,128)(2,1)S(1)} %broadcast_select_fusion.6.refs_11_), channel_id=1, source_target_pairs={{0,1},{1,0},{2,3},{3,2},{4,5},{5,4},{6,7},{7,6},{8,9},{9,8},{10,11... | collective-permute-start | bytes 393224 | tf_op jit(solution)/shard_map/ppermute | solution.py:260
  20.4 0.0 collective-permute-done.3
  20.4 0.1 broadcast_select_fusion.top
  20.5 1.0 %copy-done.13 = bf16[4,256,256]{2,1,0:T(8,128)(2,1)S(1)} copy-done((bf16[4,256,256]{2,1,0:T(8,128)(2,1)S(1)}, bf16[4,256,256]{2,1,0:T(8,128)(2,1)}, u32[]{:S(2)}) %copy-start.13) | copy-done | bytes 524312
  21.5 2.1 %shard_map.49.part = bf16[8,256,256]{2,1,0:T(8,128)(2,1)} custom-call(bf16[4,256,256]{2,1,0:T(8,128)(2,1)S(1)} %copy-done.13, bf16[4,256,256]{2,1,0:T(8,128)(2,1)} %collective-permute-done.2.got, bf16[4,256,256]{2,1,0:T(8,128)(2,1)S(1)} %broadcast_select_fusion.top), custom_call_target="tpu_custom_call" | custom-call | flops 99999997952 | tf_op jit(solution)/shard_map/pallas_call | solution.py:62
  23.6 1.5 %collective-permute-start.4 = (bf16[8,256,256]{2,1,0:T(8,128)(2,1)}, bf16[8,256,256]{2,1,0:T(8,128)(2,1)}, u32[]{:S(2)}, u32[]{:S(2)}) collective-permute-start(bf16[8,256,256]{2,1,0:T(8,128)(2,1)} %shard_map.49.part), channel_id=1, source_target_pairs={{0,8},{4,20},{8,0},{12,28},{16,24},{20,4},{24,16},{28,12},{1,9},{5... | collective-permute-start | bytes 3145736 | tf_op jit(solution)/shard_map/ppermute | solution.py:305
  25.1 1.7 %collective-permute-done.1.gate.refs_14_ = bf16[256,256]{1,0:T(8,128)(2,1)S(1)} collective-permute-done((bf16[256,256]{1,0:T(8,128)(2,1)S(1)}, bf16[256,256]{1,0:T(8,128)(2,1)S(1)}, u32[]{:S(2)}, u32[]{:S(2)}) %collective-permute-start.1) | collective-permute-done | bytes 131104 | tf_op jit(solution)/shard_map/ppermute | solution.py:260
  26.9 1.0 %shard_map.48.refs_0_ = bf16[4,4,256,256]{3,2,1,0:T(8,128)(2,1)S(1)} custom-call(bf16[4,256,4,256]{3,2,1,0:T(4,128)(2,1)S(1)} %copy-done.1, bf16[256,256]{1,0:T(8,128)(2,1)S(1)} %collective-permute-done.1.gate.refs_14_), custom_call_target="tpu_custom_call" | custom-call | flops 1000000000 | tf_op jit(solution)/shard_map/pallas_call | solution.py:62
  27.8 0.0 copy-start.2
  27.9 1.3 %copy-done.2 = bf16[4,4,256,256]{3,2,1,0:T(8,128)(2,1)} copy-done((bf16[4,4,256,256]{3,2,1,0:T(8,128)(2,1)}, bf16[4,4,256,256]{3,2,1,0:T(8,128)(2,1)S(1)}, u32[]{:S(2)}) %copy-start.2) | copy-done | bytes 2097176
  29.2 0.0 collective-permute-done.7
  29.2 0.7 %broadcast_select_fusion.1.refs_12_ = bf16[2,256,256]{2,1,0:T(8,128)(2,1)} fusion(bf16[2,256,256]{2,1,0:T(8,128)(2,1)S(1)} %collective-permute-done.7, bf16[2,256,256]{2,1,0:T(8,128)(2,1)S(1)} %get-tuple-element.24, pred[]{:T(512)S(6)} %gt.18), kind=kLoop, calls=%fused_computation.5 | loop fusion | flops 131072 | bytes 786433 | tf_op jit(solution)/shard_map/jit(_where)/select_n | solution.py:256
  29.9 1.7 %collective-permute-start.8 = (bf16[2,256,256]{2,1,0:T(8,128)(2,1)S(1)}, bf16[2,256,256]{2,1,0:T(8,128)(2,1)S(1)}, u32[]{:S(2)}, u32[]{:S(2)}) collective-permute-start(bf16[2,256,256]{2,1,0:T(8,128)(2,1)S(1)} %pad_maximum_fusion.1), channel_id=1, source_target_pairs={{0,8},{4,20},{1,9},{5,21},{2,10},{6,22},{3,11},{7,23}} | collective-permute-start | bytes 786440 | tf_op jit(solution)/shard_map/ppermute | solution.py:300
  31.7 1.3 %collective-permute-start.11 = (bf16[256,256]{1,0:T(8,128)(2,1)}, bf16[256,256]{1,0:T(8,128)(2,1)S(1)}, u32[]{:S(2)}, u32[]{:S(2)}) collective-permute-start(bf16[256,256]{1,0:T(8,128)(2,1)} %get-tuple-element.26), channel_id=1, source_target_pairs={{0,2},{1,3},{4,6},{5,7},{8,10},{9,11},{12,14},{13,15},{16,18},{17,... | collective-permute-start | bytes 393224 | tf_op jit(solution)/shard_map/ppermute | solution.py:255
  33.0 5.9 %collective-permute-start.12 = (bf16[2,256,256]{2,1,0:T(8,128)(2,1)}, bf16[2,256,256]{2,1,0:T(8,128)(2,1)S(1)}, u32[]{:S(2)}, u32[]{:S(2)}) collective-permute-start(bf16[2,256,256]{2,1,0:T(8,128)(2,1)} %broadcast_select_fusion.1.refs_12_), channel_id=1, source_target_pairs={{0,1},{1,0},{2,3},{3,2},{4,5},{5,4},{6,7},{7,6},{8,9},{9,8},{10,11... | collective-permute-start | bytes 786440 | tf_op jit(solution)/shard_map/ppermute | solution.py:260
  38.9 1.6 %collective-permute-done.8 = bf16[2,256,256]{2,1,0:T(8,128)(2,1)S(1)} collective-permute-done((bf16[2,256,256]{2,1,0:T(8,128)(2,1)S(1)}, bf16[2,256,256]{2,1,0:T(8,128)(2,1)S(1)}, u32[]{:S(2)}, u32[]{:S(2)}) %collective-permute-start.8) | collective-permute-done | bytes 262176 | tf_op jit(solution)/shard_map/ppermute | solution.py:300
  40.5 0.0 collective-permute-done.4.got
  40.5 1.7 %shard_map.50 = bf16[8,256,256]{2,1,0:T(8,128)(2,1)S(1)} custom-call(s32[1]{0:T(128)} %bitcast.2.taken, bf16[8,256,256]{2,1,0:T(8,128)(2,1)} %shard_map.49.part, bf16[8,256,256]{2,1,0:T(8,128)(2,1)} %collective-permute-done.4.got), custom_call_target="tpu_custom_call" | custom-call | flops 99999997952 | tf_op jit(solution)/shard_map/pallas_call | solution.py:62
  42.3 0.8 %collective-permute-start.5 = (bf16[256,256]{1,0:T(8,128)(2,1)S(1)}, bf16[256,256]{1,0:T(8,128)(2,1)S(1)}, u32[]{:S(2)}, u32[]{:S(2)}) collective-permute-start(bf16[256,256]{1,0:T(8,128)(2,1)S(1)} %slice_bitcast_fusion), channel_id=1, source_target_pairs={{0,16},{4,12},{8,24},{12,4},{16,0},{20,28},{24,8},{28,20},{1,17},{... | collective-permute-start | bytes 393224 | tf_op jit(solution)/shard_map/ppermute | solution.py:311
  43.1 0.9 %pad_maximum_fusion = bf16[5,256,256]{2,1,0:T(8,128)(2,1)} fusion(bf16[2,256,256]{2,1,0:T(8,128)(2,1)S(1)} %broadcast_select_fusion.2, bf16[3,256,256]{2,1,0:T(8,128)(2,1)S(1)} %slice.21), kind=kLoop, calls=%fused_computation | loop fusion | flops 327680 | bytes 1310720 | tf_op jit(solution)/shard_map/concatenate | solution.py:312
  44.0 1.3 %collective-permute-start.9 = (bf16[5,256,256]{2,1,0:T(8,128)(2,1)}, bf16[5,256,256]{2,1,0:T(8,128)(2,1)}, u32[]{:S(2)}, u32[]{:S(2)}) collective-permute-start(bf16[5,256,256]{2,1,0:T(8,128)(2,1)} %pad_maximum_fusion), channel_id=1, source_target_pairs={{0,16},{4,12},{8,24},{12,4},{16,0},{20,28},{24,8},{28,20},{1,17},{... | collective-permute-start | bytes 1966088 | tf_op jit(solution)/shard_map/ppermute | solution.py:312
  45.3 0.0 collective-permute-done.11
  45.3 1.6 %broadcast_select_fusion.5.refs_13_ = bf16[256,256]{1,0:T(8,128)(2,1)} fusion(bf16[256,256]{1,0:T(8,128)(2,1)S(1)} %collective-permute-done.11, bf16[256,256]{1,0:T(8,128)(2,1)} %get-tuple-element.26, pred[]{:T(512)S(6)} %gt.18), kind=kLoop, calls=%fused_computation.12 | loop fusion | flops 65536 | bytes 393217 | tf_op jit(solution)/shard_map/jit(_where)/select_n | solution.py:256
  46.9 0.5 collective-permute-done.5
  47.3 0.0 copy-start.3
  47.4 0.7 %copy-done.7 = bf16[2,256,256]{2,1,0:T(8,128)(2,1)} copy-done((bf16[2,256,256]{2,1,0:T(8,128)(2,1)}, bf16[2,256,256]{2,1,0:T(8,128)(2,1)S(1)}, u32[]{:S(2)}) %copy-start.7) | copy-done | bytes 262168
  48.1 1.3 %collective-permute-start.13 = (bf16[256,256]{1,0:T(8,128)(2,1)S(1)}, bf16[256,256]{1,0:T(8,128)(2,1)}, u32[]{:S(2)}, u32[]{:S(2)}) collective-permute-start(bf16[256,256]{1,0:T(8,128)(2,1)S(1)} %fusion.refs_1_), channel_id=1, source_target_pairs={{1,3},{4,6},{9,11},{12,14},{17,19},{20,22},{25,27},{28,30}} | collective-permute-start | bytes 393224 | tf_op jit(solution)/shard_map/ppermute | solution.py:320
  49.4 0.1 collective-permute-start.16
  49.5 0.5 collective-permute-start.6
  50.0 1.3 %collective-permute-start.14 = (bf16[256,256]{1,0:T(8,128)(2,1)S(1)}, bf16[256,256]{1,0:T(8,128)(2,1)S(1)}, u32[]{:S(2)}, u32[]{:S(2)}) collective-permute-start(bf16[256,256]{1,0:T(8,128)(2,1)S(1)} %broadcast_select_fusion.3), channel_id=1, source_target_pairs={{1,0},{3,2},{4,5},{6,7},{9,8},{11,10},{12,13},{14,15},{17,16},{19,... | collective-permute-start | bytes 393224 | tf_op jit(solution)/shard_map/ppermute | solution.py:325
  51.3 4.5 %collective-permute-start.18 = (bf16[256,256]{1,0:T(8,128)(2,1)}, bf16[256,256]{1,0:T(8,128)(2,1)S(1)}, u32[]{:S(2)}, u32[]{:S(2)}) collective-permute-start(bf16[256,256]{1,0:T(8,128)(2,1)} %broadcast_select_fusion.5.refs_13_), channel_id=1, source_target_pairs={{0,1},{1,0},{2,3},{3,2},{4,5},{5,4},{6,7},{7,6},{8,9},{9,8},{10,11... | collective-permute-start | bytes 393224 | tf_op jit(solution)/shard_map/ppermute | solution.py:260
  55.8 1.0 %slice_add_fusion.refs_3_ = bf16[3,256,256]{2,1,0:T(8,128)(2,1)S(1)} fusion(bf16[5,256,256]{2,1,0:T(8,128)(2,1)} %collective-permute-done.9, bf16[8,256,256]{2,1,0:T(8,128)(2,1)S(1)} %shard_map.50), kind=kLoop, calls=%fused_computation.2 | loop fusion | flops 196608 | bytes 1179648 | tf_op jit(solution)/shard_map/add | solution.py:313
  56.9 0.1 collective-permute-start.10
  57.0 1.1 %slice_select_fusion.refs_9_ = bf16[2,256,256]{2,1,0:T(8,128)(2,1)S(1)} fusion(bf16[5,256,256]{2,1,0:T(8,128)(2,1)} %collective-permute-done.9, pred[]{:T(512)S(6)} %gt.22, bf16[2,256,256]{2,1,0:T(8,128)(2,1)} %copy-done.16, bf16[1,256,256]{2,1,0:T(8,128)(2,1)} %copy-done.15, bf16[1,256,256]{2,1,0:T(8,128)(2,1)} %copy-done.14, pred[]{:T(512)S(6)} %gt.21), kind=kLoop, calls=%fused_computation.3 | loop fusion | flops 393216 | bytes 1048578 | tf_op jit(solution)/shard_map/jit(_where)/select_n | solution.py:266
  58.1 1.5 %collective-permute-done.14 = bf16[256,256]{1,0:T(8,128)(2,1)S(1)} collective-permute-done((bf16[256,256]{1,0:T(8,128)(2,1)S(1)}, bf16[256,256]{1,0:T(8,128)(2,1)S(1)}, u32[]{:S(2)}, u32[]{:S(2)}) %collective-permute-start.14) | collective-permute-done | bytes 131104 | tf_op jit(solution)/shard_map/ppermute | solution.py:325
  59.7 0.6 collective-permute-start.15
  60.2 1.3 %collective-permute-done.18.refs_16_ = bf16[256,256]{1,0:T(8,128)(2,1)S(1)} collective-permute-done((bf16[256,256]{1,0:T(8,128)(2,1)}, bf16[256,256]{1,0:T(8,128)(2,1)S(1)}, u32[]{:S(2)}, u32[]{:S(2)}) %collective-permute-start.18) | collective-permute-done | bytes 131104 | tf_op jit(solution)/shard_map/ppermute | solution.py:260
  61.6 6.7 %shard_map.51 = bf16[4,256,4,256]{3,2,1,0:T(4,128)(2,1)} custom-call(s32[2]{0:T(128)S(1)} %copy-done.11, s32[1,512]{1,0:T(1,128)S(1)} %get-tuple-element.18.goes, bf16[2,256,256]{2,1,0:T(8,128)(2,1)S(1)} %copy-done.5, bf16[2,256,256]{2,1,0:T(8,128)(2,1)S(1)} %copy-done.6, bf16[4,4,256,256]{3,2,1,0:T(8,128)(2,1)S(1)} %copy-done.3, ...), custom_call_target="tpu_custom_call" | custom-call | flops 1000000 | tf_op jit(solution)/shard_map/pallas_call | solution.py:62
  (47 shorter events, 0.3 us)
Async XLA Ops:
  0.0 1.6 %copy-start = (bf16[4,256,4,256]{3,2,1,0:T(4,128)(2,1)S(1)}, bf16[4,256,4,256]{3,2,1,0:T(4,128)(2,1)}, u32[]{:S(2)}) copy-start(bf16[4,256,4,256]{3,2,1,0:T(4,128)(2,1)} %a.5) | copy-start | bytes 6291460
  1.6 10.6 %copy-start.1 = (bf16[4,256,4,256]{3,2,1,0:T(4,128)(2,1)S(1)}, bf16[4,256,4,256]{3,2,1,0:T(4,128)(2,1)}, u32[]{:S(2)}) copy-start(bf16[4,256,4,256]{3,2,1,0:T(4,128)(2,1)} %a.5) | copy-start | bytes 6291460
  1.6 10.6 %copy-start.9 = (s32[2,256]{1,0:T(2,128)S(1)}, s32[2,256]{1,0:T(2,128)}, u32[]{:S(2)}) copy-start(s32[2,256]{1,0:T(2,128)} %row.1) | copy-start | bytes 6148
  1.8 14.3 %collective-permute-start = (bf16[256,256]{1,0:T(8,128)(2,1)S(1)}, bf16[256,256]{1,0:T(8,128)(2,1)S(1)}, u32[]{:S(2)}, u32[]{:S(2)}) collective-permute-start(bf16[256,256]{1,0:T(8,128)(2,1)S(1)} %get-tuple-element.17.first_piece), channel_id=1, source_target_pairs={{0,2},{1,3},{4,6},{5,7},{8,10},{9,11},{12,14},{13,15},{16,18},{17,... | collective-permute-start | bytes 393224 | tf_op jit(solution)/shard_map/ppermute | solution.py:255
  7.9 12.5 %collective-permute-start.3 = (bf16[4,256,256]{2,1,0:T(8,128)(2,1)S(1)}, bf16[4,256,256]{2,1,0:T(8,128)(2,1)}, u32[]{:S(2)}, u32[]{:S(2)}) collective-permute-start(bf16[4,256,256]{2,1,0:T(8,128)(2,1)S(1)} %get-tuple-element.23), channel_id=1, source_target_pairs={{0,16},{4,12},{1,17},{5,13},{2,18},{6,14},{3,19},{7,15}} | collective-permute-start | bytes 1572872 | tf_op jit(solution)/shard_map/ppermute | solution.py:274
  12.2 3.1 %copy-start.10 = (s32[2]{0:T(128)}, s32[2]{0:T(128)S(1)}, u32[]{:S(2)}) copy-start(s32[2]{0:T(128)S(1)} %pad_add_fusion.me) | copy-start | bytes 28
  15.3 0.8 %copy-start.12 = (bf16[4,256,256]{2,1,0:T(8,128)(2,1)}, bf16[4,256,256]{2,1,0:T(8,128)(2,1)S(1)}, u32[]{:S(2)}) copy-start(bf16[4,256,256]{2,1,0:T(8,128)(2,1)S(1)} %get-tuple-element.19.keep) | copy-start | bytes 1572868
  16.1 4.4 %collective-permute-start.2 = (bf16[4,256,256]{2,1,0:T(8,128)(2,1)}, bf16[4,256,256]{2,1,0:T(8,128)(2,1)}, u32[]{:S(2)}, u32[]{:S(2)}) collective-permute-start(bf16[4,256,256]{2,1,0:T(8,128)(2,1)} %get-tuple-element.22), channel_id=1, source_target_pairs={{0,4},{4,0},{8,12},{12,8},{16,20},{20,16},{24,28},{28,24},{1,5},{5... | collective-permute-start | bytes 1572872 | tf_op jit(solution)/shard_map/ppermute | solution.py:263
  16.2 13.0 %collective-permute-start.7 = (bf16[2,256,256]{2,1,0:T(8,128)(2,1)S(1)}, bf16[2,256,256]{2,1,0:T(8,128)(2,1)S(1)}, u32[]{:S(2)}, u32[]{:S(2)}) collective-permute-start(bf16[2,256,256]{2,1,0:T(8,128)(2,1)S(1)} %get-tuple-element.24), channel_id=1, source_target_pairs={{0,2},{1,3},{4,6},{5,7},{8,10},{9,11},{12,14},{13,15},{16,18},{17,... | collective-permute-start | bytes 786440 | tf_op jit(solution)/shard_map/ppermute | solution.py:255
  17.5 9.3 %collective-permute-start.1 = (bf16[256,256]{1,0:T(8,128)(2,1)S(1)}, bf16[256,256]{1,0:T(8,128)(2,1)S(1)}, u32[]{:S(2)}, u32[]{:S(2)}) collective-permute-start(bf16[256,256]{1,0:T(8,128)(2,1)S(1)} %broadcast_select_fusion.6.refs_11_), channel_id=1, source_target_pairs={{0,1},{1,0},{2,3},{3,2},{4,5},{5,4},{6,7},{7,6},{8,9},{9,8},{10,11... | collective-permute-start | bytes 393224 | tf_op jit(solution)/shard_map/ppermute | solution.py:260
  20.5 1.0 %copy-start.13 = (bf16[4,256,256]{2,1,0:T(8,128)(2,1)S(1)}, bf16[4,256,256]{2,1,0:T(8,128)(2,1)}, u32[]{:S(2)}) copy-start(bf16[4,256,256]{2,1,0:T(8,128)(2,1)} %copy-done.12) | copy-start | bytes 1572868
  23.6 16.9 %collective-permute-start.4 = (bf16[8,256,256]{2,1,0:T(8,128)(2,1)}, bf16[8,256,256]{2,1,0:T(8,128)(2,1)}, u32[]{:S(2)}, u32[]{:S(2)}) collective-permute-start(bf16[8,256,256]{2,1,0:T(8,128)(2,1)} %shard_map.49.part), channel_id=1, source_target_pairs={{0,8},{4,20},{8,0},{12,28},{16,24},{20,4},{24,16},{28,12},{1,9},{5... | collective-permute-start | bytes 3145736 | tf_op jit(solution)/shard_map/ppermute | solution.py:305
  26.9 13.6 %copy-start.14 = (bf16[1,256,256]{2,1,0:T(8,128)(2,1)}, bf16[1,256,256]{2,1,0:T(8,128)(2,1)S(1)}, u32[]{:S(2)}) copy-start(bf16[1,256,256]{2,1,0:T(8,128)(2,1)S(1)} %get-tuple-element.29) | copy-start | bytes 393220
  26.9 13.6 %copy-start.15 = (bf16[1,256,256]{2,1,0:T(8,128)(2,1)}, bf16[1,256,256]{2,1,0:T(8,128)(2,1)S(1)}, u32[]{:S(2)}) copy-start(bf16[1,256,256]{2,1,0:T(8,128)(2,1)S(1)} %get-tuple-element.30) | copy-start | bytes 393220
  27.8 1.3 %copy-start.2 = (bf16[4,4,256,256]{3,2,1,0:T(8,128)(2,1)}, bf16[4,4,256,256]{3,2,1,0:T(8,128)(2,1)S(1)}, u32[]{:S(2)}) copy-start(bf16[4,4,256,256]{3,2,1,0:T(8,128)(2,1)S(1)} %shard_map.48.refs_0_) | copy-start | bytes 6291460
  29.9 10.5 %collective-permute-start.8 = (bf16[2,256,256]{2,1,0:T(8,128)(2,1)S(1)}, bf16[2,256,256]{2,1,0:T(8,128)(2,1)S(1)}, u32[]{:S(2)}, u32[]{:S(2)}) collective-permute-start(bf16[2,256,256]{2,1,0:T(8,128)(2,1)S(1)} %pad_maximum_fusion.1), channel_id=1, source_target_pairs={{0,8},{4,20},{1,9},{5,21},{2,10},{6,22},{3,11},{7,23}} | collective-permute-start | bytes 786440 | tf_op jit(solution)/shard_map/ppermute | solution.py:300
  31.7 13.6 %collective-permute-start.11 = (bf16[256,256]{1,0:T(8,128)(2,1)}, bf16[256,256]{1,0:T(8,128)(2,1)S(1)}, u32[]{:S(2)}, u32[]{:S(2)}) collective-permute-start(bf16[256,256]{1,0:T(8,128)(2,1)} %get-tuple-element.26), channel_id=1, source_target_pairs={{0,2},{1,3},{4,6},{5,7},{8,10},{9,11},{12,14},{13,15},{16,18},{17,... | collective-permute-start | bytes 393224 | tf_op jit(solution)/shard_map/ppermute | solution.py:255
  33.0 14.4 %collective-permute-start.12 = (bf16[2,256,256]{2,1,0:T(8,128)(2,1)}, bf16[2,256,256]{2,1,0:T(8,128)(2,1)S(1)}, u32[]{:S(2)}, u32[]{:S(2)}) collective-permute-start(bf16[2,256,256]{2,1,0:T(8,128)(2,1)} %broadcast_select_fusion.1.refs_12_), channel_id=1, source_target_pairs={{0,1},{1,0},{2,3},{3,2},{4,5},{5,4},{6,7},{7,6},{8,9},{9,8},{10,11... | collective-permute-start | bytes 786440 | tf_op jit(solution)/shard_map/ppermute | solution.py:260
  40.5 1.8 %copy-start.16 = (bf16[2,256,256]{2,1,0:T(8,128)(2,1)}, bf16[2,256,256]{2,1,0:T(8,128)(2,1)S(1)}, u32[]{:S(2)}) copy-start(bf16[2,256,256]{2,1,0:T(8,128)(2,1)S(1)} %collective-permute-done.8) | copy-start | bytes 786436
  42.3 5.0 %collective-permute-start.5 = (bf16[256,256]{1,0:T(8,128)(2,1)S(1)}, bf16[256,256]{1,0:T(8,128)(2,1)S(1)}, u32[]{:S(2)}, u32[]{:S(2)}) collective-permute-start(bf16[256,256]{1,0:T(8,128)(2,1)S(1)} %slice_bitcast_fusion), channel_id=1, source_target_pairs={{0,16},{4,12},{8,24},{12,4},{16,0},{20,28},{24,8},{28,20},{1,17},{... | collective-permute-start | bytes 393224 | tf_op jit(solution)/shard_map/ppermute | solution.py:311
  44.0 11.8 %collective-permute-start.9 = (bf16[5,256,256]{2,1,0:T(8,128)(2,1)}, bf16[5,256,256]{2,1,0:T(8,128)(2,1)}, u32[]{:S(2)}, u32[]{:S(2)}) collective-permute-start(bf16[5,256,256]{2,1,0:T(8,128)(2,1)} %pad_maximum_fusion), channel_id=1, source_target_pairs={{0,16},{4,12},{8,24},{12,4},{16,0},{20,28},{24,8},{28,20},{1,17},{... | collective-permute-start | bytes 1966088 | tf_op jit(solution)/shard_map/ppermute | solution.py:312
  47.3 14.2 %copy-start.3 = (bf16[4,4,256,256]{3,2,1,0:T(8,128)(2,1)S(1)}, bf16[4,4,256,256]{3,2,1,0:T(8,128)(2,1)}, u32[]{:S(2)}) copy-start(bf16[4,4,256,256]{3,2,1,0:T(8,128)(2,1)} %copy-done.2) | copy-start | bytes 6291460
  47.4 14.2 %copy-start.11 = (s32[2]{0:T(128)S(1)}, s32[2]{0:T(128)}, u32[]{:S(2)}) copy-start(s32[2]{0:T(128)} %copy-done.10) | copy-start | bytes 28
  47.4 0.7 %copy-start.7 = (bf16[2,256,256]{2,1,0:T(8,128)(2,1)}, bf16[2,256,256]{2,1,0:T(8,128)(2,1)S(1)}, u32[]{:S(2)}) copy-start(bf16[2,256,256]{2,1,0:T(8,128)(2,1)S(1)} %collective-permute-done.12.refs_15_) | copy-start | bytes 786436
  48.1 1.9 %collective-permute-start.13 = (bf16[256,256]{1,0:T(8,128)(2,1)S(1)}, bf16[256,256]{1,0:T(8,128)(2,1)}, u32[]{:S(2)}, u32[]{:S(2)}) collective-permute-start(bf16[256,256]{1,0:T(8,128)(2,1)S(1)} %fusion.refs_1_), channel_id=1, source_target_pairs={{1,3},{4,6},{9,11},{12,14},{17,19},{20,22},{25,27},{28,30}} | collective-permute-start | bytes 393224 | tf_op jit(solution)/shard_map/ppermute | solution.py:320
  49.4 12.2 %copy-start.4 = (bf16[256,256]{1,0:T(8,128)(2,1)S(1)}, bf16[256,256]{1,0:T(8,128)(2,1)}, u32[]{:S(2)}) copy-start(bf16[256,256]{1,0:T(8,128)(2,1)} %broadcast_select_fusion.5.refs_13_) | copy-start | bytes 393220
  49.4 12.2 %copy-start.5 = (bf16[2,256,256]{2,1,0:T(8,128)(2,1)S(1)}, bf16[2,256,256]{2,1,0:T(8,128)(2,1)}, u32[]{:S(2)}) copy-start(bf16[2,256,256]{2,1,0:T(8,128)(2,1)} %lower.1) | copy-start | bytes 786436
  49.4 12.2 %copy-start.6 = (bf16[2,256,256]{2,1,0:T(8,128)(2,1)S(1)}, bf16[2,256,256]{2,1,0:T(8,128)(2,1)}, u32[]{:S(2)}) copy-start(bf16[2,256,256]{2,1,0:T(8,128)(2,1)} %upper.1) | copy-start | bytes 786436
  49.4 12.2 %copy-start.8 = (bf16[2,256,256]{2,1,0:T(8,128)(2,1)S(1)}, bf16[2,256,256]{2,1,0:T(8,128)(2,1)}, u32[]{:S(2)}) copy-start(bf16[2,256,256]{2,1,0:T(8,128)(2,1)} %copy-done.7) | copy-start | bytes 786436
  49.4 12.1 %collective-permute-start.16 = (bf16[4,256,256]{2,1,0:T(8,128)(2,1)S(1)}, bf16[4,256,256]{2,1,0:T(8,128)(2,1)S(1)}, u32[]{:S(2)}, u32[]{:S(2)}) collective-permute-start(bf16[4,256,256]{2,1,0:T(8,128)(2,1)S(1)} %slice.23.refs_7_), channel_id=1, source_target_pairs={{0,4},{4,0},{8,12},{12,8},{16,20},{20,16},{24,28},{28,24},{1,5},{5... | collective-permute-start | bytes 1572872 | tf_op jit(solution)/shard_map/ppermute | solution.py:263
  49.5 10.1 %collective-permute-start.6 = (bf16[256,256]{1,0:T(8,128)(2,1)S(1)}, bf16[256,256]{1,0:T(8,128)(2,1)S(1)}, u32[]{:S(2)}, u32[]{:S(2)}) collective-permute-start(bf16[256,256]{1,0:T(8,128)(2,1)S(1)} %fusion.refs_1_), channel_id=1, source_target_pairs={{0,4},{4,0},{8,12},{12,8},{16,20},{20,16},{24,28},{28,24},{1,5},{5... | collective-permute-start | bytes 393224 | tf_op jit(solution)/shard_map/ppermute | solution.py:263
  50.0 9.6 %collective-permute-start.14 = (bf16[256,256]{1,0:T(8,128)(2,1)S(1)}, bf16[256,256]{1,0:T(8,128)(2,1)S(1)}, u32[]{:S(2)}, u32[]{:S(2)}) collective-permute-start(bf16[256,256]{1,0:T(8,128)(2,1)S(1)} %broadcast_select_fusion.3), channel_id=1, source_target_pairs={{1,0},{3,2},{4,5},{6,7},{9,8},{11,10},{12,13},{14,15},{17,16},{19,... | collective-permute-start | bytes 393224 | tf_op jit(solution)/shard_map/ppermute | solution.py:325
  51.3 10.2 %collective-permute-start.18 = (bf16[256,256]{1,0:T(8,128)(2,1)}, bf16[256,256]{1,0:T(8,128)(2,1)S(1)}, u32[]{:S(2)}, u32[]{:S(2)}) collective-permute-start(bf16[256,256]{1,0:T(8,128)(2,1)} %broadcast_select_fusion.5.refs_13_), channel_id=1, source_target_pairs={{0,1},{1,0},{2,3},{3,2},{4,5},{5,4},{6,7},{7,6},{8,9},{9,8},{10,11... | collective-permute-start | bytes 393224 | tf_op jit(solution)/shard_map/ppermute | solution.py:260
  56.9 4.6 %collective-permute-start.10 = (bf16[3,256,256]{2,1,0:T(8,128)(2,1)S(1)}, bf16[3,256,256]{2,1,0:T(8,128)(2,1)S(1)}, u32[]{:S(2)}, u32[]{:S(2)}) collective-permute-start(bf16[3,256,256]{2,1,0:T(8,128)(2,1)S(1)} %slice_add_fusion.refs_3_), channel_id=1, source_target_pairs={{0,4},{4,0},{8,12},{12,8},{16,20},{20,16},{24,28},{28,24},{1,5},{5... | collective-permute-start | bytes 1179656 | tf_op jit(solution)/shard_map/ppermute | solution.py:263
  59.6 1.9 %collective-permute-start.17 = (bf16[2,256,256]{2,1,0:T(8,128)(2,1)S(1)}, bf16[2,256,256]{2,1,0:T(8,128)(2,1)S(1)}, u32[]{:S(2)}, u32[]{:S(2)}) collective-permute-start(bf16[2,256,256]{2,1,0:T(8,128)(2,1)S(1)} %slice_select_fusion.refs_9_), channel_id=1, source_target_pairs={{0,4},{4,0},{8,12},{12,8},{16,20},{20,16},{24,28},{28,24},{1,5},{5... | collective-permute-start | bytes 786440 | tf_op jit(solution)/shard_map/ppermute | solution.py:263
  59.7 1.9 %collective-permute-start.15 = (bf16[256,256]{1,0:T(8,128)(2,1)S(1)}, bf16[256,256]{1,0:T(8,128)(2,1)S(1)}, u32[]{:S(2)}, u32[]{:S(2)}) collective-permute-start(bf16[256,256]{1,0:T(8,128)(2,1)S(1)} %broadcast_select_fusion.4.refs_5_), channel_id=1, source_target_pairs={{0,4},{4,0},{8,12},{12,8},{16,20},{20,16},{24,28},{28,24},{1,5},{5... | collective-permute-start | bytes 393224 | tf_op jit(solution)/shard_map/ppermute | solution.py:263
